TPU v7x, 128 devices: a whole 4x4x4 slice. The times are simulated.
128 devices in a mesh: gx: 16 (over y_lo, z, core), gy: 8 (over y_hi, x).
Axes of the slice: x: 4, y: 4 (y_hi: 2, y_lo: 2; y = y_hi * 2 + y_lo), z: 4, core: 2. Of those that a mesh axis runs over, the one named last changes fastest.
Arguments:
- source_now: float32 [128, 128, 1024], P('gx', 'gy'), may hold values from -6 to 6
- source_prev: float32 [128, 128, 1024], P('gx', 'gy'), may hold values from -6 to 6
- receiver_now: float32 [128, 128, 1024], P('gx', 'gy'), may hold values from -6 to 6
- receiver_prev: float32 [128, 128, 1024], P('gx', 'gy'), may hold values from -6 to 6
- velocity_sq: float32 [128, 128, 1024], P('gx', 'gy'), may hold values from 0.02 to 0.18
- source_cells: int32 [4], replicated, may hold values from 0 to 16777215
- source_wavelet: float32 [2, 4], replicated, may hold values from -16 to 16
- receiver_cells: int32 [4096], replicated, may hold values from 0 to 16777215
- receiver_traces: float32 [2, 4096], replicated, may hold values from -12 to 12
Outputs:
- source_next: float32 [128, 128, 1024], P('gx', 'gy')
- receiver_next: float32 [128, 128, 1024], P('gx', 'gy')
- image: float32 [17, 64, 64, 512], P(None, 'gx', 'gy')
Inputs may be any that keep to these rules, and one draw needn't show every extreme that they name: `source_cells`: each entry is a flat cell index (x 128 + y) * 1024 + z of the grid; indices may repeat. `receiver_cells`: each entry is a flat cell index (x 128 + y) * 1024 + z of the grid; indices may repeat.
All inputs are finite; a program needn't handle non-finite values.
Results may differ from a plain program's by a relative error of at most 0.00002.
Values sent between devices are 32-bit elements; how exact they have to be, the bound alone decides.
No kernel may reach another device: no remote copies, remote signals or barrier semaphores. Data moves between devices by JAX's collectives and lax.ppermute only.
A program may use at most 128 MiB of HBM per device.

v0:
```python
import jax
import jax.numpy as jnp
from jax import lax
from jax.sharding import PartitionSpec as P

NOFF = 17


COEF = (-205.0 / 72.0, 8.0 / 5.0, -1.0 / 5.0, 8.0 / 315.0, -1.0 / 560.0)


def with_halo(cells, sides, width):
    for axis, dim in sides:
        count = lax.axis_size(axis)
        ends = count - 1
        head = lax.slice_in_dim(cells, 0, width, axis=dim)
        tail = lax.slice_in_dim(cells, cells.shape[dim] - width, cells.shape[dim], axis=dim)
        cells = jnp.concatenate(
            [
                lax.ppermute(tail, axis, [(i, (i + 1) % count) for i in range(ends)]),
                cells,
                lax.ppermute(head, axis, [((i + 1) % count, i) for i in range(ends)]),
            ],
            axis=dim,
        )
    return cells


def interior_laplace(extended):
    size_x = extended.shape[1] - 8
    size_y = extended.shape[2] - 8
    size_z = extended.shape[3]
    center = extended[:, 4 : 4 + size_x, 4 : 4 + size_y]
    total = 3.0 * COEF[0] * center
    for distance in range(1, 5):
        near = extended[:, 4 + distance : 4 + distance + size_x, 4 : 4 + size_y]
        near = near + extended[:, 4 - distance : 4 - distance + size_x, 4 : 4 + size_y]
        near = near + extended[:, 4 : 4 + size_x, 4 + distance : 4 + distance + size_y]
        near = near + extended[:, 4 : 4 + size_x, 4 - distance : 4 - distance + size_y]
        edge = jnp.zeros(center.shape[:3] + (distance,), jnp.float32)
        upper = jnp.concatenate((center[:, :, :, distance:], edge), axis=3)
        lower = jnp.concatenate((edge, center[:, :, :, : size_z - distance]), axis=3)
        near = near + upper + lower
        total = total + COEF[distance] * near
    return total


def locate(cells, anchor_x, anchor_y, span_x, span_y, rows_y, depth):
    plane_size = rows_y * depth
    cell_x = cells // plane_size
    remainder = cells - cell_x * plane_size
    cell_y = remainder // depth
    cell_z = remainder - cell_y * depth
    local_x = cell_x - anchor_x
    local_y = cell_y - anchor_y
    inside = (local_x >= 0) & (local_x < span_x) & (local_y >= 0) & (local_y < span_y)
    return jnp.where(
        inside, (local_x * span_y + local_y) * depth + cell_z, 2 * span_x * span_y * depth
    )


def lag_products(extended, width):
    reach = (NOFF - 1) // 2
    gathers = []
    for offset in range(-reach, reach + 1):
        left = extended[0, reach - offset : reach - offset + width : 2]
        right = extended[1, reach + offset : reach + offset + width : 2]
        gathers.append(left * right)
    return jnp.stack(gathers)


def local(
    source_now,
    source_prev,
    receiver_now,
    receiver_prev,
    velocity_sq,
    source_cells,
    source_wavelet,
    receiver_cells,
    receiver_traces,
):
    width_x, width_y, depth = source_now.shape
    rows_y = width_y * lax.axis_size("gy")
    anchor_x = lax.axis_index("gx") * width_x
    anchor_y = lax.axis_index("gy") * width_y
    reach = (NOFF - 1) // 2
    fields = jnp.stack((source_now, receiver_now))
    older = jnp.stack((source_prev, receiver_prev))
    recorded = []
    for instant in range(source_wavelet.shape[0]):
        extended = with_halo(fields, (("gx", 1), ("gy", 2)), 4)
        volume = width_x * width_y * depth
        first = locate(source_cells, anchor_x - 0, anchor_y - 0, width_x, width_y, rows_y, depth)
        second = locate(receiver_cells, anchor_x - 0, anchor_y - 0, width_x, width_y, rows_y, depth)
        second = jnp.where(second < volume, second + volume, second)
        target = jnp.concatenate((first, second))
        amounts = jnp.concatenate((source_wavelet[instant], receiver_traces[instant]))
        flat = jnp.zeros((2 * volume,), jnp.float32).at[target].add(amounts, mode="drop")
        updated = (
            2.0 * fields
            - older
            + velocity_sq[None]
            * (interior_laplace(extended) + flat.reshape(2, width_x, width_y, depth))
        )
        older, fields = (fields, updated)
        recorded.append(fields)
    image = jnp.zeros((NOFF, width_x // 2, width_y // 2, depth // 2), jnp.float32)
    for snapshot in recorded:
        coarse = snapshot[:, :, ::2, ::2]
        slabs = with_halo(coarse, (("gx", 1),), reach)
        image = image + lag_products(slabs, width_x)
    return (fields[0], fields[1], image)


def solution(mesh):
    return jax.shard_map(
        local,
        mesh=mesh,
        in_specs=(
            P("gx", "gy", None),
            P("gx", "gy", None),
            P("gx", "gy", None),
            P("gx", "gy", None),
            P("gx", "gy", None),
            P(),
            P(),
            P(),
            P(),
        ),
        out_specs=(P("gx", "gy", None), P("gx", "gy", None), P(None, "gx", "gy", None)),
        check_vma=False,
    )
```

profile of v0, /device:TPU:24, one launch (start us, length us, event | category | flops | bytes accessed | tf_op | source)
XLA Modules:
  0.0 186.8 jit_solution(13662127806362285616)
XLA Ops:
  0.6 2.4 %fusion.63 = (f32[2,4,16,1024]{3,2,1,0:T(8,128)}, f32[2,4,16,1024]{3,2,1,0:T(8,128)}) fusion(f32[1,8,16,1024]{3,2,1,0:T(8,128)} %bitcast.17, f32[1,8,16,1024]{3,2,1,0:T(8,128)} %bitcast.27), kind=kLoop, calls=%fused_computation.123 | loop fusion | flops 262144 | bytes 2097152 | tf_op jit(solution)/shard_map/stack | solution.py:88
  3.0 5.6 %collective-permute-start = (f32[2,4,16,1024]{3,2,1,0:T(8,128)}, f32[2,4,16,1024]{3,2,1,0:T(8,128)S(1)}, u32[]{:S(2)}, u32[]{:S(2)}) collective-permute-start(f32[2,4,16,1024]{3,2,1,0:T(8,128)} %get-tuple-element.37), channel_id=1, source_target_pairs={{8,0},{16,8},{24,16},{32,24},{40,32},{48,40},{56,48},{64,56},{72,6... | collective-permute-start | bytes 1572872 | tf_op jit(solution)/shard_map/ppermute | solution.py:22
  8.6 1.9 %collective-permute-start.1 = (f32[2,4,16,1024]{3,2,1,0:T(8,128)}, f32[2,4,16,1024]{3,2,1,0:T(8,128)S(1)}, u32[]{:S(2)}, u32[]{:S(2)}) collective-permute-start(f32[2,4,16,1024]{3,2,1,0:T(8,128)} %get-tuple-element.36), channel_id=1, source_target_pairs={{0,8},{8,16},{16,24},{24,32},{32,40},{40,48},{48,56},{56,64},{64,7... | collective-permute-start | bytes 1572872 | tf_op jit(solution)/shard_map/ppermute | solution.py:20
  11.9 1.7 fusion.35
  13.8 1.7 collective-permute-done
  15.6 5.8 %collective-permute-done.1 = f32[2,4,16,1024]{3,2,1,0:T(8,128)S(1)} collective-permute-done((f32[2,4,16,1024]{3,2,1,0:T(8,128)}, f32[2,4,16,1024]{3,2,1,0:T(8,128)S(1)}, u32[]{:S(2)}, u32[]{:S(2)}) %collective-permute-start.1) | collective-permute-done | bytes 524320 | tf_op jit(solution)/shard_map/ppermute | solution.py:20
  22.8 5.0 %collective-permute-start.2 = (f32[2,16,4,1024]{3,1,2,0:T(8,128)}, f32[2,16,4,1024]{3,1,2,0:T(8,128)}, u32[]{:S(2)}, u32[]{:S(2)}) collective-permute-start(f32[2,16,4,1024]{3,1,2,0:T(8,128)} %copy.21), channel_id=1, source_target_pairs={{1,0},{2,1},{3,2},{4,3},{5,4},{6,5},{7,6},{9,8},{10,9},{11,10},{12... | collective-permute-start | bytes 1572872 | tf_op jit(solution)/shard_map/ppermute | solution.py:22
  28.9 1.9 %collective-permute-start.3 = (f32[2,16,4,1024]{3,1,2,0:T(8,128)}, f32[2,16,4,1024]{3,1,2,0:T(8,128)}, u32[]{:S(2)}, u32[]{:S(2)}) collective-permute-start(f32[2,16,4,1024]{3,1,2,0:T(8,128)} %copy.23), channel_id=1, source_target_pairs={{0,1},{1,2},{2,3},{3,4},{4,5},{5,6},{6,7},{8,9},{9,10},{10,11},{11... | collective-permute-start | bytes 1572872 | tf_op jit(solution)/shard_map/ppermute | solution.py:20
  30.9 24.5 %scatter_custom_fusion.1 = f32[262144]{0:T(1024)} fusion(s32[4100]{0:T(1024)S(1)} %fusion.68, f32[4100]{0:T(1024)S(1)} %get-tuple-element.43, f32[]{:T(128)} %constant.78.clone.1), kind=kCustom, calls=%fused_computation.133 | custom fusion | flops 4100 | bytes 1048580 | tf_op jit(solution)/shard_map/scatter-add | solution.py:99
  55.4 2.4 %reshape.97 = f32[2,8,16,1024]{3,2,1,0:T(8,128)} reshape(f32[262144]{0:T(1024)} %scatter_custom_fusion.1) | data formatting | bytes 2097152 | tf_op jit(solution)/shard_map/reshape | solution.py:104
  57.8 24.4 %scatter_custom_fusion = f32[262144]{0:T(1024)} fusion(s32[4100]{0:T(1024)S(1)} %fusion.68, f32[4100]{0:T(1024)S(1)} %get-tuple-element.42, f32[]{:T(128)} %constant.78.clone.1), kind=kCustom, calls=%fused_computation.135 | custom fusion | flops 4100 | bytes 1048580 | tf_op jit(solution)/shard_map/scatter-add | solution.py:99
  82.2 2.4 %reshape.96 = f32[2,8,16,1024]{3,2,1,0:T(8,128)} reshape(f32[262144]{0:T(1024)} %scatter_custom_fusion) | data formatting | bytes 2097152 | tf_op jit(solution)/shard_map/reshape | solution.py:104
  90.9 4.3 %fusion.49 = f32[2,8,16,1024]{3,2,1,0:T(8,128)S(1)} fusion(f32[2,8,16,1024]{3,2,1,0:T(8,128)S(1)} %copy-done.6, f32[2,16,20,1024]{3,2,1,0:T(8,128)S(1)} %get-tuple-element.11, f32[2,16,20,1024]{3,2,1,0:T(8,128)S(1)} %get-tuple-element.10, f32[2,12,16,1024]{3,2,1,0:T(8,128)S(1)} %get-tuple-element.35, f32[2,12,16,1024]{3,2,1,0:T(8,128)S(1)} %get-tuple-element.34, ...), kind=kLoop, calls=%fused_computation.95 | loop fusion | flops 9437184 | bytes 29863936 | tf_op jit(solution)/shard_map/add | solution.py:101
  97.9 1.7 fusion.77
  99.6 1.7 fusion.76
  101.3 9.0 %slice.490 = f32[2,8,8,512]{3,2,1,0:T(8,128)S(1)} slice(f32[2,8,16,1024]{3,2,1,0:T(8,128)S(1)} %fusion.49), slice={[0:2:1], [0:8:1], [0:16:2], [0:1024:2]} | slice | bytes 524288 | tf_op jit(solution)/shard_map/slice | solution.py:110
  110.3 1.9 %collective-permute-start.9 = (f32[2,8,8,512]{3,2,1,0:T(8,128)S(1)}, f32[2,8,8,512]{3,2,1,0:T(8,128)S(1)}, u32[]{:S(2)}, u32[]{:S(2)}) collective-permute-start(f32[2,8,8,512]{3,2,1,0:T(8,128)S(1)} %slice.490), channel_id=1, source_target_pairs={{0,8},{8,16},{16,24},{24,32},{32,40},{40,48},{48,56},{56,64},{64,7... | collective-permute-start | bytes 786440 | tf_op jit(solution)/shard_map/ppermute | solution.py:20
  112.2 5.8 %collective-permute-start.8 = (f32[2,8,8,512]{3,2,1,0:T(8,128)S(1)}, f32[2,8,8,512]{3,2,1,0:T(8,128)S(1)}, u32[]{:S(2)}, u32[]{:S(2)}) collective-permute-start(f32[2,8,8,512]{3,2,1,0:T(8,128)S(1)} %slice.490), channel_id=1, source_target_pairs={{8,0},{16,8},{24,16},{32,24},{40,32},{48,40},{56,48},{64,56},{72,6... | collective-permute-start | bytes 786440 | tf_op jit(solution)/shard_map/ppermute | solution.py:22
  118.0 1.9 %collective-permute-start.5 = (f32[2,4,16,1024]{3,2,1,0:T(8,128)}, f32[2,4,16,1024]{3,2,1,0:T(8,128)S(1)}, u32[]{:S(2)}, u32[]{:S(2)}) collective-permute-start(f32[2,4,16,1024]{3,2,1,0:T(8,128)} %get-tuple-element.25), channel_id=1, source_target_pairs={{0,8},{8,16},{16,24},{24,32},{32,40},{40,48},{48,56},{56,64},{64,7... | collective-permute-start | bytes 1572872 | tf_op jit(solution)/shard_map/ppermute | solution.py:20
  119.9 5.8 %collective-permute-start.4 = (f32[2,4,16,1024]{3,2,1,0:T(8,128)}, f32[2,4,16,1024]{3,2,1,0:T(8,128)S(1)}, u32[]{:S(2)}, u32[]{:S(2)}) collective-permute-start(f32[2,4,16,1024]{3,2,1,0:T(8,128)} %get-tuple-element.24), channel_id=1, source_target_pairs={{8,0},{16,8},{24,16},{32,24},{40,32},{48,40},{56,48},{64,56},{72,6... | collective-permute-start | bytes 1572872 | tf_op jit(solution)/shard_map/ppermute | solution.py:22
  125.6 1.8 fusion.75
  127.8 3.0 %collective-permute-done.5 = f32[2,4,16,1024]{3,2,1,0:T(8,128)S(1)} collective-permute-done((f32[2,4,16,1024]{3,2,1,0:T(8,128)}, f32[2,4,16,1024]{3,2,1,0:T(8,128)S(1)}, u32[]{:S(2)}, u32[]{:S(2)}) %collective-permute-start.5) | collective-permute-done | bytes 524320 | tf_op jit(solution)/shard_map/ppermute | solution.py:20
  130.8 1.9 collective-permute-done.4
  133.2 7.5 %collective-permute-start.6 = (f32[2,16,4,1024]{3,1,2,0:T(8,128)S(1)}, f32[2,16,4,1024]{3,1,2,0:T(8,128)S(1)}, u32[]{:S(2)}, u32[]{:S(2)}) collective-permute-start(f32[2,16,4,1024]{3,1,2,0:T(8,128)S(1)} %copy.25), channel_id=1, source_target_pairs={{1,0},{2,1},{3,2},{4,3},{5,4},{6,5},{7,6},{9,8},{10,9},{11,10},{12... | collective-permute-start | bytes 1572872 | tf_op jit(solution)/shard_map/ppermute | solution.py:22
  141.1 2.1 %collective-permute-start.7 = (f32[2,16,4,1024]{3,1,2,0:T(8,128)S(1)}, f32[2,16,4,1024]{3,1,2,0:T(8,128)S(1)}, u32[]{:S(2)}, u32[]{:S(2)}) collective-permute-start(f32[2,16,4,1024]{3,1,2,0:T(8,128)S(1)} %copy.27), channel_id=1, source_target_pairs={{0,1},{1,2},{2,3},{3,4},{4,5},{5,6},{6,7},{8,9},{9,10},{10,11},{11... | collective-permute-start | bytes 1572872 | tf_op jit(solution)/shard_map/ppermute | solution.py:20
  143.3 4.1 %collective-permute-done.6 = f32[2,16,4,1024]{3,1,2,0:T(8,128)S(1)} collective-permute-done((f32[2,16,4,1024]{3,1,2,0:T(8,128)S(1)}, f32[2,16,4,1024]{3,1,2,0:T(8,128)S(1)}, u32[]{:S(2)}, u32[]{:S(2)}) %collective-permute-start.6) | collective-permute-done | bytes 524320 | tf_op jit(solution)/shard_map/ppermute | solution.py:22
  147.8 8.0 %collective-permute-done.7 = f32[2,16,4,1024]{3,1,2,0:T(8,128)S(1)} collective-permute-done((f32[2,16,4,1024]{3,1,2,0:T(8,128)S(1)}, f32[2,16,4,1024]{3,1,2,0:T(8,128)S(1)}, u32[]{:S(2)}, u32[]{:S(2)}) %collective-permute-start.7) | collective-permute-done | bytes 524320 | tf_op jit(solution)/shard_map/ppermute | solution.py:20
  159.0 4.6 %fusion.11 = f32[2,8,16,1024]{3,2,1,0:T(8,128)S(1)} fusion(f32[2,8,16,1024]{3,2,1,0:T(8,128)S(1)} %copy-done.5, f32[2,8,16,1024]{3,2,1,0:T(8,128)S(1)} %fusion.49, f32[2,4,16,1024]{3,2,1,0:T(8,128)S(1)} %collective-permute-done.5, f32[2,4,16,1024]{3,2,1,0:T(8,128)S(1)} %collective-permute-done.4, f32[2,16,20,1024]{3,2,1,0:T(8,128)S(1)} %get-tuple-element.7, ...), kind=kLoop, calls=%fused_computation.52 | loop fusion | flops 11272192 | bytes 22523904 | tf_op jit(solution)/shard_map/add | solution.py:101
  163.6 9.0 %slice.525 = f32[2,8,8,512]{3,2,1,0:T(8,128)S(1)} slice(f32[2,8,16,1024]{3,2,1,0:T(8,128)S(1)} %fusion.11), slice={[0:2:1], [0:8:1], [0:16:2], [0:1024:2]} | slice | bytes 524288 | tf_op jit(solution)/shard_map/slice | solution.py:110
  172.6 1.9 %collective-permute-start.11 = (f32[2,8,8,512]{3,2,1,0:T(8,128)S(1)}, f32[2,8,8,512]{3,2,1,0:T(8,128)S(1)}, u32[]{:S(2)}, u32[]{:S(2)}) collective-permute-start(f32[2,8,8,512]{3,2,1,0:T(8,128)S(1)} %slice.525), channel_id=1, source_target_pairs={{0,8},{8,16},{16,24},{24,32},{32,40},{40,48},{48,56},{56,64},{64,7... | collective-permute-start | bytes 786440 | tf_op jit(solution)/shard_map/ppermute | solution.py:20
  174.6 5.8 %collective-permute-start.10 = (f32[2,8,8,512]{3,2,1,0:T(8,128)S(1)}, f32[2,8,8,512]{3,2,1,0:T(8,128)S(1)}, u32[]{:S(2)}, u32[]{:S(2)}) collective-permute-start(f32[2,8,8,512]{3,2,1,0:T(8,128)S(1)} %slice.525), channel_id=1, source_target_pairs={{8,0},{16,8},{24,16},{32,24},{40,32},{48,40},{56,48},{64,56},{72,6... | collective-permute-start | bytes 786440 | tf_op jit(solution)/shard_map/ppermute | solution.py:22
  182.4 1.8 collective-permute-done.10
  (107 shorter events, 22.3 us)
Async XLA Ops:
  0.6 9.9 %copy-start = (f32[8,16,1024]{2,1,0:T(8,128)S(1)}, f32[8,16,1024]{2,1,0:T(8,128)}, u32[]{:S(2)}) copy-start(f32[8,16,1024]{2,1,0:T(8,128)} %param.9) | copy-start | bytes 1572868
  0.6 9.9 %copy-start.1 = (f32[8,16,1024]{2,1,0:T(8,128)S(1)}, f32[8,16,1024]{2,1,0:T(8,128)}, u32[]{:S(2)}) copy-start(f32[8,16,1024]{2,1,0:T(8,128)} %param.11) | copy-start | bytes 1572868
  3.0 12.6 %collective-permute-start = (f32[2,4,16,1024]{3,2,1,0:T(8,128)}, f32[2,4,16,1024]{3,2,1,0:T(8,128)S(1)}, u32[]{:S(2)}, u32[]{:S(2)}) collective-permute-start(f32[2,4,16,1024]{3,2,1,0:T(8,128)} %get-tuple-element.37), channel_id=1, source_target_pairs={{8,0},{16,8},{24,16},{32,24},{40,32},{48,40},{56,48},{64,56},{72,6... | collective-permute-start | bytes 1572872 | tf_op jit(solution)/shard_map/ppermute | solution.py:22
  8.6 12.8 %collective-permute-start.1 = (f32[2,4,16,1024]{3,2,1,0:T(8,128)}, f32[2,4,16,1024]{3,2,1,0:T(8,128)S(1)}, u32[]{:S(2)}, u32[]{:S(2)}) collective-permute-start(f32[2,4,16,1024]{3,2,1,0:T(8,128)} %get-tuple-element.36), channel_id=1, source_target_pairs={{0,8},{8,16},{16,24},{24,32},{32,40},{40,48},{48,56},{56,64},{64,7... | collective-permute-start | bytes 1572872 | tf_op jit(solution)/shard_map/ppermute | solution.py:20
  11.9 1.7 copy-start.16
  11.9 1.7 copy-start.18
  11.9 1.9 copy-start.19
  11.9 1.9 %copy-start.17 = (s32[4096]{0:T(1024)S(1)}, s32[4096]{0:T(1024)}, u32[]{:S(2)}) copy-start(s32[4096]{0:T(1024)} %param.16) | copy-start | bytes 49156
  22.8 63.0 %collective-permute-start.2 = (f32[2,16,4,1024]{3,1,2,0:T(8,128)}, f32[2,16,4,1024]{3,1,2,0:T(8,128)}, u32[]{:S(2)}, u32[]{:S(2)}) collective-permute-start(f32[2,16,4,1024]{3,1,2,0:T(8,128)} %copy.21), channel_id=1, source_target_pairs={{1,0},{2,1},{3,2},{4,3},{5,4},{6,5},{7,6},{9,8},{10,9},{11,10},{12... | collective-permute-start | bytes 1572872 | tf_op jit(solution)/shard_map/ppermute | solution.py:22
  28.9 58.3 %collective-permute-start.3 = (f32[2,16,4,1024]{3,1,2,0:T(8,128)}, f32[2,16,4,1024]{3,1,2,0:T(8,128)}, u32[]{:S(2)}, u32[]{:S(2)}) collective-permute-start(f32[2,16,4,1024]{3,1,2,0:T(8,128)} %copy.23), channel_id=1, source_target_pairs={{0,1},{1,2},{2,3},{3,4},{4,5},{5,6},{6,7},{8,9},{9,10},{10,11},{11... | collective-permute-start | bytes 1572872 | tf_op jit(solution)/shard_map/ppermute | solution.py:20
  88.5 1.2 copy-start.2
  88.6 1.5 copy-start.3
  88.6 1.8 copy-start.4
  88.6 2.1 %copy-start.6 = (f32[2,8,16,1024]{3,2,1,0:T(8,128)S(1)}, f32[2,8,16,1024]{3,2,1,0:T(8,128)}, u32[]{:S(2)}) copy-start(f32[2,8,16,1024]{3,2,1,0:T(8,128)} %reshape.96) | copy-start | bytes 3145732
  88.6 2.3 %copy-start.12 = (f32[8,16,1024]{2,1,0:T(8,128)S(1)}, f32[8,16,1024]{2,1,0:T(8,128)}, u32[]{:S(2)}) copy-start(f32[8,16,1024]{2,1,0:T(8,128)} %param.13) | copy-start | bytes 1572868
  110.3 17.2 %collective-permute-start.9 = (f32[2,8,8,512]{3,2,1,0:T(8,128)S(1)}, f32[2,8,8,512]{3,2,1,0:T(8,128)S(1)}, u32[]{:S(2)}, u32[]{:S(2)}) collective-permute-start(f32[2,8,8,512]{3,2,1,0:T(8,128)S(1)} %slice.490), channel_id=1, source_target_pairs={{0,8},{8,16},{16,24},{24,32},{32,40},{40,48},{48,56},{56,64},{64,7... | collective-permute-start | bytes 786440 | tf_op jit(solution)/shard_map/ppermute | solution.py:20
  112.2 15.3 %collective-permute-start.8 = (f32[2,8,8,512]{3,2,1,0:T(8,128)S(1)}, f32[2,8,8,512]{3,2,1,0:T(8,128)S(1)}, u32[]{:S(2)}, u32[]{:S(2)}) collective-permute-start(f32[2,8,8,512]{3,2,1,0:T(8,128)S(1)} %slice.490), channel_id=1, source_target_pairs={{8,0},{16,8},{24,16},{32,24},{40,32},{48,40},{56,48},{64,56},{72,6... | collective-permute-start | bytes 786440 | tf_op jit(solution)/shard_map/ppermute | solution.py:22
  118.0 12.8 %collective-permute-start.5 = (f32[2,4,16,1024]{3,2,1,0:T(8,128)}, f32[2,4,16,1024]{3,2,1,0:T(8,128)S(1)}, u32[]{:S(2)}, u32[]{:S(2)}) collective-permute-start(f32[2,4,16,1024]{3,2,1,0:T(8,128)} %get-tuple-element.25), channel_id=1, source_target_pairs={{0,8},{8,16},{16,24},{24,32},{32,40},{40,48},{48,56},{56,64},{64,7... | collective-permute-start | bytes 1572872 | tf_op jit(solution)/shard_map/ppermute | solution.py:20
  119.9 12.8 %collective-permute-start.4 = (f32[2,4,16,1024]{3,2,1,0:T(8,128)}, f32[2,4,16,1024]{3,2,1,0:T(8,128)S(1)}, u32[]{:S(2)}, u32[]{:S(2)}) collective-permute-start(f32[2,4,16,1024]{3,2,1,0:T(8,128)} %get-tuple-element.24), channel_id=1, source_target_pairs={{8,0},{16,8},{24,16},{32,24},{40,32},{48,40},{56,48},{64,56},{72,6... | collective-permute-start | bytes 1572872 | tf_op jit(solution)/shard_map/ppermute | solution.py:22
  133.2 14.2 %collective-permute-start.6 = (f32[2,16,4,1024]{3,1,2,0:T(8,128)S(1)}, f32[2,16,4,1024]{3,1,2,0:T(8,128)S(1)}, u32[]{:S(2)}, u32[]{:S(2)}) collective-permute-start(f32[2,16,4,1024]{3,1,2,0:T(8,128)S(1)} %copy.25), channel_id=1, source_target_pairs={{1,0},{2,1},{3,2},{4,3},{5,4},{6,5},{7,6},{9,8},{10,9},{11,10},{12... | collective-permute-start | bytes 1572872 | tf_op jit(solution)/shard_map/ppermute | solution.py:22
  141.1 14.7 %collective-permute-start.7 = (f32[2,16,4,1024]{3,1,2,0:T(8,128)S(1)}, f32[2,16,4,1024]{3,1,2,0:T(8,128)S(1)}, u32[]{:S(2)}, u32[]{:S(2)}) collective-permute-start(f32[2,16,4,1024]{3,1,2,0:T(8,128)S(1)} %copy.27), channel_id=1, source_target_pairs={{0,1},{1,2},{2,3},{3,4},{4,5},{5,6},{6,7},{8,9},{9,10},{10,11},{11... | collective-permute-start | bytes 1572872 | tf_op jit(solution)/shard_map/ppermute | solution.py:20
  143.3 12.5 %copy-start.14 = (f32[17,4,8,512]{3,2,1,0:T(8,128)}, f32[17,4,8,512]{3,2,1,0:T(8,128)S(1)}, u32[]{:S(2)}) copy-start(f32[17,4,8,512]{3,2,1,0:T(8,128)S(1)} %constant_dynamic-update-slice_fusion) | copy-start | bytes 3342340
  156.1 1.2 copy-start.5
  156.1 1.5 copy-start.7
  156.1 1.8 copy-start.8
  156.1 2.1 %copy-start.9 = (f32[2,8,16,1021]{3,2,1,0:T(8,128)S(1)}, f32[2,8,16,1021]{3,2,1,0:T(8,128)}, u32[]{:S(2)}) copy-start(f32[2,8,16,1021]{3,2,1,0:T(8,128)} %get-tuple-element.20) | copy-start | bytes 3136516
  156.1 2.5 %copy-start.10 = (f32[2,8,16,1021]{3,2,1,0:T(8,128)S(1)}, f32[2,8,16,1021]{3,2,1,0:T(8,128)}, u32[]{:S(2)}) copy-start(f32[2,8,16,1021]{3,2,1,0:T(8,128)} %get-tuple-element.21) | copy-start | bytes 3136516
  156.1 2.8 %copy-start.11 = (f32[2,8,16,1022]{3,2,1,0:T(8,128)S(1)}, f32[2,8,16,1022]{3,2,1,0:T(8,128)}, u32[]{:S(2)}) copy-start(f32[2,8,16,1022]{3,2,1,0:T(8,128)} %get-tuple-element.18) | copy-start | bytes 3139588
  156.1 2.9 %copy-start.13 = (f32[8,16,1024]{2,1,0:T(8,128)S(1)}, f32[8,16,1024]{2,1,0:T(8,128)}, u32[]{:S(2)}) copy-start(f32[8,16,1024]{2,1,0:T(8,128)} %param.13) | copy-start | bytes 1572868
  172.6 9.8 %collective-permute-start.11 = (f32[2,8,8,512]{3,2,1,0:T(8,128)S(1)}, f32[2,8,8,512]{3,2,1,0:T(8,128)S(1)}, u32[]{:S(2)}, u32[]{:S(2)}) collective-permute-start(f32[2,8,8,512]{3,2,1,0:T(8,128)S(1)} %slice.525), channel_id=1, source_target_pairs={{0,8},{8,16},{16,24},{24,32},{32,40},{40,48},{48,56},{56,64},{64,7... | collective-permute-start | bytes 786440 | tf_op jit(solution)/shard_map/ppermute | solution.py:20
  174.6 9.6 %collective-permute-start.10 = (f32[2,8,8,512]{3,2,1,0:T(8,128)S(1)}, f32[2,8,8,512]{3,2,1,0:T(8,128)S(1)}, u32[]{:S(2)}, u32[]{:S(2)}) collective-permute-start(f32[2,8,8,512]{3,2,1,0:T(8,128)S(1)} %slice.525), channel_id=1, source_target_pairs={{8,0},{16,8},{24,16},{32,24},{40,32},{48,40},{56,48},{64,56},{72,6... | collective-permute-start | bytes 786440 | tf_op jit(solution)/shard_map/ppermute | solution.py:22
  184.3 1.3 copy-start.15
where the time goes:
time: 188 us; the launch traced here: 187 us
  other arithmetic  68.6 us (36%)
  starting transfers between devices  47.1 us (25%)
  local copies, waits for them, and re-layouts  42.4 us (23%)
  waiting for transfers between devices  27.3 us (15%)
    scatter-add x2, other arithmetic, local(): jnp.zeros((2 * volume,), jnp.float32).at[target].add(amounts, mode='drop')  48.9 us
    ppermute x6, starting transfers between devices, with_halo(): lax.ppermute(head, axis, [((i + 1) % count, i) for i in range(ends)])  35.4 us
    slice x2, local copies, waits for them, and re-layouts, local(): coarse = snapshot[:, :, ::2, ::2]  18 us
    ppermute x6, waiting for transfers between devices, with_halo(): lax.ppermute(tail, axis, [(i, (i + 1) % count) for i in range(ends)])  17.8 us
    ppermute x6, starting transfers between devices, with_halo(): lax.ppermute(tail, axis, [(i, (i + 1) % count) for i in range(ends)])  11.7 us
    ppermute x6, waiting for transfers between devices, with_halo(): lax.ppermute(head, axis, [((i + 1) % count, i) for i in range(ends)])  9.5 us
    add x2, other arithmetic, local(): 2.0 * fields - older  8.93 us
    slice x4, local copies, waits for them, and re-layouts, interior_laplace(): upper = jnp.concatenate((center[:, :, :, distance:], edge), axis=3)  6.86 us
  transfers between devices with their start and end apart: 12, of which 8 were waited for; matrix products, arithmetic and copies ran while one was open for 34% of the time, Pallas kernels for 0%

commit v1 on v0

v1 whole, which is shorter than its diff:
```python
import jax
import jax.numpy as jnp
from jax import lax
from jax.experimental import pallas as pl
from jax.experimental.pallas import tpu as pltpu
from jax.sharding import PartitionSpec as P

COEF = (-205.0 / 72.0, 8.0 / 5.0, -1.0 / 5.0, 8.0 / 315.0, -1.0 / 560.0)
NOFF = 17
REACH = 8
VX, VY, VZ = 8, 16, 1024
LT = VZ // 128
KT = LT // 2
F32 = jnp.float32

FIELD = (2, VX, LT, VY, 128)
XSLAB = (2, 4, LT, VY, 128)
XSLAB_COARSE = (2, 5, LT, VY, 128)
YSLAB = (2, 4, LT, 8, 128)
COARSE = (2, VX, KT, 8, 128)


def lane_iota(shape):
    return lax.broadcasted_iota(jnp.int32, shape, len(shape) - 1)


def pick(flag, yes, no):
    return jnp.where(flag, yes, no)


def compact_even(first, second):
    lane = lane_iota((8, 128))
    index = (2 * lane) & 127
    left = jnp.take_along_axis(first, index, axis=1)
    right = jnp.take_along_axis(second, index, axis=1)
    return jnp.where(lane < 64, left, right)


def coarse_tile(ref, lead, k):
    first = ref[lead + (2 * k, pl.ds(0, 8, stride=2), slice(None))]
    second = ref[lead + (2 * k + 1, pl.ds(0, 8, stride=2), slice(None))]
    return compact_even(first, second)


def pack_rows(top_ref, bottom_ref, f, l, low, high, gy_even):
    for p in range(VX):
        i, r = p % 4, 4 * (p // 4)
        top_ref[f, i, l, r : r + 4, :] = pick(gy_even, high[p], low[p])
        bottom_ref[f, i, l, r : r + 4, :] = pick(gy_even, low[p], high[p])


def first_pack_kernel(source_ref, receiver_ref, m1, m2, m3, m4):
    gx_even = lax.rem(lax.axis_index("gx"), 2) == 0
    gy_even = lax.rem(lax.axis_index("gy"), 2) == 0

    def tile(l, carry):
        lanes = pl.ds(pl.multiple_of(l * 128, 128), 128)
        for f, ref in enumerate((source_ref, receiver_ref)):
            for p in range(4):
                low = ref[p, :, lanes]
                high = ref[p + 4, :, lanes]
                m1[f, p, l] = pick(gx_even, high, low)
                m2[f, p, l] = pick(gx_even, low, high)
            low = [ref[p, 0:4, lanes] for p in range(VX)]
            high = [ref[p, 12:16, lanes] for p in range(VX)]
            pack_rows(m3, m4, f, l, low, high, gy_even)
        return carry

    lax.fori_loop(0, LT, tile, 0)


def star(ext, f, l, lane):
    centers = [ext[f, p, l + 1, 8 : 8 + VY, :] for p in range(VX)]
    out = []
    for p in range(VX):
        center = centers[p]
        after = ext[f, p, l + 2, 8 : 8 + VY, :]
        before = ext[f, p, l, 8 : 8 + VY, :]
        total = (3.0 * COEF[0]) * center
        for d in range(1, 5):
            near = pltpu.roll(jnp.where(lane >= d, center, after), 128 - d, 1)
            near = near + pltpu.roll(jnp.where(lane < 128 - d, center, before), d, 1)
            near = near + ext[f, p, l + 1, 8 + d : 8 + d + VY, :]
            near = near + ext[f, p, l + 1, 8 - d : 8 - d + VY, :]
            if p + d < VX:
                near = near + centers[p + d]
            if p - d >= 0:
                near = near + centers[p - d]
            total = total + COEF[d] * near
        out.append(total)
    return centers, out


def clear_ext(ext):
    def tile(i, carry):
        f, p = i // VX, lax.rem(i, VX)
        ext[f, p, :, 0:8, :] = jnp.zeros((LT + 2, 8, 128), F32)
        ext[f, p, :, 24:32, :] = jnp.zeros((LT + 2, 8, 128), F32)
        for l in (0, LT + 1):
            ext[f, p, l, 8:24, :] = jnp.zeros((VY, 128), F32)
        return carry

    lax.fori_loop(0, 2 * VX, tile, 0)


def first_local_kernel(
    source_ref,
    receiver_ref,
    source_prev_ref,
    receiver_prev_ref,
    velocity_ref,
    cells_ref,
    source_cells,
    source_wavelet,
    receiver_cells,
    receiver_traces,
    partial_ref,
    inject_ref,
    ext,
    inject_now,
    words_v,
    words_s,
    sem,
):
    anchor_x = lax.axis_index("gx") * VX
    anchor_y = lax.axis_index("gy") * VY

    cells = cells_ref[...]
    local_x = (cells >> 17) - anchor_x
    local_y = ((cells >> 10) & 127) - anchor_y
    inside = (local_x >= 0) & (local_x < VX) & (local_y >= 0) & (local_y < VY)
    bit = jnp.left_shift(1, lax.broadcasted_iota(jnp.int32, (32, 128), 0))
    words_v[...] = jnp.sum(jnp.where(inside, bit, 0), axis=0, keepdims=True)
    copy = pltpu.make_async_copy(words_v, words_s, sem)
    copy.start()

    clear_ext(ext)
    for f, ref in enumerate((source_ref, receiver_ref)):

        def fill(l, carry, f=f, ref=ref):
            lanes = pl.ds(pl.multiple_of(l * 128, 128), 128)
            for p in range(VX):
                ext[f, p, l + 1, 8 : 8 + VY, :] = ref[p, :, lanes]
                inject_ref[f, p, l] = jnp.zeros((VY, 128), F32)
                inject_now[f, p, l] = jnp.zeros((VY, 128), F32)
            return carry

        lax.fori_loop(0, LT, fill, 0)

    row_lane = lane_iota((1, 128))

    def add_point(f, cell, now, later):
        x = lax.shift_right_logical(cell, 17) - anchor_x
        y = (lax.shift_right_logical(cell, 10) & 127) - anchor_y
        z = cell & 1023
        l = lax.shift_right_logical(z, 7)
        here = row_lane == (z & 127)
        for ref, amount in ((inject_now, now), (inject_ref, later)):
            spot = (f, x, l, pl.ds(y, 1), slice(None))
            ref[spot] = ref[spot] + jnp.where(here, amount, 0.0)

    for j in range(source_cells.shape[0]):
        cell = source_cells[j]
        x = lax.shift_right_logical(cell, 17) - anchor_x
        y = (lax.shift_right_logical(cell, 10) & 127) - anchor_y
        here = (x >= 0) & (x < VX) & (y >= 0) & (y < VY)

        @pl.when(here)
        def _(cell=cell, j=j):
            add_point(0, cell, source_wavelet[0, j], source_wavelet[1, j])

    copy.wait()

    def word(w, carry):
        def one(bits):
            low = bits & (-bits)
            j = (31 - lax.clz(low)) * 128 + w
            add_point(1, receiver_cells[j], receiver_traces[0, j], receiver_traces[1, j])
            return bits & (bits - 1)

        lax.while_loop(lambda bits: bits != 0, one, words_s[0, w])
        return carry

    lax.fori_loop(0, 128, word, 0)

    lane = lane_iota((VY, 128))
    for f, older in enumerate((source_prev_ref, receiver_prev_ref)):

        def tile(l, carry, f=f, older=older):
            lanes = pl.ds(pl.multiple_of(l * 128, 128), 128)
            centers, totals = star(ext, f, l, lane)
            for p in range(VX):
                v = velocity_ref[p, :, lanes]
                partial_ref[f, p, l] = (2.0 * centers[p] - older[p, :, lanes]) + v * (totals[p] + inject_now[f, p, l])
            return carry

        lax.fori_loop(0, LT, tile, 0)


def second_local_kernel(now_ref, source_ref, receiver_ref, velocity_ref, inject_ref, partial_ref, ext):
    clear_ext(ext)
    for f in range(2):

        def fill(l, carry, f=f):
            for p in range(VX):
                ext[f, p, l + 1, 8 : 8 + VY, :] = now_ref[f, p, l]
            return carry

        lax.fori_loop(0, LT, fill, 0)
    lane = lane_iota((VY, 128))
    for f, older in enumerate((source_ref, receiver_ref)):

        def tile(l, carry, f=f, older=older):
            lanes = pl.ds(pl.multiple_of(l * 128, 128), 128)
            centers, totals = star(ext, f, l, lane)
            for p in range(VX):
                v = velocity_ref[p, :, lanes]
                partial_ref[f, p, l] = (2.0 * centers[p] - older[p, :, lanes]) + v * (totals[p] + inject_ref[f, p, l])
            return carry

        lax.fori_loop(0, LT, tile, 0)


def halo_terms(m1, m2, m3, m4, rows_low, rows_high, f, l, flags):
    gx_even, has_left, has_right, gy_even, has_below, has_above = flags
    left, right = [], []
    for p in range(4):
        a, b = m1[f, p, l], m2[f, p, l]
        left.append(jnp.where(has_left, pick(gx_even, b, a), 0.0))
        right.append(jnp.where(has_right, pick(gx_even, a, b), 0.0))
    out = []
    for p in range(VX):
        i, r = p % 4, 4 * (p // 4)
        a, b = m3[f, i, l, r : r + 4, :], m4[f, i, l, r : r + 4, :]
        rows_low[p, 0:4, :] = jnp.where(has_below, pick(gy_even, b, a), 0.0)
        rows_high[p, 8:12, :] = jnp.where(has_above, pick(gy_even, a, b), 0.0)
    for p in range(VX):
        below = COEF[1] * rows_low[p, 3:11, :]
        above = COEF[1] * rows_high[p, 1:9, :]
        for d in range(2, 5):
            below = below + COEF[d] * rows_low[p, 4 - d : 12 - d, :]
            above = above + COEF[d] * rows_high[p, d : d + 8, :]
        total = jnp.concatenate((below, above), axis=0)
        for d in range(1, 5):
            if p - d < 0:
                total = total + COEF[d] * left[4 + p - d]
            if p + d >= VX:
                total = total + COEF[d] * right[p + d - VX]
        out.append(total)
    return out


def flags_of():
    gx, gy = lax.axis_index("gx"), lax.axis_index("gy")
    return (
        lax.rem(gx, 2) == 0,
        gx > 0,
        gx < lax.axis_size("gx") - 1,
        lax.rem(gy, 2) == 0,
        gy > 0,
        gy < lax.axis_size("gy") - 1,
    )


def clear_rows(rows_low, rows_high):
    for p in range(VX):
        rows_low[p] = jnp.zeros((16, 128), F32)
        rows_high[p] = jnp.zeros((16, 128), F32)


def first_halo_kernel(
    partial_ref, velocity_ref, m1, m2, m3, m4, now_ref, s1, s2, s3, s4, coarse_ref, rows_low, rows_high
):
    flags = flags_of()
    gx_even, gy_even = flags[0], flags[3]
    clear_rows(rows_low, rows_high)
    for f in range(2):

        def tile(l, carry, f=f):
            lanes = pl.ds(pl.multiple_of(l * 128, 128), 128)
            terms = halo_terms(m1, m2, m3, m4, rows_low, rows_high, f, l, flags)
            new = []
            for p in range(VX):
                value = partial_ref[f, p, l] + velocity_ref[p, :, lanes] * terms[p]
                now_ref[f, p, l] = value
                new.append(value)
            for p in range(4):
                s1[f, p, l] = pick(gx_even, new[p + 4], new[p])
                s2[f, p, l] = pick(gx_even, new[p], new[p + 4])
            pack_rows(s3, s4, f, l, [v[0:4] for v in new], [v[12:16] for v in new], gy_even)
            return carry

        lax.fori_loop(0, LT, tile, 0)
        for k in range(KT):
            low = [coarse_tile(now_ref, (f, p), k) for p in range(4)]
            high = [coarse_tile(now_ref, (f, p + 4), k) for p in range(4)]
            for p in range(4):
                coarse_ref[f, p, k] = low[p]
                coarse_ref[f, p + 4, k] = high[p]
                at = p * KT + k
                rows = slice(8 * (at % 2), 8 * (at % 2) + 8)
                s1[f, 4, at // 2, rows, :] = pick(gx_even, low[p], high[p])
                s2[f, 4, at // 2, rows, :] = pick(gx_even, high[p], low[p])


def second_halo_kernel(
    partial_ref, velocity_ref, m1, m2, m3, m4, source_ref, receiver_ref, coarse_ref, rows_low, rows_high, stage
):
    flags = flags_of()
    clear_rows(rows_low, rows_high)
    for f, out in enumerate((source_ref, receiver_ref)):

        def tile(l, carry, f=f, out=out):
            lanes = pl.ds(pl.multiple_of(l * 128, 128), 128)
            terms = halo_terms(m1, m2, m3, m4, rows_low, rows_high, f, l, flags)
            for p in range(VX):
                value = partial_ref[f, p, l] + velocity_ref[p, :, lanes] * terms[p]
                out[p, :, lanes] = value
                stage[p, l] = value
            return carry

        lax.fori_loop(0, LT, tile, 0)
        for k in range(KT):
            for p in range(VX):
                coarse_ref[f, p, k] = coarse_tile(stage, (p,), k)


def lag_sum(fields, k, write):
    for offset in range(NOFF):
        h = offset - REACH
        for a in range(VX // 2):
            left, right = 2 * a - h + REACH, 2 * a + h + REACH
            write(offset, a, k, sum(s[left] * r[right] for s, r in fields))


def first_image_kernel(coarse_ref, m1, m2, image_ref):
    gx_even, has_left, has_right = flags_of()[:3]

    def planes(f, k):
        left, right = [], []
        near1 = [coarse_tile(m1, (f, p), k) for p in range(4)]
        near2 = [coarse_tile(m2, (f, p), k) for p in range(4)]
        far1, far2 = [], []
        for p in range(4):
            at = p * KT + k
            rows = slice(8 * (at % 2), 8 * (at % 2) + 8)
            far1.append(m1[f, 4, at // 2, rows, :])
            far2.append(m2[f, 4, at // 2, rows, :])
        for far, near in ((0, 1), (1, 0)):
            pass
        for p in range(4):
            left.append(jnp.where(has_left, pick(gx_even, far2[p], far1[p]), 0.0))
        for p in range(4):
            left.append(jnp.where(has_left, pick(gx_even, near2[p], near1[p]), 0.0))
        for p in range(4):
            right.append(jnp.where(has_right, pick(gx_even, near1[p], near2[p]), 0.0))
        for p in range(4):
            right.append(jnp.where(has_right, pick(gx_even, far1[p], far2[p]), 0.0))
        return left + [coarse_ref[f, p, k] for p in range(VX)] + right

    for k in range(KT):

        def write(o, a, k, value):
            image_ref[o, a, k] = value

        lag_sum([(planes(0, k), planes(1, k))], k, write)


def second_image_kernel(coarse_ref, m1, m2, before_ref, image_ref):
    gx_even, has_left, has_right = flags_of()[:3]

    def planes(f, k):
        left, right = [], []
        for p in range(VX):
            a, b = m1[f, p, k], m2[f, p, k]
            left.append(jnp.where(has_left, pick(gx_even, b, a), 0.0))
            right.append(jnp.where(has_right, pick(gx_even, a, b), 0.0))
        return left + [coarse_ref[f, p, k] for p in range(VX)] + right

    for k in range(KT):

        def write(o, a, k, value):
            image_ref[o, a, :, k * 128 : (k + 1) * 128] = before_ref[o, a, k] + value

        lag_sum([(planes(0, k), planes(1, k))], k, write)


VMEM = pl.BlockSpec(memory_space=pltpu.VMEM)
SMEM = pl.BlockSpec(memory_space=pltpu.SMEM)


def call(kernel, ins, outs, scratch=(), name=None, cost=0, limit=12):
    return pl.pallas_call(
        kernel,
        out_shape=[jax.ShapeDtypeStruct(s, F32) for s in outs],
        in_specs=[s for s, _ in ins],
        out_specs=[VMEM] * len(outs),
        scratch_shapes=list(scratch),
        name=name,
        cost_estimate=pl.CostEstimate(flops=cost, bytes_accessed=4 << 20, transcendentals=0),
        compiler_params=pltpu.CompilerParams(vmem_limit_bytes=limit << 20),
    )(*[a for _, a in ins])


def vmem(*arrays):
    return [(VMEM, a) for a in arrays]


def smem(*arrays):
    return [(SMEM, a) for a in arrays]


def matchings(axis):
    n = lax.axis_size(axis)
    inner = [(i, i ^ 1) for i in range(n)]
    outer = [(i, (i + 1) % n if i % 2 else (i - 1) % n) for i in range(n)]
    return inner, outer


def exchange(m1, m2, m3=None, m4=None):
    x_in, x_out = matchings("gx")
    y_in, y_out = matchings("gy")
    g2 = lax.ppermute(m2, "gx", x_out)
    if m3 is not None:
        g4 = lax.ppermute(m4, "gy", y_out)
        g3 = lax.ppermute(m3, "gy", y_in)
    g1 = lax.ppermute(m1, "gx", x_in)
    if m3 is None:
        return g1, g2
    return g1, g2, g3, g4


def local(
    source_now,
    source_prev,
    receiver_now,
    receiver_prev,
    velocity_sq,
    source_cells,
    source_wavelet,
    receiver_cells,
    receiver_traces,
):
    ext = pltpu.VMEM((2, VX, LT + 2, 32, 128), F32)
    rows = pltpu.VMEM((VX, 16, 128), F32)
    sends = call(
        first_pack_kernel, vmem(source_now, receiver_now), (XSLAB, XSLAB, YSLAB, YSLAB), name="pack"
    )
    got = exchange(*sends)
    partial, inject = call(
        first_local_kernel,
        vmem(source_now, receiver_now, source_prev, receiver_prev, velocity_sq, receiver_cells.reshape(32, 128))
        + smem(source_cells, source_wavelet, receiver_cells, receiver_traces),
        (FIELD, FIELD),
        (
            ext,
            pltpu.VMEM(FIELD, F32),
            pltpu.VMEM((1, 128), jnp.int32),
            pltpu.SMEM((1, 128), jnp.int32),
            pltpu.SemaphoreType.DMA,
        ),
        name="local1",
        cost=20_000_000,
    )
    now, s1, s2, s3, s4, coarse = call(
        first_halo_kernel,
        vmem(partial, velocity_sq, *got),
        (FIELD, XSLAB_COARSE, XSLAB_COARSE, YSLAB, YSLAB, COARSE),
        (rows, rows),
        name="halo1",
    )
    got = exchange(s1, s2, s3, s4)
    (partial,) = call(
        second_local_kernel,
        vmem(now, source_now, receiver_now, velocity_sq, inject),
        (FIELD,),
        (ext,),
        name="local2",
        cost=20_000_000,
    )
    source_next, receiver_next, last = call(
        second_halo_kernel,
        vmem(partial, velocity_sq, *got),
        ((VX, VY, VZ), (VX, VY, VZ), COARSE),
        (rows, rows, pltpu.VMEM((VX, LT, VY, 128), F32)),
        name="halo2",
    )
    far = exchange(last, last)
    (image,) = call(
        first_image_kernel, vmem(coarse, got[0], got[1]), ((NOFF, VX // 2, KT, 8, 128),), name="image1", cost=5_000_000
    )
    (image,) = call(
        second_image_kernel, vmem(last, *far, image), ((NOFF, VX // 2, 8, KT * 128),), name="image2"
    )
    return source_next, receiver_next, image


def solution(mesh):
    field = P("gx", "gy", None)
    return jax.shard_map(
        local,
        mesh=mesh,
        in_specs=(field,) * 5 + (P(),) * 4,
        out_specs=(field, field, P(None, "gx", "gy", None)),
        check_vma=False,
    )
```

time: 188 us -> 56.2 us (0.30)
  the two profiles are of different devices: /device:TPU:24 before, /device:TPU:0 now
where the time goes in v1:
time: 56.2 us; the launch traced here: 55.8 us
  waiting for transfers between devices  18.1 us (32%)
  Pallas kernels  16 us (28%)
  starting transfers between devices  14.9 us (27%)
  local copies, waits for them, and re-layouts  6 us (11%)
  between operations  0.77 us (1%)
    pallas_call x7, Pallas kernels, call(): pl.pallas_call(kernel, out_shape=[jax.ShapeDtypeStruct(s, F32) for s in o...  16 us
    ppermute x3, waiting for transfers between devices, exchange(): g2 = lax.ppermute(m2, 'gx', x_out)  13 us
    ppermute x2, starting transfers between devices, exchange(): g4 = lax.ppermute(m4, 'gy', y_out)  7.81 us
    unnamed x20, local copies, waits for them, and re-layouts  6 us
    ppermute x3, starting transfers between devices, exchange(): g2 = lax.ppermute(m2, 'gx', x_out)  5.33 us
    ppermute x2, waiting for transfers between devices, exchange(): g4 = lax.ppermute(m4, 'gy', y_out)  3.72 us
    ppermute x2, starting transfers between devices, exchange(): g3 = lax.ppermute(m3, 'gy', y_in)  1.58 us
    ppermute x2, waiting for transfers between devices, exchange(): g3 = lax.ppermute(m3, 'gy', y_in)  1.37 us
  transfers between devices with their start and end apart: 10, of which 4 were waited for; matrix products, arithmetic and copies ran while one was open for 0% of the time, Pallas kernels for 20%

profile of v1, /device:TPU:0, one launch (start us, length us, event | category | flops | bytes accessed | tf_op | source)
XLA Modules:
  0.0 55.8 jit_solution(3804981438257558689)
XLA Ops:
  0.7 1.1 %copy-done.1 = f32[8,16,1024]{2,1,0:T(8,128)S(1)} copy-done((f32[8,16,1024]{2,1,0:T(8,128)S(1)}, f32[8,16,1024]{2,1,0:T(8,128)}, u32[]{:S(2)}) %copy-start.1) | copy-done | bytes 524312
  1.7 1.0 %copy-done.2 = f32[8,16,1024]{2,1,0:T(8,128)S(1)} copy-done((f32[8,16,1024]{2,1,0:T(8,128)S(1)}, f32[8,16,1024]{2,1,0:T(8,128)}, u32[]{:S(2)}) %copy-start.2) | copy-done | bytes 524312
  2.8 0.3 pack.1
  3.1 0.1 collective-permute-start
  3.2 5.2 %collective-permute-start.1 = (f32[2,4,8,16,128]{4,3,2,1,0:T(8,128)S(1)}, f32[2,4,8,16,128]{4,3,2,1,0:T(8,128)S(1)}, u32[]{:S(2)}, u32[]{:S(2)}) collective-permute-start(f32[2,4,8,16,128]{4,3,2,1,0:T(8,128)S(1)} %get-tuple-element.20), channel_id=1, source_target_pairs={{0,120},{8,16},{16,8},{24,32},{32,24},{40,48},{48,40},{56,64},{64,... | collective-permute-start | bytes 1572872 | tf_op jit(solution)/shard_map/ppermute | solution.py:423
  8.4 1.5 %collective-permute-start.2 = (f32[2,4,8,8,128]{4,3,2,1,0:T(8,128)S(1)}, f32[2,4,8,8,128]{4,3,2,1,0:T(8,128)S(1)}, u32[]{:S(2)}, u32[]{:S(2)}) collective-permute-start(f32[2,4,8,8,128]{4,3,2,1,0:T(8,128)S(1)} %get-tuple-element.21), channel_id=1, source_target_pairs={{0,1},{1,0},{2,3},{3,2},{4,5},{5,4},{6,7},{7,6},{8,9},{9,8},{10,11... | collective-permute-start | bytes 786440 | tf_op jit(solution)/shard_map/ppermute | solution.py:426
  9.9 4.4 %collective-permute-start.3 = (f32[2,4,8,8,128]{4,3,2,1,0:T(8,128)S(1)}, f32[2,4,8,8,128]{4,3,2,1,0:T(8,128)S(1)}, u32[]{:S(2)}, u32[]{:S(2)}) collective-permute-start(f32[2,4,8,8,128]{4,3,2,1,0:T(8,128)S(1)} %get-tuple-element.22), channel_id=1, source_target_pairs={{0,7},{1,2},{2,1},{3,4},{4,3},{5,6},{6,5},{7,0},{8,15},{9,10},{10,... | collective-permute-start | bytes 786440 | tf_op jit(solution)/shard_map/ppermute | solution.py:425
  14.3 1.0 %copy-done.5 = f32[8,16,1024]{2,1,0:T(8,128)S(1)} copy-done((f32[8,16,1024]{2,1,0:T(8,128)S(1)}, f32[8,16,1024]{2,1,0:T(8,128)}, u32[]{:S(2)}) %copy-start.5) | copy-done | bytes 524312
  15.4 0.7 %copy-done.6 = s32[4096]{0:T(1024)S(1)} copy-done((s32[4096]{0:T(1024)S(1)}, s32[4096]{0:T(1024)}, u32[]{:S(2)}) %copy-start.6) | copy-done | bytes 16408
  16.1 0.8 %copy-done.7 = f32[2,4096]{1,0:T(2,128)S(1)} copy-done((f32[2,4096]{1,0:T(2,128)S(1)}, f32[2,4096]{1,0:T(2,128)}, u32[]{:S(2)}) %copy-start.7) | copy-done | bytes 32792
  16.8 0.7 %copy-done.8 = f32[2,4]{1,0:T(2,128)S(1)} copy-done((f32[2,4]{1,0:T(2,128)S(1)}, f32[2,4]{1,0:T(2,128)}, u32[]{:S(2)}) %copy-start.8) | copy-done | bytes 56
  17.5 0.7 %copy-done.9 = s32[4]{0:T(128)S(1)} copy-done((s32[4]{0:T(128)S(1)}, s32[4]{0:T(128)}, u32[]{:S(2)}) %copy-start.9) | copy-done | bytes 40
  18.2 7.4 %local1.1 = (f32[2,8,8,16,128]{4,3,2,1,0:T(8,128)S(1)}, f32[2,8,8,16,128]{4,3,2,1,0:T(8,128)S(1)}) custom-call(f32[8,16,1024]{2,1,0:T(8,128)S(1)} %copy-done.1, f32[8,16,1024]{2,1,0:T(8,128)S(1)} %copy-done.2, f32[8,16,1024]{2,1,0:T(8,128)S(1)} %copy-done.4, f32[8,16,1024]{2,1,0:T(8,128)S(1)} %copy-done.5, f32[8,16,1024]{2,1,0:T(8,128)S(1)} %copy-done, ...), custom_call_target="tpu_custom_call" | custom-call | flops 20000000 | bytes 4194304 | tf_op jit(solution)/shard_map/local1/pallas_call | solution.py:393
  25.6 0.0 collective-permute-done.2.m3
  25.6 0.0 collective-permute-done.3.m4
  25.6 0.0 copy-start.3
  25.6 1.2 %halo1.1 = (f32[2,8,8,16,128]{4,3,2,1,0:T(8,128)S(1)}, f32[2,5,8,16,128]{4,3,2,1,0:T(8,128)S(1)}, f32[2,5,8,16,128]{4,3,2,1,0:T(8,128)S(1)}, f32[2,4,8,8,128]{4,...) custom-call(f32[2,8,8,16,128]{4,3,2,1,0:T(8,128)S(1)} %get-tuple-element.18.partial_ref, ...), custom_call_target="tpu_custom_call" | custom-call | bytes 4194304 | tf_op jit(solution)/shard_map/halo1/pallas_call | solution.py:393
  26.8 0.1 collective-permute-start.4
  26.9 0.1 collective-permute-start.5
  27.0 0.1 collective-permute-start.6
  27.1 3.4 %collective-permute-start.7 = (f32[2,4,8,8,128]{4,3,2,1,0:T(8,128)S(1)}, f32[2,4,8,8,128]{4,3,2,1,0:T(8,128)S(1)}, u32[]{:S(2)}, u32[]{:S(2)}) collective-permute-start(f32[2,4,8,8,128]{4,3,2,1,0:T(8,128)S(1)} %get-tuple-element.28), channel_id=1, source_target_pairs={{0,7},{1,2},{2,1},{3,4},{4,3},{5,6},{6,5},{7,0},{8,15},{9,10},{10,... | collective-permute-start | bytes 786440 | tf_op jit(solution)/shard_map/ppermute | solution.py:425
  30.5 3.8 %local2.1.partial_ref = f32[2,8,8,16,128]{4,3,2,1,0:T(8,128)S(1)} custom-call(f32[2,8,8,16,128]{4,3,2,1,0:T(8,128)S(1)} %get-tuple-element.23.now_ref, f32[8,16,1024]{2,1,0:T(8,128)S(1)} %copy-done.1, f32[8,16,1024]{2,1,0:T(8,128)S(1)} %copy-done.3, f32[8,16,1024]{2,1,0:T(8,128)S(1)} %copy-done, f32[2,8,8,16,128]{4,3,2,1,0:T(8,128)S(1)} %get-tuple-element.24.inject_ref), custom_call_target="tpu_custom_call" | custom-call | flops 20000000 | bytes 4194304 | tf_op jit(solution)/shard_map/local2/pallas_call | solution.py:393
  34.3 1.4 %collective-permute-done.6.m3 = f32[2,4,8,8,128]{4,3,2,1,0:T(8,128)S(1)} collective-permute-done((f32[2,4,8,8,128]{4,3,2,1,0:T(8,128)S(1)}, f32[2,4,8,8,128]{4,3,2,1,0:T(8,128)S(1)}, u32[]{:S(2)}, u32[]{:S(2)}) %collective-permute-start.6) | collective-permute-done | bytes 262176 | tf_op jit(solution)/shard_map/ppermute | solution.py:426
  35.6 3.7 %collective-permute-done.7.m4 = f32[2,4,8,8,128]{4,3,2,1,0:T(8,128)S(1)} collective-permute-done((f32[2,4,8,8,128]{4,3,2,1,0:T(8,128)S(1)}, f32[2,4,8,8,128]{4,3,2,1,0:T(8,128)S(1)}, u32[]{:S(2)}, u32[]{:S(2)}) %collective-permute-start.7) | collective-permute-done | bytes 262176 | tf_op jit(solution)/shard_map/ppermute | solution.py:425
  39.4 5.4 %collective-permute-done.5.m2 = f32[2,5,8,16,128]{4,3,2,1,0:T(8,128)S(1)} collective-permute-done((f32[2,5,8,16,128]{4,3,2,1,0:T(8,128)S(1)}, f32[2,5,8,16,128]{4,3,2,1,0:T(8,128)S(1)}, u32[]{:S(2)}, u32[]{:S(2)}) %collective-permute-start.5) | collective-permute-done | bytes 655392 | tf_op jit(solution)/shard_map/ppermute | solution.py:423
  44.8 1.9 %halo2.1 = (f32[8,16,1024]{2,1,0:T(8,128)}, f32[8,16,1024]{2,1,0:T(8,128)}, f32[2,8,4,8,128]{4,3,2,1,0:T(8,128)S(1)}) custom-call(f32[2,8,8,16,128]{4,3,2,1,0:T(8,128)S(1)} %local2.1.partial_ref, f32[8,16,1024]{2,1,0:T(8,128)S(1)} %copy-done, f32[2,5,8,16,128]{4,3,2,1,0:T(8,128)S(1)} %collective-permute-done.4.m1, ...), custom_call_target="tpu_custom_call" | custom-call | bytes 4194304 | tf_op jit(solution)/shard_map/halo2/pallas_call | solution.py:393
  46.7 0.0 collective-permute-start.9
  46.7 0.0 collective-permute-start.8
  46.7 0.2 image1.1.before_ref
  46.9 7.7 %collective-permute-done.9.m2 = f32[2,8,4,8,128]{4,3,2,1,0:T(8,128)S(1)} collective-permute-done((f32[2,8,4,8,128]{4,3,2,1,0:T(8,128)S(1)}, f32[2,8,4,8,128]{4,3,2,1,0:T(8,128)S(1)}, u32[]{:S(2)}, u32[]{:S(2)}) %collective-permute-start.9) | collective-permute-done | bytes 262176 | tf_op jit(solution)/shard_map/ppermute | solution.py:423
  54.6 0.0 collective-permute-done.8.m1
  54.6 1.2 %image2.1 = f32[17,4,8,512]{3,2,1,0:T(8,128)} custom-call(f32[2,8,4,8,128]{4,3,2,1,0:T(8,128)S(1)} %get-tuple-element.31.coarse_ref, f32[2,8,4,8,128]{4,3,2,1,0:T(8,128)S(1)} %collective-permute-done.8.m1, f32[2,8,4,8,128]{4,3,2,1,0:T(8,128)S(1)} %collective-permute-done.9.m2, f32[17,4,4,8,128]{4,3,2,1,0:T(8,128)S(1)} %image1.1.before_ref), custom_call_target="tpu_custom_call" | custom-call | bytes 4194304 | tf_op jit(solution)/shard_map/image2/pallas_call | solution.py:393
  (15 shorter events, 0.0 us)
Async XLA Ops:
  0.6 13.7 %copy-start = (f32[8,16,1024]{2,1,0:T(8,128)S(1)}, f32[8,16,1024]{2,1,0:T(8,128)}, u32[]{:S(2)}) copy-start(f32[8,16,1024]{2,1,0:T(8,128)} %velocity_ref.7) | copy-start | bytes 1572868
  0.6 1.1 %copy-start.1 = (f32[8,16,1024]{2,1,0:T(8,128)S(1)}, f32[8,16,1024]{2,1,0:T(8,128)}, u32[]{:S(2)}) copy-start(f32[8,16,1024]{2,1,0:T(8,128)} %source_ref.5) | copy-start | bytes 1572868
  1.7 1.0 %copy-start.2 = (f32[8,16,1024]{2,1,0:T(8,128)S(1)}, f32[8,16,1024]{2,1,0:T(8,128)}, u32[]{:S(2)}) copy-start(f32[8,16,1024]{2,1,0:T(8,128)} %receiver_ref.5) | copy-start | bytes 1572868
  2.8 11.5 %copy-start.4 = (f32[8,16,1024]{2,1,0:T(8,128)S(1)}, f32[8,16,1024]{2,1,0:T(8,128)}, u32[]{:S(2)}) copy-start(f32[8,16,1024]{2,1,0:T(8,128)} %source_prev_ref.1) | copy-start | bytes 1572868
  3.1 22.5 %collective-permute-start = (f32[2,4,8,16,128]{4,3,2,1,0:T(8,128)S(1)}, f32[2,4,8,16,128]{4,3,2,1,0:T(8,128)S(1)}, u32[]{:S(2)}, u32[]{:S(2)}) collective-permute-start(f32[2,4,8,16,128]{4,3,2,1,0:T(8,128)S(1)} %get-tuple-element.19), channel_id=1, source_target_pairs={{0,8},{8,0},{16,24},{24,16},{32,40},{40,32},{48,56},{56,48},{64,72... | collective-permute-start | bytes 1572872 | tf_op jit(solution)/shard_map/ppermute | solution.py:427
  3.2 22.4 %collective-permute-start.1 = (f32[2,4,8,16,128]{4,3,2,1,0:T(8,128)S(1)}, f32[2,4,8,16,128]{4,3,2,1,0:T(8,128)S(1)}, u32[]{:S(2)}, u32[]{:S(2)}) collective-permute-start(f32[2,4,8,16,128]{4,3,2,1,0:T(8,128)S(1)} %get-tuple-element.20), channel_id=1, source_target_pairs={{0,120},{8,16},{16,8},{24,32},{32,24},{40,48},{48,40},{56,64},{64,... | collective-permute-start | bytes 1572872 | tf_op jit(solution)/shard_map/ppermute | solution.py:423
  8.4 17.2 %collective-permute-start.2 = (f32[2,4,8,8,128]{4,3,2,1,0:T(8,128)S(1)}, f32[2,4,8,8,128]{4,3,2,1,0:T(8,128)S(1)}, u32[]{:S(2)}, u32[]{:S(2)}) collective-permute-start(f32[2,4,8,8,128]{4,3,2,1,0:T(8,128)S(1)} %get-tuple-element.21), channel_id=1, source_target_pairs={{0,1},{1,0},{2,3},{3,2},{4,5},{5,4},{6,7},{7,6},{8,9},{9,8},{10,11... | collective-permute-start | bytes 786440 | tf_op jit(solution)/shard_map/ppermute | solution.py:426
  9.9 15.7 %collective-permute-start.3 = (f32[2,4,8,8,128]{4,3,2,1,0:T(8,128)S(1)}, f32[2,4,8,8,128]{4,3,2,1,0:T(8,128)S(1)}, u32[]{:S(2)}, u32[]{:S(2)}) collective-permute-start(f32[2,4,8,8,128]{4,3,2,1,0:T(8,128)S(1)} %get-tuple-element.22), channel_id=1, source_target_pairs={{0,7},{1,2},{2,1},{3,4},{4,3},{5,6},{6,5},{7,0},{8,15},{9,10},{10,... | collective-permute-start | bytes 786440 | tf_op jit(solution)/shard_map/ppermute | solution.py:425
  14.3 1.0 %copy-start.5 = (f32[8,16,1024]{2,1,0:T(8,128)S(1)}, f32[8,16,1024]{2,1,0:T(8,128)}, u32[]{:S(2)}) copy-start(f32[8,16,1024]{2,1,0:T(8,128)} %receiver_prev_ref.1) | copy-start | bytes 1572868
  15.4 0.7 %copy-start.6 = (s32[4096]{0:T(1024)S(1)}, s32[4096]{0:T(1024)}, u32[]{:S(2)}) copy-start(s32[4096]{0:T(1024)} %receiver_cells.1) | copy-start | bytes 49156
  16.1 0.8 %copy-start.7 = (f32[2,4096]{1,0:T(2,128)S(1)}, f32[2,4096]{1,0:T(2,128)}, u32[]{:S(2)}) copy-start(f32[2,4096]{1,0:T(2,128)} %receiver_traces.1) | copy-start | bytes 98308
  16.8 0.7 %copy-start.8 = (f32[2,4]{1,0:T(2,128)S(1)}, f32[2,4]{1,0:T(2,128)}, u32[]{:S(2)}) copy-start(f32[2,4]{1,0:T(2,128)} %source_wavelet.1) | copy-start | bytes 100
  17.5 0.7 %copy-start.9 = (s32[4]{0:T(128)S(1)}, s32[4]{0:T(128)}, u32[]{:S(2)}) copy-start(s32[4]{0:T(128)} %source_cells.1) | copy-start | bytes 52
  25.6 4.9 %copy-start.3 = (f32[8,16,1024]{2,1,0:T(8,128)S(1)}, f32[8,16,1024]{2,1,0:T(8,128)}, u32[]{:S(2)}) copy-start(f32[8,16,1024]{2,1,0:T(8,128)} %receiver_ref.5) | copy-start | bytes 1572868
  26.8 12.5 %collective-permute-start.4 = (f32[2,5,8,16,128]{4,3,2,1,0:T(8,128)S(1)}, f32[2,5,8,16,128]{4,3,2,1,0:T(8,128)S(1)}, u32[]{:S(2)}, u32[]{:S(2)}) collective-permute-start(f32[2,5,8,16,128]{4,3,2,1,0:T(8,128)S(1)} %get-tuple-element.25), channel_id=1, source_target_pairs={{0,8},{8,0},{16,24},{24,16},{32,40},{40,32},{48,56},{56,48},{64,72... | collective-permute-start | bytes 1966088 | tf_op jit(solution)/shard_map/ppermute | solution.py:427
  26.9 17.8 %collective-permute-start.5 = (f32[2,5,8,16,128]{4,3,2,1,0:T(8,128)S(1)}, f32[2,5,8,16,128]{4,3,2,1,0:T(8,128)S(1)}, u32[]{:S(2)}, u32[]{:S(2)}) collective-permute-start(f32[2,5,8,16,128]{4,3,2,1,0:T(8,128)S(1)} %get-tuple-element.26), channel_id=1, source_target_pairs={{0,120},{8,16},{16,8},{24,32},{32,24},{40,48},{48,40},{56,64},{64,... | collective-permute-start | bytes 1966088 | tf_op jit(solution)/shard_map/ppermute | solution.py:423
  27.0 8.6 %collective-permute-start.6 = (f32[2,4,8,8,128]{4,3,2,1,0:T(8,128)S(1)}, f32[2,4,8,8,128]{4,3,2,1,0:T(8,128)S(1)}, u32[]{:S(2)}, u32[]{:S(2)}) collective-permute-start(f32[2,4,8,8,128]{4,3,2,1,0:T(8,128)S(1)} %get-tuple-element.27), channel_id=1, source_target_pairs={{0,1},{1,0},{2,3},{3,2},{4,5},{5,4},{6,7},{7,6},{8,9},{9,8},{10,11... | collective-permute-start | bytes 786440 | tf_op jit(solution)/shard_map/ppermute | solution.py:426
  27.1 12.2 %collective-permute-start.7 = (f32[2,4,8,8,128]{4,3,2,1,0:T(8,128)S(1)}, f32[2,4,8,8,128]{4,3,2,1,0:T(8,128)S(1)}, u32[]{:S(2)}, u32[]{:S(2)}) collective-permute-start(f32[2,4,8,8,128]{4,3,2,1,0:T(8,128)S(1)} %get-tuple-element.28), channel_id=1, source_target_pairs={{0,7},{1,2},{2,1},{3,4},{4,3},{5,6},{6,5},{7,0},{8,15},{9,10},{10,... | collective-permute-start | bytes 786440 | tf_op jit(solution)/shard_map/ppermute | solution.py:425
  46.7 7.9 %collective-permute-start.9 = (f32[2,8,4,8,128]{4,3,2,1,0:T(8,128)S(1)}, f32[2,8,4,8,128]{4,3,2,1,0:T(8,128)S(1)}, u32[]{:S(2)}, u32[]{:S(2)}) collective-permute-start(f32[2,8,4,8,128]{4,3,2,1,0:T(8,128)S(1)} %get-tuple-element.31.coarse_ref), channel_id=1, source_target_pairs={{0,120},{8,16},{16,8},{24,32},{32,24},{40,48},{48,40},{56,64},{64,... | collective-permute-start | bytes 786440 | tf_op jit(solution)/shard_map/ppermute | solution.py:423
  46.7 7.9 %collective-permute-start.8 = (f32[2,8,4,8,128]{4,3,2,1,0:T(8,128)S(1)}, f32[2,8,4,8,128]{4,3,2,1,0:T(8,128)S(1)}, u32[]{:S(2)}, u32[]{:S(2)}) collective-permute-start(f32[2,8,4,8,128]{4,3,2,1,0:T(8,128)S(1)} %get-tuple-element.31.coarse_ref), channel_id=1, source_target_pairs={{0,8},{8,0},{16,24},{24,16},{32,40},{40,32},{48,56},{56,48},{64,72... | collective-permute-start | bytes 786440 | tf_op jit(solution)/shard_map/ppermute | solution.py:427

commit v2 on v1

--- a/solution.py
+++ b/solution.py
@@ -49,13 +49,21 @@
         bottom_ref[f, i, l, r : r + 4, :] = pick(gy_even, low[p], high[p])
 
 
-def first_pack_kernel(source_ref, receiver_ref, m1, m2, m3, m4):
+def first_pack_kernel(source_hbm, receiver_hbm, m1, m2, m3, m4, source_ref, receiver_ref, sems):
     gx_even = lax.rem(lax.axis_index("gx"), 2) == 0
     gy_even = lax.rem(lax.axis_index("gy"), 2) == 0
-
-    def tile(l, carry):
-        lanes = pl.ds(pl.multiple_of(l * 128, 128), 128)
-        for f, ref in enumerate((source_ref, receiver_ref)):
+    copies = [
+        pltpu.make_async_copy(source_hbm, source_ref, sems.at[0]),
+        pltpu.make_async_copy(receiver_hbm, receiver_ref, sems.at[1]),
+    ]
+    for copy in copies:
+        copy.start()
+
+    for f, ref in enumerate((source_ref, receiver_ref)):
+        copies[f].wait()
+
+        def tile(l, carry, f=f, ref=ref):
+            lanes = pl.ds(pl.multiple_of(l * 128, 128), 128)
             for p in range(4):
                 low = ref[p, :, lanes]
                 high = ref[p + 4, :, lanes]
@@ -64,9 +72,9 @@
             low = [ref[p, 0:4, lanes] for p in range(VX)]
             high = [ref[p, 12:16, lanes] for p in range(VX)]
             pack_rows(m3, m4, f, l, low, high, gy_even)
-        return carry
-
-    lax.fori_loop(0, LT, tile, 0)
+            return carry
+
+        lax.fori_loop(0, LT, tile, 0)
 
 
 def star(ext, f, l, lane):
@@ -106,46 +114,72 @@
 def first_local_kernel(
     source_ref,
     receiver_ref,
+    source_prev_hbm,
+    receiver_prev_hbm,
+    velocity_hbm,
+    cells_hbm,
+    source_cells_hbm,
+    source_wavelet_hbm,
+    receiver_cells_hbm,
+    receiver_traces_hbm,
+    partial_ref,
+    inject_ref,
+    velocity_ref,
+    ext,
+    inject_now,
     source_prev_ref,
     receiver_prev_ref,
-    velocity_ref,
     cells_ref,
     source_cells,
     source_wavelet,
     receiver_cells,
     receiver_traces,
-    partial_ref,
-    inject_ref,
-    ext,
-    inject_now,
     words_v,
     words_s,
-    sem,
+    sems,
+    word_sem,
 ):
     anchor_x = lax.axis_index("gx") * VX
     anchor_y = lax.axis_index("gy") * VY
 
+    pairs = (
+        (cells_hbm, cells_ref),
+        (source_cells_hbm, source_cells),
+        (source_wavelet_hbm, source_wavelet),
+        (receiver_cells_hbm, receiver_cells),
+        (receiver_traces_hbm, receiver_traces),
+        (velocity_hbm, velocity_ref),
+        (source_prev_hbm, source_prev_ref),
+        (receiver_prev_hbm, receiver_prev_ref),
+    )
+    copies = [pltpu.make_async_copy(a, b, sems.at[i]) for i, (a, b) in enumerate(pairs)]
+    for copy in copies:
+        copy.start()
+
+    clear_ext(ext)
+    for f, ref in enumerate((source_ref, receiver_ref)):
+
+        def fill(l, carry, f=f, ref=ref):
+            lanes = pl.ds(pl.multiple_of(l * 128, 128), 128)
+            for p in range(VX):
+                ext[f, p, l + 1, 8 : 8 + VY, :] = ref[p, :, lanes]
+                inject_ref[f, p, l] = jnp.zeros((VY, 128), F32)
+                inject_now[f, p, l] = jnp.zeros((VY, 128), F32)
+            return carry
+
+        lax.fori_loop(0, LT, fill, 0)
+
+    copies[0].wait()
     cells = cells_ref[...]
     local_x = (cells >> 17) - anchor_x
     local_y = ((cells >> 10) & 127) - anchor_y
     inside = (local_x >= 0) & (local_x < VX) & (local_y >= 0) & (local_y < VY)
     bit = jnp.left_shift(1, lax.broadcasted_iota(jnp.int32, (32, 128), 0))
     words_v[...] = jnp.sum(jnp.where(inside, bit, 0), axis=0, keepdims=True)
-    copy = pltpu.make_async_copy(words_v, words_s, sem)
-    copy.start()
-
-    clear_ext(ext)
-    for f, ref in enumerate((source_ref, receiver_ref)):
-
-        def fill(l, carry, f=f, ref=ref):
-            lanes = pl.ds(pl.multiple_of(l * 128, 128), 128)
-            for p in range(VX):
-                ext[f, p, l + 1, 8 : 8 + VY, :] = ref[p, :, lanes]
-                inject_ref[f, p, l] = jnp.zeros((VY, 128), F32)
-                inject_now[f, p, l] = jnp.zeros((VY, 128), F32)
-            return carry
-
-        lax.fori_loop(0, LT, fill, 0)
+    word_copy = pltpu.make_async_copy(words_v, words_s, word_sem)
+    word_copy.start()
+    for copy in copies[1:]:
+        copy.wait()
 
     row_lane = lane_iota((1, 128))
 
@@ -169,7 +203,7 @@
         def _(cell=cell, j=j):
             add_point(0, cell, source_wavelet[0, j], source_wavelet[1, j])
 
-    copy.wait()
+    word_copy.wait()
 
     def word(w, carry):
         def one(bits):
@@ -325,16 +359,14 @@
                 coarse_ref[f, p, k] = coarse_tile(stage, (p,), k)
 
 
-def lag_sum(fields, k, write):
-    for offset in range(NOFF):
-        h = offset - REACH
-        for a in range(VX // 2):
-            left, right = 2 * a - h + REACH, 2 * a + h + REACH
-            write(offset, a, k, sum(s[left] * r[right] for s, r in fields))
-
-
-def first_image_kernel(coarse_ref, m1, m2, image_ref):
+def first_image_kernel(coarse_ref, m1, m2, source_ref, receiver_ref, image_ref, source_hbm, receiver_hbm, sems):
     gx_even, has_left, has_right = flags_of()[:3]
+    copies = [
+        pltpu.make_async_copy(source_ref, source_hbm, sems.at[0]),
+        pltpu.make_async_copy(receiver_ref, receiver_hbm, sems.at[1]),
+    ]
+    for copy in copies:
+        copy.start()
 
     def planes(f, k):
         left, right = [], []
@@ -346,8 +378,6 @@
             rows = slice(8 * (at % 2), 8 * (at % 2) + 8)
             far1.append(m1[f, 4, at // 2, rows, :])
             far2.append(m2[f, 4, at // 2, rows, :])
-        for far, near in ((0, 1), (1, 0)):
-            pass
         for p in range(4):
             left.append(jnp.where(has_left, pick(gx_even, far2[p], far1[p]), 0.0))
         for p in range(4):
@@ -359,55 +389,67 @@
         return left + [coarse_ref[f, p, k] for p in range(VX)] + right
 
     for k in range(KT):
-
-        def write(o, a, k, value):
-            image_ref[o, a, k] = value
-
-        lag_sum([(planes(0, k), planes(1, k))], k, write)
-
-
-def second_image_kernel(coarse_ref, m1, m2, before_ref, image_ref):
+        source, receiver = planes(0, k), planes(1, k)
+        for offset in range(NOFF):
+            h = offset - REACH
+            for a in range(VX // 2):
+                image_ref[offset, a, k] = source[2 * a - h + REACH] * receiver[2 * a + h + REACH]
+    for copy in copies:
+        copy.wait()
+
+
+def second_image_kernel(coarse_ref, m1, m2, before_ref, image_hbm, span, stage, sems):
     gx_even, has_left, has_right = flags_of()[:3]
-
-    def planes(f, k):
-        left, right = [], []
+    for f in range(2):
         for p in range(VX):
-            a, b = m1[f, p, k], m2[f, p, k]
-            left.append(jnp.where(has_left, pick(gx_even, b, a), 0.0))
-            right.append(jnp.where(has_right, pick(gx_even, a, b), 0.0))
-        return left + [coarse_ref[f, p, k] for p in range(VX)] + right
-
-    for k in range(KT):
-
-        def write(o, a, k, value):
-            image_ref[o, a, :, k * 128 : (k + 1) * 128] = before_ref[o, a, k] + value
-
-        lag_sum([(planes(0, k), planes(1, k))], k, write)
+            span[f, p + REACH] = coarse_ref[f, p]
+            for k in range(KT):
+                a, b = m1[f, p, k], m2[f, p, k]
+                span[f, p, k] = jnp.where(has_left, pick(gx_even, b, a), 0.0)
+                span[f, p + REACH + VX, k] = jnp.where(has_right, pick(gx_even, a, b), 0.0)
+
+    copies = []
+    for a in range(VX // 2):
+        for offset in range(NOFF):
+            h = offset - REACH
+            left, right = 2 * a - h + REACH, 2 * a + h + REACH
+            for k in range(KT):
+                value = before_ref[offset, a, k] + span[0, left, k] * span[1, right, k]
+                stage[offset, a, :, k * 128 : (k + 1) * 128] = value
+        copy = pltpu.make_async_copy(stage.at[:, a], image_hbm.at[:, a], sems.at[a])
+        copy.start()
+        copies.append(copy)
+    for copy in copies:
+        copy.wait()
 
 
 VMEM = pl.BlockSpec(memory_space=pltpu.VMEM)
-SMEM = pl.BlockSpec(memory_space=pltpu.SMEM)
+HBM = pl.BlockSpec(memory_space=pltpu.HBM)
 
 
 def call(kernel, ins, outs, scratch=(), name=None, cost=0, limit=12):
     return pl.pallas_call(
         kernel,
-        out_shape=[jax.ShapeDtypeStruct(s, F32) for s in outs],
+        out_shape=[jax.ShapeDtypeStruct(s, F32) for _, s in outs],
         in_specs=[s for s, _ in ins],
-        out_specs=[VMEM] * len(outs),
+        out_specs=[s for s, _ in outs],
         scratch_shapes=list(scratch),
         name=name,
         cost_estimate=pl.CostEstimate(flops=cost, bytes_accessed=4 << 20, transcendentals=0),
         compiler_params=pltpu.CompilerParams(vmem_limit_bytes=limit << 20),
-    )(*[a for _, a in ins])
-
-
-def vmem(*arrays):
-    return [(VMEM, a) for a in arrays]
-
-
-def smem(*arrays):
-    return [(SMEM, a) for a in arrays]
+    )(*[pltpu.with_memory_space_constraint(a, pltpu.HBM) if s is HBM else a for s, a in ins])
+
+
+def vmem(*items):
+    return [(VMEM, a) for a in items]
+
+
+def hbm(*items):
+    return [(HBM, a) for a in items]
+
+
+def dma(count):
+    return pltpu.SemaphoreType.DMA((count,))
 
 
 def matchings(axis):
@@ -417,12 +459,25 @@
     return inner, outer
 
 
+def y_outer():
+    nx, ny = lax.axis_size("gx"), lax.axis_size("gy")
+    pairs = []
+    for x in range(nx):
+        for y in range(ny):
+            other = y + 1 if y % 2 else y - 1
+            if 0 <= other < ny:
+                pairs.append((x * ny + y, x * ny + other))
+            else:
+                pairs.append((x * ny + y, (x ^ 1) * ny + y))
+    return pairs
+
+
 def exchange(m1, m2, m3=None, m4=None):
     x_in, x_out = matchings("gx")
-    y_in, y_out = matchings("gy")
+    y_in, _ = matchings("gy")
     g2 = lax.ppermute(m2, "gx", x_out)
     if m3 is not None:
-        g4 = lax.ppermute(m4, "gy", y_out)
+        g4 = lax.ppermute(m4, ("gx", "gy"), y_outer())
         g3 = lax.ppermute(m3, "gy", y_in)
     g1 = lax.ppermute(m1, "gx", x_in)
     if m3 is None:
@@ -443,20 +498,34 @@
 ):
     ext = pltpu.VMEM((2, VX, LT + 2, 32, 128), F32)
     rows = pltpu.VMEM((VX, 16, 128), F32)
-    sends = call(
-        first_pack_kernel, vmem(source_now, receiver_now), (XSLAB, XSLAB, YSLAB, YSLAB), name="pack"
+    block = (VX, VY, VZ)
+    *sends, source, receiver = call(
+        first_pack_kernel,
+        hbm(source_now, receiver_now),
+        vmem(XSLAB, XSLAB, YSLAB, YSLAB, block, block),
+        (dma(2),),
+        name="pack",
     )
     got = exchange(*sends)
-    partial, inject = call(
+    partial, inject, velocity = call(
         first_local_kernel,
-        vmem(source_now, receiver_now, source_prev, receiver_prev, velocity_sq, receiver_cells.reshape(32, 128))
-        + smem(source_cells, source_wavelet, receiver_cells, receiver_traces),
-        (FIELD, FIELD),
+        vmem(source, receiver)
+        + hbm(source_prev, receiver_prev, velocity_sq, receiver_cells.reshape(32, 128))
+        + hbm(source_cells, source_wavelet, receiver_cells, receiver_traces),
+        vmem(FIELD, FIELD, block),
         (
             ext,
             pltpu.VMEM(FIELD, F32),
+            pltpu.VMEM(block, F32),
+            pltpu.VMEM(block, F32),
+            pltpu.VMEM((32, 128), jnp.int32),
+            pltpu.SMEM(source_cells.shape, jnp.int32),
+            pltpu.SMEM(source_wavelet.shape, F32),
+            pltpu.SMEM(receiver_cells.shape, jnp.int32),
+            pltpu.SMEM(receiver_traces.shape, F32),
             pltpu.VMEM((1, 128), jnp.int32),
             pltpu.SMEM((1, 128), jnp.int32),
+            dma(8),
             pltpu.SemaphoreType.DMA,
         ),
         name="local1",
@@ -464,33 +533,46 @@
     )
     now, s1, s2, s3, s4, coarse = call(
         first_halo_kernel,
-        vmem(partial, velocity_sq, *got),
-        (FIELD, XSLAB_COARSE, XSLAB_COARSE, YSLAB, YSLAB, COARSE),
+        vmem(partial, velocity, *got),
+        vmem(FIELD, XSLAB_COARSE, XSLAB_COARSE, YSLAB, YSLAB, COARSE),
         (rows, rows),
         name="halo1",
     )
     got = exchange(s1, s2, s3, s4)
     (partial,) = call(
         second_local_kernel,
-        vmem(now, source_now, receiver_now, velocity_sq, inject),
-        (FIELD,),
+        vmem(now, source, receiver, velocity, inject),
+        vmem(FIELD),
         (ext,),
         name="local2",
         cost=20_000_000,
     )
-    source_next, receiver_next, last = call(
+    source, receiver, last = call(
         second_halo_kernel,
-        vmem(partial, velocity_sq, *got),
-        ((VX, VY, VZ), (VX, VY, VZ), COARSE),
+        vmem(partial, velocity, *got),
+        vmem(block, block, COARSE),
         (rows, rows, pltpu.VMEM((VX, LT, VY, 128), F32)),
         name="halo2",
     )
     far = exchange(last, last)
+    image, source_next, receiver_next = call(
+        first_image_kernel,
+        vmem(coarse, got[0], got[1], source, receiver),
+        vmem((NOFF, VX // 2, KT, 8, 128)) + hbm(block, block),
+        (dma(2),),
+        name="image1",
+        cost=5_000_000,
+    )
     (image,) = call(
-        first_image_kernel, vmem(coarse, got[0], got[1]), ((NOFF, VX // 2, KT, 8, 128),), name="image1", cost=5_000_000
-    )
-    (image,) = call(
-        second_image_kernel, vmem(last, *far, image), ((NOFF, VX // 2, 8, KT * 128),), name="image2"
+        second_image_kernel,
+        vmem(last, *far, image),
+        hbm((NOFF, VX // 2, 8, KT * 128)),
+        (
+            pltpu.VMEM((2, 2 * REACH + VX, KT, 8, 128), F32),
+            pltpu.VMEM((NOFF, VX // 2, 8, KT * 128), F32),
+            dma(VX // 2),
+        ),
+        name="image2",
     )
     return source_next, receiver_next, image
 

time: 56.2 us -> 49.4 us (0.88)
  local copies, waits for them, and re-layouts: 6 us -> 0 us
  waiting for transfers between devices: 18.1 us -> 17.1 us
  Pallas kernels: 16 us -> 16.9 us
    ppermute x2, starting transfers between devices: 7.81 us -> 0.01 us  [exchange(): g4 = lax.ppermute(m4, ('gx', 'gy'), y_outer())]
    ppermute x3, starting transfers between devices: 5.33 us -> 12.8 us  [exchange(): g2 = lax.ppermute(m2, 'gx', x_out)]
    unnamed x20 -> x0, local copies, waits for them, and re-layouts: 6 us -> none
    ppermute x2, waiting for transfers between devices: 3.72 us -> 0.01 us  [exchange(): g4 = lax.ppermute(m4, ('gx', 'gy'), y_outer())]
    ppermute x3, waiting for transfers between devices: 13 us -> 14.5 us  [exchange(): g2 = lax.ppermute(m2, 'gx', x_out)]
    ppermute x2, waiting for transfers between devices: 1.37 us -> 2.58 us  [exchange(): g3 = lax.ppermute(m3, 'gy', y_in)]
    pallas_call x7, Pallas kernels: 16 us -> 16.9 us  [call(): pl.pallas_call(kernel, out_shape=[jax.ShapeDtypeStruct(s, F32) for _, s i...]
  transfers between devices with their start and end apart: 10 -> 10, of which waited for: 4 -> 4; matrix products, arithmetic and copies ran while one was open for 0% -> 0% of each run, Pallas kernels for 20% -> 25%
where the time goes in v2:
time: 49.4 us; the launch traced here: 49.2 us
  waiting for transfers between devices  17.1 us (35%)
  Pallas kernels  16.9 us (34%)
  starting transfers between devices  14.5 us (29%)
  between operations  0.72 us (1%)
    pallas_call x7, Pallas kernels, call(): pl.pallas_call(kernel, out_shape=[jax.ShapeDtypeStruct(s, F32) for _, s i...  16.9 us
    ppermute x3, waiting for transfers between devices, exchange(): g2 = lax.ppermute(m2, 'gx', x_out)  14.5 us
    ppermute x3, starting transfers between devices, exchange(): g2 = lax.ppermute(m2, 'gx', x_out)  12.8 us
    ppermute x2, waiting for transfers between devices, exchange(): g3 = lax.ppermute(m3, 'gy', y_in)  2.58 us
    ppermute x2, starting transfers between devices, exchange(): g3 = lax.ppermute(m3, 'gy', y_in)  1.49 us
  transfers between devices with their start and end apart: 10, of which 4 were waited for; matrix products, arithmetic and copies ran while one was open for 0% of the time, Pallas kernels for 25%

profile of v2, /device:TPU:0, one launch (start us, length us, event | category | flops | bytes accessed | tf_op | source)
XLA Modules:
  0.0 49.2 jit_solution(692134315557673363)
XLA Ops:
  0.6 1.4 %pack.1 = (f32[2,4,8,16,128]{4,3,2,1,0:T(8,128)S(1)}, f32[2,4,8,16,128]{4,3,2,1,0:T(8,128)S(1)}, f32[2,4,8,8,128]{4,3,2,1,0:T(8,128)S(1)}, f32[2,4,8,8,128]{4,3,...) custom-call(f32[8,16,1024]{2,1,0:T(8,128)} %source_hbm.1, f32[8,16,1024]{2,1,0:T(8,128)} %receiver_hbm.1), custom_call_target="tpu_custom_call" | custom-call | bytes 4194304 | tf_op jit(solution)/shard_map/pack/pallas_call | solution.py:431
  2.0 0.1 collective-permute-start
  2.1 5.2 %collective-permute-start.1 = (f32[2,4,8,16,128]{4,3,2,1,0:T(8,128)S(1)}, f32[2,4,8,16,128]{4,3,2,1,0:T(8,128)S(1)}, u32[]{:S(2)}, u32[]{:S(2)}) collective-permute-start(f32[2,4,8,16,128]{4,3,2,1,0:T(8,128)S(1)} %get-tuple-element.29), channel_id=1, source_target_pairs={{0,120},{8,16},{16,8},{24,32},{32,24},{40,48},{48,40},{56,64},{64,... | collective-permute-start | bytes 1572872 | tf_op jit(solution)/shard_map/ppermute | solution.py:478
  7.3 1.5 %collective-permute-start.2 = (f32[2,4,8,8,128]{4,3,2,1,0:T(8,128)S(1)}, f32[2,4,8,8,128]{4,3,2,1,0:T(8,128)S(1)}, u32[]{:S(2)}, u32[]{:S(2)}) collective-permute-start(f32[2,4,8,8,128]{4,3,2,1,0:T(8,128)S(1)} %get-tuple-element.30), channel_id=1, source_target_pairs={{0,1},{1,0},{2,3},{3,2},{4,5},{5,4},{6,7},{7,6},{8,9},{9,8},{10,11... | collective-permute-start | bytes 786440 | tf_op jit(solution)/shard_map/ppermute | solution.py:481
  8.8 0.0 collective-permute-start.3
  8.8 7.3 %local1.1 = (f32[2,8,8,16,128]{4,3,2,1,0:T(8,128)S(1)}, f32[2,8,8,16,128]{4,3,2,1,0:T(8,128)S(1)}, f32[8,16,1024]{2,1,0:T(8,128)S(1)}) custom-call(f32[8,16,1024]{2,1,0:T(8,128)S(1)} %get-tuple-element.24.source_ref, f32[8,16,1024]{2,1,0:T(8,128)S(1)} %get-tuple-element.25.receiver_ref, f32[8,16,1024]{2,1,0:T(8,128)} %source_prev_hbm.1, ...), custom_call_target="tpu_custom_call" | custom-call | flops 20000000 | bytes 4194304 | tf_op jit(solution)/shard_map/local1/pallas_call | solution.py:431
  16.2 0.0 collective-permute-done.2.m3
  16.2 0.0 collective-permute-done.3.m4
  16.2 0.0 collective-permute-done.m1
  16.2 3.6 %collective-permute-done.1.m2 = f32[2,4,8,16,128]{4,3,2,1,0:T(8,128)S(1)} collective-permute-done((f32[2,4,8,16,128]{4,3,2,1,0:T(8,128)S(1)}, f32[2,4,8,16,128]{4,3,2,1,0:T(8,128)S(1)}, u32[]{:S(2)}, u32[]{:S(2)}) %collective-permute-start.1) | collective-permute-done | bytes 524320 | tf_op jit(solution)/shard_map/ppermute | solution.py:478
  19.8 1.2 %halo1.1 = (f32[2,8,8,16,128]{4,3,2,1,0:T(8,128)S(1)}, f32[2,5,8,16,128]{4,3,2,1,0:T(8,128)S(1)}, f32[2,5,8,16,128]{4,3,2,1,0:T(8,128)S(1)}, f32[2,4,8,8,128]{4,...) custom-call(f32[2,8,8,16,128]{4,3,2,1,0:T(8,128)S(1)} %get-tuple-element.26.partial_ref, ...), custom_call_target="tpu_custom_call" | custom-call | bytes 4194304 | tf_op jit(solution)/shard_map/halo1/pallas_call | solution.py:431
  21.1 0.1 collective-permute-start.4
  21.1 3.9 %collective-permute-start.5 = (f32[2,5,8,16,128]{4,3,2,1,0:T(8,128)S(1)}, f32[2,5,8,16,128]{4,3,2,1,0:T(8,128)S(1)}, u32[]{:S(2)}, u32[]{:S(2)}) collective-permute-start(f32[2,5,8,16,128]{4,3,2,1,0:T(8,128)S(1)} %get-tuple-element.34), channel_id=1, source_target_pairs={{0,120},{8,16},{16,8},{24,32},{32,24},{40,48},{48,40},{56,64},{64,... | collective-permute-start | bytes 1966088 | tf_op jit(solution)/shard_map/ppermute | solution.py:478
  25.1 0.0 collective-permute-start.6
  25.1 0.0 collective-permute-start.7
  25.1 3.8 %local2.1.partial_ref = f32[2,8,8,16,128]{4,3,2,1,0:T(8,128)S(1)} custom-call(f32[2,8,8,16,128]{4,3,2,1,0:T(8,128)S(1)} %get-tuple-element.35.now_ref, f32[8,16,1024]{2,1,0:T(8,128)S(1)} %get-tuple-element.24.source_ref, f32[8,16,1024]{2,1,0:T(8,128)S(1)} %get-tuple-element.25.receiver_ref, f32[8,16,1024]{2,1,0:T(8,128)S(1)} %get-tuple-element.27.velocity_ref, ...), custom_call_target="tpu_custom_call" | custom-call | flops 20000000 | bytes 4194304 | tf_op jit(solution)/shard_map/local2/pallas_call | solution.py:431
  28.9 2.6 %collective-permute-done.6.m3 = f32[2,4,8,8,128]{4,3,2,1,0:T(8,128)S(1)} collective-permute-done((f32[2,4,8,8,128]{4,3,2,1,0:T(8,128)S(1)}, f32[2,4,8,8,128]{4,3,2,1,0:T(8,128)S(1)}, u32[]{:S(2)}, u32[]{:S(2)}) %collective-permute-start.6) | collective-permute-done | bytes 262176 | tf_op jit(solution)/shard_map/ppermute | solution.py:481
  31.5 0.0 collective-permute-done.7.m4
  31.5 0.0 collective-permute-done.4.m1
  31.5 7.5 %collective-permute-done.5.m2 = f32[2,5,8,16,128]{4,3,2,1,0:T(8,128)S(1)} collective-permute-done((f32[2,5,8,16,128]{4,3,2,1,0:T(8,128)S(1)}, f32[2,5,8,16,128]{4,3,2,1,0:T(8,128)S(1)}, u32[]{:S(2)}, u32[]{:S(2)}) %collective-permute-start.5) | collective-permute-done | bytes 655392 | tf_op jit(solution)/shard_map/ppermute | solution.py:478
  39.0 1.1 %halo2.1 = (f32[8,16,1024]{2,1,0:T(8,128)S(1)}, f32[8,16,1024]{2,1,0:T(8,128)S(1)}, f32[2,8,4,8,128]{4,3,2,1,0:T(8,128)S(1)}) custom-call(f32[2,8,8,16,128]{4,3,2,1,0:T(8,128)S(1)} %local2.1.partial_ref, f32[8,16,1024]{2,1,0:T(8,128)S(1)} %get-tuple-element.27.velocity_ref, f32[2,5,8,16,128]{4,3,2,1,0:T(8,128)S(1)} %collective-permute-done.4.m1, ...), custom_call_target="tpu_custom_call" | custom-call | bytes 4194304 | tf_op jit(solution)/shard_map/halo2/pallas_call | solution.py:431
  40.1 3.6 %collective-permute-start.9 = (f32[2,8,4,8,128]{4,3,2,1,0:T(8,128)S(1)}, f32[2,8,4,8,128]{4,3,2,1,0:T(8,128)S(1)}, u32[]{:S(2)}, u32[]{:S(2)}) collective-permute-start(f32[2,8,4,8,128]{4,3,2,1,0:T(8,128)S(1)} %get-tuple-element.43.coarse_ref), channel_id=1, source_target_pairs={{0,120},{8,16},{16,8},{24,32},{32,24},{40,48},{48,40},{56,64},{64,... | collective-permute-start | bytes 786440 | tf_op jit(solution)/shard_map/ppermute | solution.py:478
  43.8 0.0 collective-permute-start.8
  43.8 1.0 %image1.1 = (f32[17,4,4,8,128]{4,3,2,1,0:T(8,128)S(1)}, f32[8,16,1024]{2,1,0:T(8,128)}, f32[8,16,1024]{2,1,0:T(8,128)}) custom-call(f32[2,8,4,8,128]{4,3,2,1,0:T(8,128)S(1)} %get-tuple-element.32.coarse_ref, f32[2,5,8,16,128]{4,3,2,1,0:T(8,128)S(1)} %collective-permute-done.4.m1, f32[2,5,8,16,128]{4,3,2,1,0:T(8,128)S(1)} %collective-permute-done.5.m2, ...), custom_call_target="tpu_custom_call" | custom-call | flops 5000000 | bytes 4194304 | tf_op jit(solution)/shard_map/image1/pallas_call | solution.py:431
  44.8 3.3 %collective-permute-done.9.m2 = f32[2,8,4,8,128]{4,3,2,1,0:T(8,128)S(1)} collective-permute-done((f32[2,8,4,8,128]{4,3,2,1,0:T(8,128)S(1)}, f32[2,8,4,8,128]{4,3,2,1,0:T(8,128)S(1)}, u32[]{:S(2)}, u32[]{:S(2)}) %collective-permute-start.9) | collective-permute-done | bytes 262176 | tf_op jit(solution)/shard_map/ppermute | solution.py:478
  48.1 0.0 collective-permute-done.8.m1
  48.1 1.1 %image2.1 = f32[17,4,8,512]{3,2,1,0:T(8,128)} custom-call(f32[2,8,4,8,128]{4,3,2,1,0:T(8,128)S(1)} %get-tuple-element.43.coarse_ref, f32[2,8,4,8,128]{4,3,2,1,0:T(8,128)S(1)} %collective-permute-done.8.m1, f32[2,8,4,8,128]{4,3,2,1,0:T(8,128)S(1)} %collective-permute-done.9.m2, f32[17,4,4,8,128]{4,3,2,1,0:T(8,128)S(1)} %get-tuple-element.44.before_ref), custom_call_target="tpu_custom_call" | custom-call | bytes 4194304 | tf_op jit(solution)/shard_map/image2/pallas_call | solution.py:431
Async XLA Ops:
  2.0 14.2 %collective-permute-start = (f32[2,4,8,16,128]{4,3,2,1,0:T(8,128)S(1)}, f32[2,4,8,16,128]{4,3,2,1,0:T(8,128)S(1)}, u32[]{:S(2)}, u32[]{:S(2)}) collective-permute-start(f32[2,4,8,16,128]{4,3,2,1,0:T(8,128)S(1)} %get-tuple-element.28), channel_id=1, source_target_pairs={{0,8},{8,0},{16,24},{24,16},{32,40},{40,32},{48,56},{56,48},{64,72... | collective-permute-start | bytes 1572872 | tf_op jit(solution)/shard_map/ppermute | solution.py:482
  2.1 17.7 %collective-permute-start.1 = (f32[2,4,8,16,128]{4,3,2,1,0:T(8,128)S(1)}, f32[2,4,8,16,128]{4,3,2,1,0:T(8,128)S(1)}, u32[]{:S(2)}, u32[]{:S(2)}) collective-permute-start(f32[2,4,8,16,128]{4,3,2,1,0:T(8,128)S(1)} %get-tuple-element.29), channel_id=1, source_target_pairs={{0,120},{8,16},{16,8},{24,32},{32,24},{40,48},{48,40},{56,64},{64,... | collective-permute-start | bytes 1572872 | tf_op jit(solution)/shard_map/ppermute | solution.py:478
  7.3 8.8 %collective-permute-start.2 = (f32[2,4,8,8,128]{4,3,2,1,0:T(8,128)S(1)}, f32[2,4,8,8,128]{4,3,2,1,0:T(8,128)S(1)}, u32[]{:S(2)}, u32[]{:S(2)}) collective-permute-start(f32[2,4,8,8,128]{4,3,2,1,0:T(8,128)S(1)} %get-tuple-element.30), channel_id=1, source_target_pairs={{0,1},{1,0},{2,3},{3,2},{4,5},{5,4},{6,7},{7,6},{8,9},{9,8},{10,11... | collective-permute-start | bytes 786440 | tf_op jit(solution)/shard_map/ppermute | solution.py:481
  8.8 7.3 %collective-permute-start.3 = (f32[2,4,8,8,128]{4,3,2,1,0:T(8,128)S(1)}, f32[2,4,8,8,128]{4,3,2,1,0:T(8,128)S(1)}, u32[]{:S(2)}, u32[]{:S(2)}) collective-permute-start(f32[2,4,8,8,128]{4,3,2,1,0:T(8,128)S(1)} %get-tuple-element.31), channel_id=1, source_target_pairs={{0,8},{1,2},{2,1},{3,4},{4,3},{5,6},{6,5},{7,15},{8,0},{9,10},{10,... | collective-permute-start | bytes 786440 | tf_op jit(solution)/shard_map/ppermute | solution.py:480
  21.1 10.4 %collective-permute-start.4 = (f32[2,5,8,16,128]{4,3,2,1,0:T(8,128)S(1)}, f32[2,5,8,16,128]{4,3,2,1,0:T(8,128)S(1)}, u32[]{:S(2)}, u32[]{:S(2)}) collective-permute-start(f32[2,5,8,16,128]{4,3,2,1,0:T(8,128)S(1)} %get-tuple-element.33), channel_id=1, source_target_pairs={{0,8},{8,0},{16,24},{24,16},{32,40},{40,32},{48,56},{56,48},{64,72... | collective-permute-start | bytes 1966088 | tf_op jit(solution)/shard_map/ppermute | solution.py:482
  21.1 17.8 %collective-permute-start.5 = (f32[2,5,8,16,128]{4,3,2,1,0:T(8,128)S(1)}, f32[2,5,8,16,128]{4,3,2,1,0:T(8,128)S(1)}, u32[]{:S(2)}, u32[]{:S(2)}) collective-permute-start(f32[2,5,8,16,128]{4,3,2,1,0:T(8,128)S(1)} %get-tuple-element.34), channel_id=1, source_target_pairs={{0,120},{8,16},{16,8},{24,32},{32,24},{40,48},{48,40},{56,64},{64,... | collective-permute-start | bytes 1966088 | tf_op jit(solution)/shard_map/ppermute | solution.py:478
  25.1 6.4 %collective-permute-start.6 = (f32[2,4,8,8,128]{4,3,2,1,0:T(8,128)S(1)}, f32[2,4,8,8,128]{4,3,2,1,0:T(8,128)S(1)}, u32[]{:S(2)}, u32[]{:S(2)}) collective-permute-start(f32[2,4,8,8,128]{4,3,2,1,0:T(8,128)S(1)} %get-tuple-element.37), channel_id=1, source_target_pairs={{0,1},{1,0},{2,3},{3,2},{4,5},{5,4},{6,7},{7,6},{8,9},{9,8},{10,11... | collective-permute-start | bytes 786440 | tf_op jit(solution)/shard_map/ppermute | solution.py:481
  25.1 6.4 %collective-permute-start.7 = (f32[2,4,8,8,128]{4,3,2,1,0:T(8,128)S(1)}, f32[2,4,8,8,128]{4,3,2,1,0:T(8,128)S(1)}, u32[]{:S(2)}, u32[]{:S(2)}) collective-permute-start(f32[2,4,8,8,128]{4,3,2,1,0:T(8,128)S(1)} %get-tuple-element.38), channel_id=1, source_target_pairs={{0,8},{1,2},{2,1},{3,4},{4,3},{5,6},{6,5},{7,15},{8,0},{9,10},{10,... | collective-permute-start | bytes 786440 | tf_op jit(solution)/shard_map/ppermute | solution.py:480
  40.1 8.0 %collective-permute-start.9 = (f32[2,8,4,8,128]{4,3,2,1,0:T(8,128)S(1)}, f32[2,8,4,8,128]{4,3,2,1,0:T(8,128)S(1)}, u32[]{:S(2)}, u32[]{:S(2)}) collective-permute-start(f32[2,8,4,8,128]{4,3,2,1,0:T(8,128)S(1)} %get-tuple-element.43.coarse_ref), channel_id=1, source_target_pairs={{0,120},{8,16},{16,8},{24,32},{32,24},{40,48},{48,40},{56,64},{64,... | collective-permute-start | bytes 786440 | tf_op jit(solution)/shard_map/ppermute | solution.py:478
  43.8 4.3 %collective-permute-start.8 = (f32[2,8,4,8,128]{4,3,2,1,0:T(8,128)S(1)}, f32[2,8,4,8,128]{4,3,2,1,0:T(8,128)S(1)}, u32[]{:S(2)}, u32[]{:S(2)}) collective-permute-start(f32[2,8,4,8,128]{4,3,2,1,0:T(8,128)S(1)} %get-tuple-element.43.coarse_ref), channel_id=1, source_target_pairs={{0,8},{8,0},{16,24},{24,16},{32,40},{40,32},{48,56},{56,48},{64,72... | collective-permute-start | bytes 786440 | tf_op jit(solution)/shard_map/ppermute | solution.py:482

commit v3 on v2

v3 whole, which is shorter than its diff:
```python
import functools

import jax
import jax.numpy as jnp
from jax import lax
from jax.experimental import pallas as pl
from jax.experimental.pallas import tpu as pltpu
from jax.sharding import PartitionSpec as P

COEF = (-205.0 / 72.0, 8.0 / 5.0, -1.0 / 5.0, 8.0 / 315.0, -1.0 / 560.0)
NOFF = 17
REACH = 8
VX, VY, VZ = 8, 16, 1024
LT = VZ // 128
KT = LT // 2
F32 = jnp.float32

FIELD = (VX, LT, VY, 128)
XSLAB = (2, 4, LT, VY, 128)
XSLAB_COARSE = (2, 5, LT, VY, 128)
YSLAB = (2, 4, LT, 8, 128)
COARSE = (2, VX, KT, 8, 128)


def lane_iota(shape):
    return lax.broadcasted_iota(jnp.int32, shape, len(shape) - 1)


def pick(flag, yes, no):
    return jnp.where(flag, yes, no)


def compact_even(first, second):
    lane = lane_iota((8, 128))
    index = (2 * lane) & 127
    left = jnp.take_along_axis(first, index, axis=1)
    right = jnp.take_along_axis(second, index, axis=1)
    return jnp.where(lane < 64, left, right)


def coarse_tile(ref, lead, k):
    first = ref[lead + (2 * k, pl.ds(0, 8, stride=2), slice(None))]
    second = ref[lead + (2 * k + 1, pl.ds(0, 8, stride=2), slice(None))]
    return compact_even(first, second)


def pack_rows(top_ref, bottom_ref, f, l, low, high, gy_even):
    for p in range(VX):
        i, r = p % 4, 4 * (p // 4)
        top_ref[f, i, l, r : r + 4, :] = pick(gy_even, high[p], low[p])
        bottom_ref[f, i, l, r : r + 4, :] = pick(gy_even, low[p], high[p])


def first_pack_kernel(
    source_hbm,
    receiver_hbm,
    m1,
    m2,
    m3,
    m4,
    source_ref,
    receiver_ref,
    sems,
):
    gx_even = lax.rem(lax.axis_index("gx"), 2) == 0
    gy_even = lax.rem(lax.axis_index("gy"), 2) == 0
    copies = start_all(((source_hbm, source_ref), (receiver_hbm, receiver_ref)), sems)
    for f, ref in enumerate((source_ref, receiver_ref)):
        copies[f].wait()

        def tile(l, carry, f=f, ref=ref):
            lanes = pl.ds(pl.multiple_of(l * 128, 128), 128)
            for p in range(4):
                low = ref[p, :, lanes]
                high = ref[p + 4, :, lanes]
                m1[f, p, l] = pick(gx_even, high, low)
                m2[f, p, l] = pick(gx_even, low, high)
            low = [ref[p, 0:4, lanes] for p in range(VX)]
            high = [ref[p, 12:16, lanes] for p in range(VX)]
            pack_rows(m3, m4, f, l, low, high, gy_even)
            return carry

        lax.fori_loop(0, LT, tile, 0)


def star(ext, l, lane):
    centers = [ext[p, l + 1, 8 : 8 + VY, :] for p in range(VX)]
    out = []
    for p in range(VX):
        center = centers[p]
        after = ext[p, l + 2, 8 : 8 + VY, :]
        before = ext[p, l, 8 : 8 + VY, :]
        total = (3.0 * COEF[0]) * center
        for d in range(1, 5):
            near = pltpu.roll(jnp.where(lane >= d, center, after), 128 - d, 1)
            near = near + pltpu.roll(jnp.where(lane < 128 - d, center, before), d, 1)
            near = near + ext[p, l + 1, 8 + d : 8 + d + VY, :]
            near = near + ext[p, l + 1, 8 - d : 8 - d + VY, :]
            if p + d < VX:
                near = near + centers[p + d]
            if p - d >= 0:
                near = near + centers[p - d]
            total = total + COEF[d] * near
        out.append(total)
    return centers, out


def clear_ext(ext):
    def tile(p, carry):
        ext[p, :, 0:8, :] = jnp.zeros((LT + 2, 8, 128), F32)
        ext[p, :, 24:32, :] = jnp.zeros((LT + 2, 8, 128), F32)
        for l in (0, LT + 1):
            ext[p, l, 8:24, :] = jnp.zeros((VY, 128), F32)
        return carry

    lax.fori_loop(0, VX, tile, 0)


def lanes_of(l):
    return pl.ds(pl.multiple_of(l * 128, 128), 128)


def locate(cell):
    x = lax.shift_right_logical(cell, 17) - lax.axis_index("gx") * VX
    y = (lax.shift_right_logical(cell, 10) & 127) - lax.axis_index("gy") * VY
    return x, y, cell & 1023


def add_point(ref, cell, amount, velocity_ref=None):
    x, y, z = locate(cell)
    l = lax.shift_right_logical(z, 7)
    value = jnp.full((VY, 128), amount, F32)
    if velocity_ref is not None:
        value = value * velocity_ref[x, :, lanes_of(l)]
    row = lax.broadcasted_iota(jnp.int32, (VY, 128), 0)
    here = (row == y) & (lane_iota((VY, 128)) == (z & 127))
    ref[x, l] = ref[x, l] + jnp.where(here, value, 0.0)


def add_sources(ref, cells, wavelet, instant, velocity_ref):
    for j in range(cells.shape[0]):
        cell = cells[j]
        x, y, _ = locate(cell)
        here = (x >= 0) & (x < VX) & (y >= 0) & (y < VY)

        @pl.when(here)
        def _(cell=cell, j=j):
            add_point(ref, cell, wavelet[instant, j], velocity_ref)


def stencil(ext, older, velocity_ref, partial_ref, inject_ref=None):
    lane = lane_iota((VY, 128))

    def tile(l, carry):
        centers, totals = star(ext, l, lane)
        for p in range(VX):
            total = totals[p]
            if inject_ref is not None:
                total = total + inject_ref[p, l]
            v = velocity_ref[p, :, lanes_of(l)]
            partial_ref[p, l] = (2.0 * centers[p] - older[p, :, lanes_of(l)]) + v * total
        return carry

    lax.fori_loop(0, LT, tile, 0)


def start_all(pairs, sems):
    copies = [pltpu.make_async_copy(a, b, sems.at[i]) for i, (a, b) in enumerate(pairs)]
    for copy in copies:
        copy.start()
    return copies


def fill_ext(ext, ref):
    def tile(l, carry):
        for p in range(VX):
            ext[p, l + 1, 8 : 8 + VY, :] = ref[p, :, lanes_of(l)]
        return carry

    lax.fori_loop(0, LT, tile, 0)


def fill_ext_tiled(ext, ref):
    def tile(l, carry):
        for p in range(VX):
            ext[p, l + 1, 8 : 8 + VY, :] = ref[p, l]
        return carry

    lax.fori_loop(0, LT, tile, 0)


def first_receiver_kernel(
    now_ref,
    velocity_ref,
    prev_hbm,
    grid_hbm,
    cells_hbm,
    traces_hbm,
    partial_ref,
    inject_ref,
    ext,
    prev_ref,
    grid_ref,
    cells,
    traces,
    words_v,
    words_s,
    sems,
    word_sem,
):
    copies = start_all(
        ((grid_hbm, grid_ref), (cells_hbm, cells), (traces_hbm, traces), (prev_hbm, prev_ref)), sems
    )
    clear_ext(ext)
    fill_ext(ext, now_ref)

    copies[0].wait()
    x, y, _ = locate(grid_ref[...])
    inside = (x >= 0) & (x < VX) & (y >= 0) & (y < VY)
    bit = jnp.left_shift(1, lax.broadcasted_iota(jnp.int32, (32, 128), 0))
    words_v[...] = jnp.sum(jnp.where(inside, bit, 0), axis=0, keepdims=True)
    word_copy = pltpu.make_async_copy(words_v, words_s, word_sem)
    word_copy.start()

    def clear(l, carry):
        for p in range(VX):
            inject_ref[p, l] = jnp.zeros((VY, 128), F32)
        return carry

    lax.fori_loop(0, LT, clear, 0)
    copies[3].wait()
    stencil(ext, prev_ref, velocity_ref, partial_ref)
    for copy in copies[1:3]:
        copy.wait()
    word_copy.wait()

    def words_from(first, carry):
        words = [words_s[0, 8 * first + k] for k in range(8)]
        some = functools.reduce(lax.bitwise_or, words)

        @pl.when(some != 0)
        def _():
            for k in range(8):

                def one(bits, k=k):
                    low = bits & (-bits)
                    j = (31 - lax.clz(low)) * 128 + 8 * first + k
                    cell = cells[j]
                    add_point(partial_ref, cell, traces[0, j], velocity_ref)
                    add_point(inject_ref, cell, traces[1, j])
                    return bits & (bits - 1)

                lax.while_loop(lambda bits: bits != 0, one, words[k])

        return carry

    lax.fori_loop(0, 16, words_from, 0)


def first_source_kernel(
    now_ref,
    prev_hbm,
    velocity_hbm,
    cells_hbm,
    wavelet_hbm,
    partial_ref,
    velocity_ref,
    ext,
    prev_ref,
    cells,
    wavelet,
    sems,
):
    copies = start_all(
        ((velocity_hbm, velocity_ref), (prev_hbm, prev_ref), (cells_hbm, cells), (wavelet_hbm, wavelet)), sems
    )
    clear_ext(ext)
    fill_ext(ext, now_ref)
    for copy in copies:
        copy.wait()
    stencil(ext, prev_ref, velocity_ref, partial_ref)
    add_sources(partial_ref, cells, wavelet, 0, velocity_ref)


def source_kernel(
    fill, instant, now_ref, older_ref, velocity_ref, cells_hbm, wavelet_hbm, partial_ref, ext, cells, wavelet, sems
):
    copies = start_all(((cells_hbm, cells), (wavelet_hbm, wavelet)), sems)
    clear_ext(ext)
    fill(ext, now_ref)
    stencil(ext, older_ref, velocity_ref, partial_ref)
    for copy in copies:
        copy.wait()
    add_sources(partial_ref, cells, wavelet, instant, velocity_ref)


def second_local_kernel(
    source_ref,
    receiver_ref,
    source_old,
    receiver_old,
    velocity_ref,
    inject_ref,
    cells_hbm,
    wavelet_hbm,
    source_part,
    receiver_part,
    ext,
    cells,
    wavelet,
    sems,
):
    source_kernel(
        fill_ext_tiled, 1, source_ref, source_old, velocity_ref, cells_hbm, wavelet_hbm, source_part, ext, cells, wavelet, sems
    )
    fill_ext_tiled(ext, receiver_ref)
    stencil(ext, receiver_old, velocity_ref, receiver_part, inject_ref)


def halo_terms(m1, m2, m3, m4, rows_low, rows_high, f, l, flags):
    gx_even, has_left, has_right, gy_even, has_below, has_above = flags
    left, right = [], []
    for p in range(4):
        a, b = m1[f, p, l], m2[f, p, l]
        left.append(jnp.where(has_left, pick(gx_even, b, a), 0.0))
        right.append(jnp.where(has_right, pick(gx_even, a, b), 0.0))
    out = []
    for p in range(VX):
        i, r = p % 4, 4 * (p // 4)
        a, b = m3[f, i, l, r : r + 4, :], m4[f, i, l, r : r + 4, :]
        rows_low[p, 0:4, :] = jnp.where(has_below, pick(gy_even, b, a), 0.0)
        rows_high[p, 8:12, :] = jnp.where(has_above, pick(gy_even, a, b), 0.0)
    for p in range(VX):
        below = COEF[1] * rows_low[p, 3:11, :]
        above = COEF[1] * rows_high[p, 1:9, :]
        for d in range(2, 5):
            below = below + COEF[d] * rows_low[p, 4 - d : 12 - d, :]
            above = above + COEF[d] * rows_high[p, d : d + 8, :]
        total = jnp.concatenate((below, above), axis=0)
        for d in range(1, 5):
            if p - d < 0:
                total = total + COEF[d] * left[4 + p - d]
            if p + d >= VX:
                total = total + COEF[d] * right[p + d - VX]
        out.append(total)
    return out


def flags_of():
    gx, gy = lax.axis_index("gx"), lax.axis_index("gy")
    return (
        lax.rem(gx, 2) == 0,
        gx > 0,
        gx < lax.axis_size("gx") - 1,
        lax.rem(gy, 2) == 0,
        gy > 0,
        gy < lax.axis_size("gy") - 1,
    )


def clear_rows(rows_low, rows_high):
    for p in range(VX):
        rows_low[p] = jnp.zeros((16, 128), F32)
        rows_high[p] = jnp.zeros((16, 128), F32)


def first_halo_kernel(
    source_part,
    receiver_part,
    velocity_ref,
    m2,
    m1,
    m3,
    m4,
    source_ref,
    receiver_ref,
    s1,
    s2,
    s3,
    s4,
    coarse_ref,
    rows_low,
    rows_high,
):
    flags = flags_of()
    gx_even, gy_even = flags[0], flags[3]
    clear_rows(rows_low, rows_high)
    for f, (part, out) in enumerate(((source_part, source_ref), (receiver_part, receiver_ref))):

        def tile(l, carry, f=f, part=part, out=out):
            terms = halo_terms(m1, m2, m3, m4, rows_low, rows_high, f, l, flags)
            new = []
            for p in range(VX):
                value = part[p, l] + velocity_ref[p, :, lanes_of(l)] * terms[p]
                out[p, l] = value
                new.append(value)
            for p in range(4):
                s1[f, p, l] = pick(gx_even, new[p + 4], new[p])
                s2[f, p, l] = pick(gx_even, new[p], new[p + 4])
            pack_rows(s3, s4, f, l, [v[0:4] for v in new], [v[12:16] for v in new], gy_even)
            return carry

        lax.fori_loop(0, LT, tile, 0)
        for k in range(KT):
            low = [coarse_tile(out, (p,), k) for p in range(4)]
            high = [coarse_tile(out, (p + 4,), k) for p in range(4)]
            for p in range(4):
                coarse_ref[f, p, k] = low[p]
                coarse_ref[f, p + 4, k] = high[p]
                at = p * KT + k
                rows = slice(8 * (at % 2), 8 * (at % 2) + 8)
                s1[f, 4, at // 2, rows, :] = pick(gx_even, low[p], high[p])
                s2[f, 4, at // 2, rows, :] = pick(gx_even, high[p], low[p])


def second_halo_kernel(
    source_part,
    receiver_part,
    velocity_ref,
    m2,
    m1,
    m3,
    m4,
    source_ref,
    receiver_ref,
    coarse_ref,
    rows_low,
    rows_high,
    stage,
):
    flags = flags_of()
    clear_rows(rows_low, rows_high)
    for f, (part, out) in enumerate(((source_part, source_ref), (receiver_part, receiver_ref))):

        def tile(l, carry, f=f, part=part, out=out):
            terms = halo_terms(m1, m2, m3, m4, rows_low, rows_high, f, l, flags)
            for p in range(VX):
                value = part[p, l] + velocity_ref[p, :, lanes_of(l)] * terms[p]
                out[p, :, lanes_of(l)] = value
                stage[p, l] = value
            return carry

        lax.fori_loop(0, LT, tile, 0)
        for k in range(KT):
            for p in range(VX):
                coarse_ref[f, p, k] = coarse_tile(stage, (p,), k)


def first_image_kernel(coarse_ref, m1, m2, source_ref, receiver_ref, image_ref, source_hbm, receiver_hbm, sems):
    gx_even, has_left, has_right = flags_of()[:3]
    copies = [
        pltpu.make_async_copy(source_ref, source_hbm, sems.at[0]),
        pltpu.make_async_copy(receiver_ref, receiver_hbm, sems.at[1]),
    ]
    for copy in copies:
        copy.start()

    def planes(f, k):
        left, right = [], []
        near1 = [coarse_tile(m1, (f, p), k) for p in range(4)]
        near2 = [coarse_tile(m2, (f, p), k) for p in range(4)]
        far1, far2 = [], []
        for p in range(4):
            at = p * KT + k
            rows = slice(8 * (at % 2), 8 * (at % 2) + 8)
            far1.append(m1[f, 4, at // 2, rows, :])
            far2.append(m2[f, 4, at // 2, rows, :])
        for p in range(4):
            left.append(jnp.where(has_left, pick(gx_even, far2[p], far1[p]), 0.0))
        for p in range(4):
            left.append(jnp.where(has_left, pick(gx_even, near2[p], near1[p]), 0.0))
        for p in range(4):
            right.append(jnp.where(has_right, pick(gx_even, near1[p], near2[p]), 0.0))
        for p in range(4):
            right.append(jnp.where(has_right, pick(gx_even, far1[p], far2[p]), 0.0))
        return left + [coarse_ref[f, p, k] for p in range(VX)] + right

    for k in range(KT):
        source, receiver = planes(0, k), planes(1, k)
        for offset in range(NOFF):
            h = offset - REACH
            for a in range(VX // 2):
                image_ref[offset, a, k] = source[2 * a - h + REACH] * receiver[2 * a + h + REACH]
    for copy in copies:
        copy.wait()


def second_image_kernel(coarse_ref, m1, m2, before_ref, image_hbm, span, stage, sems):
    gx_even, has_left, has_right = flags_of()[:3]
    for f in range(2):
        for p in range(VX):
            span[f, p + REACH] = coarse_ref[f, p]
            for k in range(KT):
                a, b = m1[f, p, k], m2[f, p, k]
                span[f, p, k] = jnp.where(has_left, pick(gx_even, b, a), 0.0)
                span[f, p + REACH + VX, k] = jnp.where(has_right, pick(gx_even, a, b), 0.0)

    copies = []
    for a in range(VX // 2):
        for offset in range(NOFF):
            h = offset - REACH
            left, right = 2 * a - h + REACH, 2 * a + h + REACH
            for k in range(KT):
                value = before_ref[offset, a, k] + span[0, left, k] * span[1, right, k]
                stage[offset, a, :, k * 128 : (k + 1) * 128] = value
        copy = pltpu.make_async_copy(stage.at[:, a], image_hbm.at[:, a], sems.at[a])
        copy.start()
        copies.append(copy)
    for copy in copies:
        copy.wait()


VMEM = pl.BlockSpec(memory_space=pltpu.VMEM)
HBM = pl.BlockSpec(memory_space=pltpu.HBM)


def call(kernel, ins, outs, scratch=(), name=None, limit=12):
    return pl.pallas_call(
        kernel,
        out_shape=[jax.ShapeDtypeStruct(s, F32) for _, s in outs],
        in_specs=[s for s, _ in ins],
        out_specs=[s for s, _ in outs],
        scratch_shapes=list(scratch),
        name=name,
        cost_estimate=pl.CostEstimate(flops=0, bytes_accessed=0, transcendentals=0),
        compiler_params=pltpu.CompilerParams(vmem_limit_bytes=limit << 20),
    )(*[pltpu.with_memory_space_constraint(a, pltpu.HBM) if s is HBM else a for s, a in ins])


def vmem(*items):
    return [(VMEM, a) for a in items]


def hbm(*items):
    return [(HBM, a) for a in items]


def arrived(flops, *arrays):
    n = len(arrays)
    return pl.pallas_call(
        lambda *refs: None,
        out_shape=[jax.ShapeDtypeStruct(a.shape, F32) for a in arrays],
        in_specs=[VMEM] * n,
        out_specs=[VMEM] * n,
        input_output_aliases={i: i for i in range(n)},
        name="arrived",
        cost_estimate=pl.CostEstimate(flops=flops, bytes_accessed=0, transcendentals=0),
        compiler_params=pltpu.CompilerParams(vmem_limit_bytes=12 << 20),
    )(*arrays)


def dma(count):
    return pltpu.SemaphoreType.DMA((count,))


def inner(axis):
    return [(i, i ^ 1) for i in range(lax.axis_size(axis))]


def x_outer():
    nx, ny = lax.axis_size("gx"), lax.axis_size("gy")
    pairs = []
    for x in range(nx):
        for y in range(ny):
            other = x + 1 if x % 2 else x - 1
            if 0 <= other < nx:
                pairs.append((x * ny + y, other * ny + y))
            elif y < 2 or y >= ny - 2:
                pairs.append((x * ny + y, x * ny + (y ^ 1)))
            else:
                pairs.append((x * ny + y, other % nx * ny + y))
    return pairs


def y_outer():
    nx, ny = lax.axis_size("gx"), lax.axis_size("gy")
    pairs = []
    for x in range(nx):
        for y in range(ny):
            other = y + 1 if y % 2 else y - 1
            if 0 <= other < ny:
                pairs.append((x * ny + y, x * ny + other))
            else:
                pairs.append((x * ny + y, (x ^ 1) * ny + y))
    return pairs


def along_x(m1, m2):
    return lax.ppermute(m1, "gx", inner("gx")), lax.ppermute(m2, ("gx", "gy"), x_outer())


def inner_y(m3):
    return lax.ppermute(m3, "gy", inner("gy"))


def outer_y(m4):
    return lax.ppermute(m4, ("gx", "gy"), y_outer())


def local(
    source_now,
    source_prev,
    receiver_now,
    receiver_prev,
    velocity_sq,
    source_cells,
    source_wavelet,
    receiver_cells,
    receiver_traces,
):
    block = (VX, VY, VZ)
    ext = pltpu.VMEM((VX, LT + 2, 32, 128), F32)
    rows = pltpu.VMEM((VX, 16, 128), F32)
    whole = pltpu.VMEM(block, F32)
    m1, m2, m3, m4, source, receiver = call(
        first_pack_kernel,
        hbm(source_now, receiver_now),
        vmem(XSLAB, XSLAB, YSLAB, YSLAB, block, block),
        (dma(2),),
        name="pack",
    )
    g1, g2 = along_x(m1, m2)
    g3 = inner_y(m3)
    source_scratch = (
        ext,
        pltpu.SMEM(source_cells.shape, jnp.int32),
        pltpu.SMEM(source_wavelet.shape, F32),
        dma(2),
    )
    source_part, velocity = call(
        first_source_kernel,
        vmem(source) + hbm(source_prev, velocity_sq, source_cells, source_wavelet),
        vmem(FIELD, block),
        (
            ext,
            whole,
            pltpu.SMEM(source_cells.shape, jnp.int32),
            pltpu.SMEM(source_wavelet.shape, F32),
            dma(4),
        ),
        name="source1",
    )
    m4, source_part = lax.optimization_barrier((m4, source_part))
    g4 = outer_y(m4)
    receiver_part, inject = call(
        first_receiver_kernel,
        vmem(receiver, velocity)
        + hbm(receiver_prev, receiver_cells.reshape(32, 128), receiver_cells, receiver_traces),
        vmem(FIELD, FIELD),
        (
            ext,
            whole,
            pltpu.VMEM((32, 128), jnp.int32),
            pltpu.SMEM(receiver_cells.shape, jnp.int32),
            pltpu.SMEM(receiver_traces.shape, F32),
            pltpu.VMEM((1, 128), jnp.int32),
            pltpu.SMEM((1, 128), jnp.int32),
            dma(4),
            pltpu.SemaphoreType.DMA,
        ),
        name="receiver1",
    )
    source1, receiver1, m1, m2, m3, m4, coarse = call(
        first_halo_kernel,
        vmem(source_part, receiver_part, velocity, g2, g1, g3, g4),
        vmem(FIELD, FIELD, XSLAB_COARSE, XSLAB_COARSE, YSLAB, YSLAB, COARSE),
        (rows, rows),
        name="halo1",
    )
    g4 = outer_y(m4)
    g1, g2 = along_x(m1, m2)
    g3 = inner_y(m3)
    source_part, receiver_part = call(
        second_local_kernel,
        vmem(source1, receiver1, source, receiver, velocity, inject) + hbm(source_cells, source_wavelet),
        vmem(FIELD, FIELD),
        source_scratch,
        name="local2",
    )
    g2, g4 = arrived(4300000000, g2, g4)
    source, receiver, last = call(
        second_halo_kernel,
        vmem(source_part, receiver_part, velocity, g2, g1, g3, g4),
        vmem(block, block, COARSE),
        (rows, rows, pltpu.VMEM(FIELD, F32)),
        name="halo2",
    )
    far = along_x(last, last)
    image, source_next, receiver_next = call(
        first_image_kernel,
        vmem(coarse, g1, g2, source, receiver),
        vmem((NOFF, VX // 2, KT, 8, 128)) + hbm(block, block),
        (dma(2),),
        name="image1",
    )
    (image,) = call(
        second_image_kernel,
        vmem(last, *far, image),
        hbm((NOFF, VX // 2, 8, KT * 128)),
        (
            pltpu.VMEM((2, 2 * REACH + VX, KT, 8, 128), F32),
            pltpu.VMEM((NOFF, VX // 2, 8, KT * 128), F32),
            dma(VX // 2),
        ),
        name="image2",
    )
    return source_next, receiver_next, image


def solution(mesh):
    field = P("gx", "gy", None)
    return jax.shard_map(
        local,
        mesh=mesh,
        in_specs=(field,) * 5 + (P(),) * 4,
        out_specs=(field, field, P(None, "gx", "gy", None)),
        check_vma=False,
    )
```

time: 49.4 us -> 46.8 us (0.947)
  the two profiles are of different devices: /device:TPU:0 before, /device:TPU:24 now
where the time goes in v3:
time: 46.8 us; the launch traced here: 46.2 us
  Pallas kernels  16.9 us (36%)
  waiting for transfers between devices  16.9 us (36%)
  starting transfers between devices  11.7 us (25%)
  between operations  0.71 us (2%)
    pallas_call x8, Pallas kernels, call(): pl.pallas_call(kernel, out_shape=[jax.ShapeDtypeStruct(s, F32) for _, s i...  16.9 us
    ppermute x2, waiting for transfers between devices, outer_y(): return lax.ppermute(m4, ('gx', 'gy'), y_outer())  10.8 us
    ppermute x3, waiting for transfers between devices, along_x(): lax.ppermute(m2, ('gx', 'gy'), x_outer())  6.15 us
    ppermute x2, starting transfers between devices, outer_y(): return lax.ppermute(m4, ('gx', 'gy'), y_outer())  5.01 us
    ppermute x3, starting transfers between devices, along_x(): lax.ppermute(m2, ('gx', 'gy'), x_outer())  4.86 us
    ppermute x2, starting transfers between devices, inner_y(): return lax.ppermute(m3, 'gy', inner('gy'))  1.49 us
  transfers between devices with their start and end apart: 10, of which 4 were waited for; matrix products, arithmetic and copies ran while one was open for 0% of the time, Pallas kernels for 26%

profile of v3, /device:TPU:24, one launch (start us, length us, event | category | flops | bytes accessed | tf_op | source)
XLA Modules:
  0.0 46.2 jit_solution(9388120428169794748)
XLA Ops:
  0.6 1.4 %pack.1 = (f32[2,4,8,16,128]{4,3,2,1,0:T(8,128)S(1)}, f32[2,4,8,16,128]{4,3,2,1,0:T(8,128)S(1)}, f32[2,4,8,8,128]{4,3,2,1,0:T(8,128)S(1)}, f32[2,4,8,8,128]{4,3,...) custom-call(f32[8,16,1024]{2,1,0:T(8,128)} %source_hbm.1, f32[8,16,1024]{2,1,0:T(8,128)} %receiver_hbm.1), custom_call_target="tpu_custom_call" | custom-call | tf_op jit(solution)/shard_map/pack/pallas_call | solution.py:518
  2.0 3.7 %collective-permute-start = (f32[2,4,8,16,128]{4,3,2,1,0:T(8,128)S(1)}, f32[2,4,8,16,128]{4,3,2,1,0:T(8,128)S(1)}, u32[]{:S(2)}, u32[]{:S(2)}) collective-permute-start(f32[2,4,8,16,128]{4,3,2,1,0:T(8,128)S(1)} %get-tuple-element.39), channel_id=1, source_target_pairs={{0,1},{1,0},{2,122},{3,123},{4,124},{5,125},{6,7},{7,6},{8,16},{9,... | collective-permute-start | bytes 1572872 | tf_op jit(solution)/shard_map/ppermute | solution.py:589
  5.8 0.0 collective-permute-start.1
  5.8 1.5 %collective-permute-start.2 = (f32[2,4,8,8,128]{4,3,2,1,0:T(8,128)S(1)}, f32[2,4,8,8,128]{4,3,2,1,0:T(8,128)S(1)}, u32[]{:S(2)}, u32[]{:S(2)}) collective-permute-start(f32[2,4,8,8,128]{4,3,2,1,0:T(8,128)S(1)} %get-tuple-element.41), channel_id=1, source_target_pairs={{0,1},{1,0},{2,3},{3,2},{4,5},{5,4},{6,7},{7,6},{8,9},{9,8},{10,11... | collective-permute-start | bytes 786440 | tf_op jit(solution)/shard_map/ppermute | solution.py:593
  7.3 3.0 %source1.1 = (f32[8,8,16,128]{3,2,1,0:T(8,128)S(1)}, f32[8,16,1024]{2,1,0:T(8,128)S(1)}) custom-call(f32[8,16,1024]{2,1,0:T(8,128)S(1)} %get-tuple-element.33.now_ref.source_old, f32[8,16,1024]{2,1,0:T(8,128)} %prev_hbm.2, f32[8,16,1024]{2,1,0:T(8,128)} %velocity_hbm.1, s32[4]{0:T(128)} %cells_hbm.5, f32[2,4]{1,0:T(2,128)} %wavelet_hbm.3), custom_call_target="tpu_custom_call" | custom-call | tf_op jit(solution)/shard_map/source1/pallas_call | solution.py:518
  10.3 2.6 %collective-permute-start.3 = (f32[2,4,8,8,128]{4,3,2,1,0:T(8,128)S(1)}, f32[2,4,8,8,128]{4,3,2,1,0:T(8,128)S(1)}, u32[]{:S(2)}, u32[]{:S(2)}) collective-permute-start(f32[2,4,8,8,128]{4,3,2,1,0:T(8,128)S(1)} %get-tuple-element.42), channel_id=1, source_target_pairs={{0,8},{1,2},{2,1},{3,4},{4,3},{5,6},{6,5},{7,15},{8,0},{9,10},{10,... | collective-permute-start | bytes 786440 | tf_op jit(solution)/shard_map/ppermute | solution.py:597
  12.8 4.3 %receiver1.1 = (f32[8,8,16,128]{3,2,1,0:T(8,128)S(1)}, f32[8,8,16,128]{3,2,1,0:T(8,128)S(1)}) custom-call(f32[8,16,1024]{2,1,0:T(8,128)S(1)} %get-tuple-element.36.now_ref.receiver_old, f32[8,16,1024]{2,1,0:T(8,128)S(1)} %get-tuple-element.37.velocity_ref, f32[8,16,1024]{2,1,0:T(8,128)} %prev_hbm.3, s32[32,128]{1,0:T(8,128)} %bitcast.1, s32[4096]{0:T(1024)} %cells_hbm.4, ...), custom_call_target="tpu_custom_call" | custom-call | tf_op jit(solution)/shard_map/receiver1/pallas_call | solution.py:518
  17.2 0.0 collective-permute-done.2.m3
  17.2 5.3 %collective-permute-done.3.m4 = f32[2,4,8,8,128]{4,3,2,1,0:T(8,128)S(1)} collective-permute-done((f32[2,4,8,8,128]{4,3,2,1,0:T(8,128)S(1)}, f32[2,4,8,8,128]{4,3,2,1,0:T(8,128)S(1)}, u32[]{:S(2)}, u32[]{:S(2)}) %collective-permute-start.3) | collective-permute-done | bytes 262176 | tf_op jit(solution)/shard_map/ppermute | solution.py:597
  22.5 0.0 collective-permute-done.m2
  22.5 0.0 collective-permute-done.1.m1
  22.5 1.2 %halo1.1 = (f32[8,8,16,128]{3,2,1,0:T(8,128)S(1)}, f32[8,8,16,128]{3,2,1,0:T(8,128)S(1)}, f32[2,5,8,16,128]{4,3,2,1,0:T(8,128)S(1)}, f32[2,5,8,16,128]{4,3,2,1,0...) custom-call(f32[8,8,16,128]{3,2,1,0:T(8,128)S(1)} %get-tuple-element, ...), custom_call_target="tpu_custom_call" | custom-call | tf_op jit(solution)/shard_map/halo1/pallas_call | solution.py:518
  23.7 0.1 collective-permute-start.5
  23.8 2.5 %collective-permute-start.6 = (f32[2,4,8,8,128]{4,3,2,1,0:T(8,128)S(1)}, f32[2,4,8,8,128]{4,3,2,1,0:T(8,128)S(1)}, u32[]{:S(2)}, u32[]{:S(2)}) collective-permute-start(f32[2,4,8,8,128]{4,3,2,1,0:T(8,128)S(1)} %get-tuple-element.46), channel_id=1, source_target_pairs={{0,8},{1,2},{2,1},{3,4},{4,3},{5,6},{6,5},{7,15},{8,0},{9,10},{10,... | collective-permute-start | bytes 786440 | tf_op jit(solution)/shard_map/ppermute | solution.py:597
  26.3 0.0 collective-permute-start.4
  26.3 0.0 collective-permute-start.7
  26.3 3.7 %local2.1 = (f32[8,8,16,128]{3,2,1,0:T(8,128)S(1)}, f32[8,8,16,128]{3,2,1,0:T(8,128)S(1)}) custom-call(f32[8,8,16,128]{3,2,1,0:T(8,128)S(1)} %get-tuple-element.48.source_ref, f32[8,8,16,128]{3,2,1,0:T(8,128)S(1)} %get-tuple-element.49.receiver_ref, f32[8,16,1024]{2,1,0:T(8,128)S(1)} %get-tuple-element.33.now_ref.source_old, ...), custom_call_target="tpu_custom_call" | custom-call | tf_op jit(solution)/shard_map/local2/pallas_call | solution.py:518
  30.0 5.4 %collective-permute-done.6.refs_1_ = f32[2,4,8,8,128]{4,3,2,1,0:T(8,128)S(1)} collective-permute-done((f32[2,4,8,8,128]{4,3,2,1,0:T(8,128)S(1)}, f32[2,4,8,8,128]{4,3,2,1,0:T(8,128)S(1)}, u32[]{:S(2)}, u32[]{:S(2)}) %collective-permute-start.6) | collective-permute-done | bytes 262176 | tf_op jit(solution)/shard_map/ppermute | solution.py:597
  35.4 0.5 %collective-permute-done.5.refs_0_ = f32[2,5,8,16,128]{4,3,2,1,0:T(8,128)S(1)} collective-permute-done((f32[2,5,8,16,128]{4,3,2,1,0:T(8,128)S(1)}, f32[2,5,8,16,128]{4,3,2,1,0:T(8,128)S(1)}, u32[]{:S(2)}, u32[]{:S(2)}) %collective-permute-start.5) | collective-permute-done | bytes 655392 | tf_op jit(solution)/shard_map/ppermute | solution.py:589
  35.9 0.0 collective-permute-done.7.m3
  35.9 0.0 collective-permute-done.4.m1
  35.9 1.1 %halo2.1 = (f32[8,16,1024]{2,1,0:T(8,128)S(1)}, f32[8,16,1024]{2,1,0:T(8,128)S(1)}, f32[2,8,4,8,128]{4,3,2,1,0:T(8,128)S(1)}) custom-call(f32[8,8,16,128]{3,2,1,0:T(8,128)S(1)} %get-tuple-element.51.source_part, f32[8,8,16,128]{3,2,1,0:T(8,128)S(1)} %get-tuple-element.52.receiver_part, f32[8,16,1024]{2,1,0:T(8,128)S(1)} %get-tuple-element.37.velocity_ref, ...), custom_call_target="tpu_custom_call" | custom-call | tf_op jit(solution)/shard_map/halo2/pallas_call | solution.py:518
  37.1 1.0 %collective-permute-start.9 = (f32[2,8,4,8,128]{4,3,2,1,0:T(8,128)S(1)}, f32[2,8,4,8,128]{4,3,2,1,0:T(8,128)S(1)}, u32[]{:S(2)}, u32[]{:S(2)}) collective-permute-start(f32[2,8,4,8,128]{4,3,2,1,0:T(8,128)S(1)} %get-tuple-element.59.coarse_ref), channel_id=1, source_target_pairs={{0,1},{1,0},{2,122},{3,123},{4,124},{5,125},{6,7},{7,6},{8,16},{9,... | collective-permute-start | bytes 786440 | tf_op jit(solution)/shard_map/ppermute | solution.py:589
  38.1 0.3 collective-permute-start.8
  38.4 1.0 %image1.1 = (f32[17,4,4,8,128]{4,3,2,1,0:T(8,128)S(1)}, f32[8,16,1024]{2,1,0:T(8,128)}, f32[8,16,1024]{2,1,0:T(8,128)}) custom-call(f32[2,8,4,8,128]{4,3,2,1,0:T(8,128)S(1)} %get-tuple-element.43.coarse_ref, f32[2,5,8,16,128]{4,3,2,1,0:T(8,128)S(1)} %collective-permute-done.4.m1, f32[2,5,8,16,128]{4,3,2,1,0:T(8,128)S(1)} %get-tuple-element.47.m2, ...), custom_call_target="tpu_custom_call" | custom-call | tf_op jit(solution)/shard_map/image1/pallas_call | solution.py:518
  39.4 5.7 %collective-permute-done.9.m2 = f32[2,8,4,8,128]{4,3,2,1,0:T(8,128)S(1)} collective-permute-done((f32[2,8,4,8,128]{4,3,2,1,0:T(8,128)S(1)}, f32[2,8,4,8,128]{4,3,2,1,0:T(8,128)S(1)}, u32[]{:S(2)}, u32[]{:S(2)}) %collective-permute-start.9) | collective-permute-done | bytes 262176 | tf_op jit(solution)/shard_map/ppermute | solution.py:589
  45.1 0.0 collective-permute-done.8.m1
  45.1 1.1 %image2.1 = f32[17,4,8,512]{3,2,1,0:T(8,128)} custom-call(f32[2,8,4,8,128]{4,3,2,1,0:T(8,128)S(1)} %get-tuple-element.59.coarse_ref, f32[2,8,4,8,128]{4,3,2,1,0:T(8,128)S(1)} %collective-permute-done.8.m1, f32[2,8,4,8,128]{4,3,2,1,0:T(8,128)S(1)} %collective-permute-done.9.m2, f32[17,4,4,8,128]{4,3,2,1,0:T(8,128)S(1)} %get-tuple-element.60.before_ref), custom_call_target="tpu_custom_call" | custom-call | tf_op jit(solution)/shard_map/image2/pallas_call | solution.py:518
  (1 shorter events, 0.0 us)
Async XLA Ops:
  2.0 20.5 %collective-permute-start = (f32[2,4,8,16,128]{4,3,2,1,0:T(8,128)S(1)}, f32[2,4,8,16,128]{4,3,2,1,0:T(8,128)S(1)}, u32[]{:S(2)}, u32[]{:S(2)}) collective-permute-start(f32[2,4,8,16,128]{4,3,2,1,0:T(8,128)S(1)} %get-tuple-element.39), channel_id=1, source_target_pairs={{0,1},{1,0},{2,122},{3,123},{4,124},{5,125},{6,7},{7,6},{8,16},{9,... | collective-permute-start | bytes 1572872 | tf_op jit(solution)/shard_map/ppermute | solution.py:589
  5.8 16.8 %collective-permute-start.1 = (f32[2,4,8,16,128]{4,3,2,1,0:T(8,128)S(1)}, f32[2,4,8,16,128]{4,3,2,1,0:T(8,128)S(1)}, u32[]{:S(2)}, u32[]{:S(2)}) collective-permute-start(f32[2,4,8,16,128]{4,3,2,1,0:T(8,128)S(1)} %get-tuple-element.40), channel_id=1, source_target_pairs={{0,8},{8,0},{16,24},{24,16},{32,40},{40,32},{48,56},{56,48},{64,72... | collective-permute-start | bytes 1572872 | tf_op jit(solution)/shard_map/ppermute | solution.py:589
  5.8 11.4 %collective-permute-start.2 = (f32[2,4,8,8,128]{4,3,2,1,0:T(8,128)S(1)}, f32[2,4,8,8,128]{4,3,2,1,0:T(8,128)S(1)}, u32[]{:S(2)}, u32[]{:S(2)}) collective-permute-start(f32[2,4,8,8,128]{4,3,2,1,0:T(8,128)S(1)} %get-tuple-element.41), channel_id=1, source_target_pairs={{0,1},{1,0},{2,3},{3,2},{4,5},{5,4},{6,7},{7,6},{8,9},{9,8},{10,11... | collective-permute-start | bytes 786440 | tf_op jit(solution)/shard_map/ppermute | solution.py:593
  10.3 12.2 %collective-permute-start.3 = (f32[2,4,8,8,128]{4,3,2,1,0:T(8,128)S(1)}, f32[2,4,8,8,128]{4,3,2,1,0:T(8,128)S(1)}, u32[]{:S(2)}, u32[]{:S(2)}) collective-permute-start(f32[2,4,8,8,128]{4,3,2,1,0:T(8,128)S(1)} %get-tuple-element.42), channel_id=1, source_target_pairs={{0,8},{1,2},{2,1},{3,4},{4,3},{5,6},{6,5},{7,15},{8,0},{9,10},{10,... | collective-permute-start | bytes 786440 | tf_op jit(solution)/shard_map/ppermute | solution.py:597
  23.7 12.2 %collective-permute-start.5 = (f32[2,5,8,16,128]{4,3,2,1,0:T(8,128)S(1)}, f32[2,5,8,16,128]{4,3,2,1,0:T(8,128)S(1)}, u32[]{:S(2)}, u32[]{:S(2)}) collective-permute-start(f32[2,5,8,16,128]{4,3,2,1,0:T(8,128)S(1)} %get-tuple-element.45), channel_id=1, source_target_pairs={{0,1},{1,0},{2,122},{3,123},{4,124},{5,125},{6,7},{7,6},{8,16},{9,... | collective-permute-start | bytes 1966088 | tf_op jit(solution)/shard_map/ppermute | solution.py:589
  23.8 11.6 %collective-permute-start.6 = (f32[2,4,8,8,128]{4,3,2,1,0:T(8,128)S(1)}, f32[2,4,8,8,128]{4,3,2,1,0:T(8,128)S(1)}, u32[]{:S(2)}, u32[]{:S(2)}) collective-permute-start(f32[2,4,8,8,128]{4,3,2,1,0:T(8,128)S(1)} %get-tuple-element.46), channel_id=1, source_target_pairs={{0,8},{1,2},{2,1},{3,4},{4,3},{5,6},{6,5},{7,15},{8,0},{9,10},{10,... | collective-permute-start | bytes 786440 | tf_op jit(solution)/shard_map/ppermute | solution.py:597
  26.3 9.7 %collective-permute-start.4 = (f32[2,5,8,16,128]{4,3,2,1,0:T(8,128)S(1)}, f32[2,5,8,16,128]{4,3,2,1,0:T(8,128)S(1)}, u32[]{:S(2)}, u32[]{:S(2)}) collective-permute-start(f32[2,5,8,16,128]{4,3,2,1,0:T(8,128)S(1)} %get-tuple-element.44), channel_id=1, source_target_pairs={{0,8},{8,0},{16,24},{24,16},{32,40},{40,32},{48,56},{56,48},{64,72... | collective-permute-start | bytes 1966088 | tf_op jit(solution)/shard_map/ppermute | solution.py:589
  26.3 9.7 %collective-permute-start.7 = (f32[2,4,8,8,128]{4,3,2,1,0:T(8,128)S(1)}, f32[2,4,8,8,128]{4,3,2,1,0:T(8,128)S(1)}, u32[]{:S(2)}, u32[]{:S(2)}) collective-permute-start(f32[2,4,8,8,128]{4,3,2,1,0:T(8,128)S(1)} %get-tuple-element.53), channel_id=1, source_target_pairs={{0,1},{1,0},{2,3},{3,2},{4,5},{5,4},{6,7},{7,6},{8,9},{9,8},{10,11... | collective-permute-start | bytes 786440 | tf_op jit(solution)/shard_map/ppermute | solution.py:593
  37.1 8.0 %collective-permute-start.9 = (f32[2,8,4,8,128]{4,3,2,1,0:T(8,128)S(1)}, f32[2,8,4,8,128]{4,3,2,1,0:T(8,128)S(1)}, u32[]{:S(2)}, u32[]{:S(2)}) collective-permute-start(f32[2,8,4,8,128]{4,3,2,1,0:T(8,128)S(1)} %get-tuple-element.59.coarse_ref), channel_id=1, source_target_pairs={{0,1},{1,0},{2,122},{3,123},{4,124},{5,125},{6,7},{7,6},{8,16},{9,... | collective-permute-start | bytes 786440 | tf_op jit(solution)/shard_map/ppermute | solution.py:589
  38.1 7.0 %collective-permute-start.8 = (f32[2,8,4,8,128]{4,3,2,1,0:T(8,128)S(1)}, f32[2,8,4,8,128]{4,3,2,1,0:T(8,128)S(1)}, u32[]{:S(2)}, u32[]{:S(2)}) collective-permute-start(f32[2,8,4,8,128]{4,3,2,1,0:T(8,128)S(1)} %get-tuple-element.59.coarse_ref), channel_id=1, source_target_pairs={{0,8},{8,0},{16,24},{24,16},{32,40},{40,32},{48,56},{56,48},{64,72... | collective-permute-start | bytes 786440 | tf_op jit(solution)/shard_map/ppermute | solution.py:589

commit v4 on v3

--- a/solution.py
+++ b/solution.py
@@ -557,7 +557,7 @@
     return [(i, i ^ 1) for i in range(lax.axis_size(axis))]
 
 
-def x_outer():
+def x_outer(near):
     nx, ny = lax.axis_size("gx"), lax.axis_size("gy")
     pairs = []
     for x in range(nx):
@@ -565,7 +565,7 @@
             other = x + 1 if x % 2 else x - 1
             if 0 <= other < nx:
                 pairs.append((x * ny + y, other * ny + y))
-            elif y < 2 or y >= ny - 2:
+            elif min(y, ny - 1 - y) < near:
                 pairs.append((x * ny + y, x * ny + (y ^ 1)))
             else:
                 pairs.append((x * ny + y, other % nx * ny + y))
@@ -585,8 +585,8 @@
     return pairs
 
 
-def along_x(m1, m2):
-    return lax.ppermute(m1, "gx", inner("gx")), lax.ppermute(m2, ("gx", "gy"), x_outer())
+def along_x(m1, m2, near=4):
+    return lax.ppermute(m1, "gx", inner("gx")), lax.ppermute(m2, ("gx", "gy"), x_outer(near))
 
 
 def inner_y(m3):
@@ -668,7 +668,7 @@
         name="halo1",
     )
     g4 = outer_y(m4)
-    g1, g2 = along_x(m1, m2)
+    g1, g2 = along_x(m1, m2, near=2)
     g3 = inner_y(m3)
     source_part, receiver_part = call(
         second_local_kernel,

time: 46.8 us -> 46.3 us (0.989); the launches traced: 46.2 us -> 46.2 us
  no operation moved by 1% of the time
where the time goes in v4:
time: 46.3 us; the launch traced here: 46.2 us
  waiting for transfers between devices  17 us (37%)
  Pallas kernels  16.7 us (36%)
  starting transfers between devices  11.7 us (25%)
  between operations  0.71 us (2%)
    pallas_call x8, Pallas kernels, call(): pl.pallas_call(kernel, out_shape=[jax.ShapeDtypeStruct(s, F32) for _, s i...  16.7 us
    ppermute x2, waiting for transfers between devices, outer_y(): return lax.ppermute(m4, ('gx', 'gy'), y_outer())  10.9 us
    ppermute x3, waiting for transfers between devices, along_x(): lax.ppermute(m2, ('gx', 'gy'), x_outer(near))  6.15 us
    ppermute x2, starting transfers between devices, outer_y(): return lax.ppermute(m4, ('gx', 'gy'), y_outer())  5.01 us
    ppermute x3, starting transfers between devices, along_x(): lax.ppermute(m2, ('gx', 'gy'), x_outer(near))  4.86 us
    ppermute x2, starting transfers between devices, inner_y(): return lax.ppermute(m3, 'gy', inner('gy'))  1.49 us
  transfers between devices with their start and end apart: 10, of which 4 were waited for; matrix products, arithmetic and copies ran while one was open for 0% of the time, Pallas kernels for 26%

profile of v4, /device:TPU:24, one launch (start us, length us, event | category | flops | bytes accessed | tf_op | source)
XLA Modules:
  0.0 46.2 jit_solution(14060183960648837316)
XLA Ops:
  0.6 1.4 %pack.1 = (f32[2,4,8,16,128]{4,3,2,1,0:T(8,128)S(1)}, f32[2,4,8,16,128]{4,3,2,1,0:T(8,128)S(1)}, f32[2,4,8,8,128]{4,3,2,1,0:T(8,128)S(1)}, f32[2,4,8,8,128]{4,3,...) custom-call(f32[8,16,1024]{2,1,0:T(8,128)} %source_hbm.1, f32[8,16,1024]{2,1,0:T(8,128)} %receiver_hbm.1), custom_call_target="tpu_custom_call" | custom-call | tf_op jit(solution)/shard_map/pack/pallas_call | solution.py:518
  2.0 3.7 %collective-permute-start = (f32[2,4,8,16,128]{4,3,2,1,0:T(8,128)S(1)}, f32[2,4,8,16,128]{4,3,2,1,0:T(8,128)S(1)}, u32[]{:S(2)}, u32[]{:S(2)}) collective-permute-start(f32[2,4,8,16,128]{4,3,2,1,0:T(8,128)S(1)} %get-tuple-element.39), channel_id=1, source_target_pairs={{0,1},{1,0},{2,3},{3,2},{4,5},{5,4},{6,7},{7,6},{8,16},{9,17},{10,... | collective-permute-start | bytes 1572872 | tf_op jit(solution)/shard_map/ppermute | solution.py:589
  5.8 0.0 collective-permute-start.1
  5.8 1.5 %collective-permute-start.2 = (f32[2,4,8,8,128]{4,3,2,1,0:T(8,128)S(1)}, f32[2,4,8,8,128]{4,3,2,1,0:T(8,128)S(1)}, u32[]{:S(2)}, u32[]{:S(2)}) collective-permute-start(f32[2,4,8,8,128]{4,3,2,1,0:T(8,128)S(1)} %get-tuple-element.41), channel_id=1, source_target_pairs={{0,1},{1,0},{2,3},{3,2},{4,5},{5,4},{6,7},{7,6},{8,9},{9,8},{10,11... | collective-permute-start | bytes 786440 | tf_op jit(solution)/shard_map/ppermute | solution.py:593
  7.3 3.0 %source1.1 = (f32[8,8,16,128]{3,2,1,0:T(8,128)S(1)}, f32[8,16,1024]{2,1,0:T(8,128)S(1)}) custom-call(f32[8,16,1024]{2,1,0:T(8,128)S(1)} %get-tuple-element.33.now_ref.source_old, f32[8,16,1024]{2,1,0:T(8,128)} %prev_hbm.2, f32[8,16,1024]{2,1,0:T(8,128)} %velocity_hbm.1, s32[4]{0:T(128)} %cells_hbm.5, f32[2,4]{1,0:T(2,128)} %wavelet_hbm.3), custom_call_target="tpu_custom_call" | custom-call | tf_op jit(solution)/shard_map/source1/pallas_call | solution.py:518
  10.3 2.6 %collective-permute-start.3 = (f32[2,4,8,8,128]{4,3,2,1,0:T(8,128)S(1)}, f32[2,4,8,8,128]{4,3,2,1,0:T(8,128)S(1)}, u32[]{:S(2)}, u32[]{:S(2)}) collective-permute-start(f32[2,4,8,8,128]{4,3,2,1,0:T(8,128)S(1)} %get-tuple-element.42), channel_id=1, source_target_pairs={{0,8},{1,2},{2,1},{3,4},{4,3},{5,6},{6,5},{7,15},{8,0},{9,10},{10,... | collective-permute-start | bytes 786440 | tf_op jit(solution)/shard_map/ppermute | solution.py:597
  12.8 4.2 %receiver1.1 = (f32[8,8,16,128]{3,2,1,0:T(8,128)S(1)}, f32[8,8,16,128]{3,2,1,0:T(8,128)S(1)}) custom-call(f32[8,16,1024]{2,1,0:T(8,128)S(1)} %get-tuple-element.36.now_ref.receiver_old, f32[8,16,1024]{2,1,0:T(8,128)S(1)} %get-tuple-element.37.velocity_ref, f32[8,16,1024]{2,1,0:T(8,128)} %prev_hbm.3, s32[32,128]{1,0:T(8,128)} %bitcast.1, s32[4096]{0:T(1024)} %cells_hbm.4, ...), custom_call_target="tpu_custom_call" | custom-call | tf_op jit(solution)/shard_map/receiver1/pallas_call | solution.py:518
  17.1 0.0 collective-permute-done.2.m3
  17.1 5.4 %collective-permute-done.3.m4 = f32[2,4,8,8,128]{4,3,2,1,0:T(8,128)S(1)} collective-permute-done((f32[2,4,8,8,128]{4,3,2,1,0:T(8,128)S(1)}, f32[2,4,8,8,128]{4,3,2,1,0:T(8,128)S(1)}, u32[]{:S(2)}, u32[]{:S(2)}) %collective-permute-start.3) | collective-permute-done | bytes 262176 | tf_op jit(solution)/shard_map/ppermute | solution.py:597
  22.5 0.0 collective-permute-done.m2
  22.5 0.0 collective-permute-done.1.m1
  22.5 1.2 %halo1.1 = (f32[8,8,16,128]{3,2,1,0:T(8,128)S(1)}, f32[8,8,16,128]{3,2,1,0:T(8,128)S(1)}, f32[2,5,8,16,128]{4,3,2,1,0:T(8,128)S(1)}, f32[2,5,8,16,128]{4,3,2,1,0...) custom-call(f32[8,8,16,128]{3,2,1,0:T(8,128)S(1)} %get-tuple-element, ...), custom_call_target="tpu_custom_call" | custom-call | tf_op jit(solution)/shard_map/halo1/pallas_call | solution.py:518
  23.7 0.1 collective-permute-start.5
  23.8 2.5 %collective-permute-start.6 = (f32[2,4,8,8,128]{4,3,2,1,0:T(8,128)S(1)}, f32[2,4,8,8,128]{4,3,2,1,0:T(8,128)S(1)}, u32[]{:S(2)}, u32[]{:S(2)}) collective-permute-start(f32[2,4,8,8,128]{4,3,2,1,0:T(8,128)S(1)} %get-tuple-element.46), channel_id=1, source_target_pairs={{0,8},{1,2},{2,1},{3,4},{4,3},{5,6},{6,5},{7,15},{8,0},{9,10},{10,... | collective-permute-start | bytes 786440 | tf_op jit(solution)/shard_map/ppermute | solution.py:597
  26.3 0.0 collective-permute-start.4
  26.3 0.0 collective-permute-start.7
  26.3 3.7 %local2.1 = (f32[8,8,16,128]{3,2,1,0:T(8,128)S(1)}, f32[8,8,16,128]{3,2,1,0:T(8,128)S(1)}) custom-call(f32[8,8,16,128]{3,2,1,0:T(8,128)S(1)} %get-tuple-element.48.source_ref, f32[8,8,16,128]{3,2,1,0:T(8,128)S(1)} %get-tuple-element.49.receiver_ref, f32[8,16,1024]{2,1,0:T(8,128)S(1)} %get-tuple-element.33.now_ref.source_old, ...), custom_call_target="tpu_custom_call" | custom-call | tf_op jit(solution)/shard_map/local2/pallas_call | solution.py:518
  30.0 5.4 %collective-permute-done.6.refs_1_ = f32[2,4,8,8,128]{4,3,2,1,0:T(8,128)S(1)} collective-permute-done((f32[2,4,8,8,128]{4,3,2,1,0:T(8,128)S(1)}, f32[2,4,8,8,128]{4,3,2,1,0:T(8,128)S(1)}, u32[]{:S(2)}, u32[]{:S(2)}) %collective-permute-start.6) | collective-permute-done | bytes 262176 | tf_op jit(solution)/shard_map/ppermute | solution.py:597
  35.4 0.5 %collective-permute-done.5.refs_0_ = f32[2,5,8,16,128]{4,3,2,1,0:T(8,128)S(1)} collective-permute-done((f32[2,5,8,16,128]{4,3,2,1,0:T(8,128)S(1)}, f32[2,5,8,16,128]{4,3,2,1,0:T(8,128)S(1)}, u32[]{:S(2)}, u32[]{:S(2)}) %collective-permute-start.5) | collective-permute-done | bytes 655392 | tf_op jit(solution)/shard_map/ppermute | solution.py:589
  35.9 0.0 collective-permute-done.7.m3
  35.9 0.0 collective-permute-done.4.m1
  35.9 1.1 %halo2.1 = (f32[8,16,1024]{2,1,0:T(8,128)S(1)}, f32[8,16,1024]{2,1,0:T(8,128)S(1)}, f32[2,8,4,8,128]{4,3,2,1,0:T(8,128)S(1)}) custom-call(f32[8,8,16,128]{3,2,1,0:T(8,128)S(1)} %get-tuple-element.51.source_part, f32[8,8,16,128]{3,2,1,0:T(8,128)S(1)} %get-tuple-element.52.receiver_part, f32[8,16,1024]{2,1,0:T(8,128)S(1)} %get-tuple-element.37.velocity_ref, ...), custom_call_target="tpu_custom_call" | custom-call | tf_op jit(solution)/shard_map/halo2/pallas_call | solution.py:518
  37.1 1.0 %collective-permute-start.9 = (f32[2,8,4,8,128]{4,3,2,1,0:T(8,128)S(1)}, f32[2,8,4,8,128]{4,3,2,1,0:T(8,128)S(1)}, u32[]{:S(2)}, u32[]{:S(2)}) collective-permute-start(f32[2,8,4,8,128]{4,3,2,1,0:T(8,128)S(1)} %get-tuple-element.59.coarse_ref), channel_id=1, source_target_pairs={{0,1},{1,0},{2,3},{3,2},{4,5},{5,4},{6,7},{7,6},{8,16},{9,17},{10,... | collective-permute-start | bytes 786440 | tf_op jit(solution)/shard_map/ppermute | solution.py:589
  38.1 0.3 collective-permute-start.8
  38.4 1.0 %image1.1 = (f32[17,4,4,8,128]{4,3,2,1,0:T(8,128)S(1)}, f32[8,16,1024]{2,1,0:T(8,128)}, f32[8,16,1024]{2,1,0:T(8,128)}) custom-call(f32[2,8,4,8,128]{4,3,2,1,0:T(8,128)S(1)} %get-tuple-element.43.coarse_ref, f32[2,5,8,16,128]{4,3,2,1,0:T(8,128)S(1)} %collective-permute-done.4.m1, f32[2,5,8,16,128]{4,3,2,1,0:T(8,128)S(1)} %get-tuple-element.47.m2, ...), custom_call_target="tpu_custom_call" | custom-call | tf_op jit(solution)/shard_map/image1/pallas_call | solution.py:518
  39.4 5.7 %collective-permute-done.9.m2 = f32[2,8,4,8,128]{4,3,2,1,0:T(8,128)S(1)} collective-permute-done((f32[2,8,4,8,128]{4,3,2,1,0:T(8,128)S(1)}, f32[2,8,4,8,128]{4,3,2,1,0:T(8,128)S(1)}, u32[]{:S(2)}, u32[]{:S(2)}) %collective-permute-start.9) | collective-permute-done | bytes 262176 | tf_op jit(solution)/shard_map/ppermute | solution.py:589
  45.1 0.0 collective-permute-done.8.m1
  45.1 1.1 %image2.1 = f32[17,4,8,512]{3,2,1,0:T(8,128)} custom-call(f32[2,8,4,8,128]{4,3,2,1,0:T(8,128)S(1)} %get-tuple-element.59.coarse_ref, f32[2,8,4,8,128]{4,3,2,1,0:T(8,128)S(1)} %collective-permute-done.8.m1, f32[2,8,4,8,128]{4,3,2,1,0:T(8,128)S(1)} %collective-permute-done.9.m2, f32[17,4,4,8,128]{4,3,2,1,0:T(8,128)S(1)} %get-tuple-element.60.before_ref), custom_call_target="tpu_custom_call" | custom-call | tf_op jit(solution)/shard_map/image2/pallas_call | solution.py:518
  (1 shorter events, 0.0 us)
Async XLA Ops:
  2.0 20.5 %collective-permute-start = (f32[2,4,8,16,128]{4,3,2,1,0:T(8,128)S(1)}, f32[2,4,8,16,128]{4,3,2,1,0:T(8,128)S(1)}, u32[]{:S(2)}, u32[]{:S(2)}) collective-permute-start(f32[2,4,8,16,128]{4,3,2,1,0:T(8,128)S(1)} %get-tuple-element.39), channel_id=1, source_target_pairs={{0,1},{1,0},{2,3},{3,2},{4,5},{5,4},{6,7},{7,6},{8,16},{9,17},{10,... | collective-permute-start | bytes 1572872 | tf_op jit(solution)/shard_map/ppermute | solution.py:589
  5.8 16.8 %collective-permute-start.1 = (f32[2,4,8,16,128]{4,3,2,1,0:T(8,128)S(1)}, f32[2,4,8,16,128]{4,3,2,1,0:T(8,128)S(1)}, u32[]{:S(2)}, u32[]{:S(2)}) collective-permute-start(f32[2,4,8,16,128]{4,3,2,1,0:T(8,128)S(1)} %get-tuple-element.40), channel_id=1, source_target_pairs={{0,8},{8,0},{16,24},{24,16},{32,40},{40,32},{48,56},{56,48},{64,72... | collective-permute-start | bytes 1572872 | tf_op jit(solution)/shard_map/ppermute | solution.py:589
  5.8 11.3 %collective-permute-start.2 = (f32[2,4,8,8,128]{4,3,2,1,0:T(8,128)S(1)}, f32[2,4,8,8,128]{4,3,2,1,0:T(8,128)S(1)}, u32[]{:S(2)}, u32[]{:S(2)}) collective-permute-start(f32[2,4,8,8,128]{4,3,2,1,0:T(8,128)S(1)} %get-tuple-element.41), channel_id=1, source_target_pairs={{0,1},{1,0},{2,3},{3,2},{4,5},{5,4},{6,7},{7,6},{8,9},{9,8},{10,11... | collective-permute-start | bytes 786440 | tf_op jit(solution)/shard_map/ppermute | solution.py:593
  10.3 12.2 %collective-permute-start.3 = (f32[2,4,8,8,128]{4,3,2,1,0:T(8,128)S(1)}, f32[2,4,8,8,128]{4,3,2,1,0:T(8,128)S(1)}, u32[]{:S(2)}, u32[]{:S(2)}) collective-permute-start(f32[2,4,8,8,128]{4,3,2,1,0:T(8,128)S(1)} %get-tuple-element.42), channel_id=1, source_target_pairs={{0,8},{1,2},{2,1},{3,4},{4,3},{5,6},{6,5},{7,15},{8,0},{9,10},{10,... | collective-permute-start | bytes 786440 | tf_op jit(solution)/shard_map/ppermute | solution.py:597
  23.7 12.2 %collective-permute-start.5 = (f32[2,5,8,16,128]{4,3,2,1,0:T(8,128)S(1)}, f32[2,5,8,16,128]{4,3,2,1,0:T(8,128)S(1)}, u32[]{:S(2)}, u32[]{:S(2)}) collective-permute-start(f32[2,5,8,16,128]{4,3,2,1,0:T(8,128)S(1)} %get-tuple-element.45), channel_id=1, source_target_pairs={{0,1},{1,0},{2,122},{3,123},{4,124},{5,125},{6,7},{7,6},{8,16},{9,... | collective-permute-start | bytes 1966088 | tf_op jit(solution)/shard_map/ppermute | solution.py:589
  23.8 11.6 %collective-permute-start.6 = (f32[2,4,8,8,128]{4,3,2,1,0:T(8,128)S(1)}, f32[2,4,8,8,128]{4,3,2,1,0:T(8,128)S(1)}, u32[]{:S(2)}, u32[]{:S(2)}) collective-permute-start(f32[2,4,8,8,128]{4,3,2,1,0:T(8,128)S(1)} %get-tuple-element.46), channel_id=1, source_target_pairs={{0,8},{1,2},{2,1},{3,4},{4,3},{5,6},{6,5},{7,15},{8,0},{9,10},{10,... | collective-permute-start | bytes 786440 | tf_op jit(solution)/shard_map/ppermute | solution.py:597
  26.3 9.7 %collective-permute-start.4 = (f32[2,5,8,16,128]{4,3,2,1,0:T(8,128)S(1)}, f32[2,5,8,16,128]{4,3,2,1,0:T(8,128)S(1)}, u32[]{:S(2)}, u32[]{:S(2)}) collective-permute-start(f32[2,5,8,16,128]{4,3,2,1,0:T(8,128)S(1)} %get-tuple-element.44), channel_id=1, source_target_pairs={{0,8},{8,0},{16,24},{24,16},{32,40},{40,32},{48,56},{56,48},{64,72... | collective-permute-start | bytes 1966088 | tf_op jit(solution)/shard_map/ppermute | solution.py:589
  26.3 9.7 %collective-permute-start.7 = (f32[2,4,8,8,128]{4,3,2,1,0:T(8,128)S(1)}, f32[2,4,8,8,128]{4,3,2,1,0:T(8,128)S(1)}, u32[]{:S(2)}, u32[]{:S(2)}) collective-permute-start(f32[2,4,8,8,128]{4,3,2,1,0:T(8,128)S(1)} %get-tuple-element.53), channel_id=1, source_target_pairs={{0,1},{1,0},{2,3},{3,2},{4,5},{5,4},{6,7},{7,6},{8,9},{9,8},{10,11... | collective-permute-start | bytes 786440 | tf_op jit(solution)/shard_map/ppermute | solution.py:593
  37.1 8.0 %collective-permute-start.9 = (f32[2,8,4,8,128]{4,3,2,1,0:T(8,128)S(1)}, f32[2,8,4,8,128]{4,3,2,1,0:T(8,128)S(1)}, u32[]{:S(2)}, u32[]{:S(2)}) collective-permute-start(f32[2,8,4,8,128]{4,3,2,1,0:T(8,128)S(1)} %get-tuple-element.59.coarse_ref), channel_id=1, source_target_pairs={{0,1},{1,0},{2,3},{3,2},{4,5},{5,4},{6,7},{7,6},{8,16},{9,17},{10,... | collective-permute-start | bytes 786440 | tf_op jit(solution)/shard_map/ppermute | solution.py:589
  38.1 7.0 %collective-permute-start.8 = (f32[2,8,4,8,128]{4,3,2,1,0:T(8,128)S(1)}, f32[2,8,4,8,128]{4,3,2,1,0:T(8,128)S(1)}, u32[]{:S(2)}, u32[]{:S(2)}) collective-permute-start(f32[2,8,4,8,128]{4,3,2,1,0:T(8,128)S(1)} %get-tuple-element.59.coarse_ref), channel_id=1, source_target_pairs={{0,8},{8,0},{16,24},{24,16},{32,40},{40,32},{48,56},{56,48},{64,72... | collective-permute-start | bytes 786440 | tf_op jit(solution)/shard_map/ppermute | solution.py:589

commit v5 on v4

--- a/solution.py
+++ b/solution.py
@@ -317,26 +317,32 @@
     stencil(ext, receiver_old, velocity_ref, receiver_part, inject_ref)
 
 
-def halo_terms(m1, m2, m3, m4, rows_low, rows_high, f, l, flags):
+def halo_terms(m1, m2, m3, m4, f, l, flags):
     gx_even, has_left, has_right, gy_even, has_below, has_above = flags
     left, right = [], []
     for p in range(4):
         a, b = m1[f, p, l], m2[f, p, l]
         left.append(jnp.where(has_left, pick(gx_even, b, a), 0.0))
         right.append(jnp.where(has_right, pick(gx_even, a, b), 0.0))
+    row = lax.broadcasted_iota(jnp.int32, (8, 128), 0)
+    step = row & 3
+    first = row < 4
+    lows, highs = [None] * VX, [None] * VX
+    for i in range(4):
+        a, b = m3[f, i, l], m4[f, i, l]
+        low = jnp.where(has_below, pick(gy_even, b, a), 0.0)
+        high = jnp.where(has_above, pick(gy_even, a, b), 0.0)
+        below, above = COEF[4] * low, COEF[4] * high
+        for d in range(1, 4):
+            below = below + jnp.where(step < d, COEF[d], 0.0) * pltpu.roll(low, 4 + d, 0)
+            above = above + jnp.where(step >= 4 - d, COEF[d], 0.0) * pltpu.roll(high, 4 - d, 0)
+        lows[i] = jnp.where(first, below, 0.0)
+        lows[i + 4] = jnp.where(first, pltpu.roll(below, 4, 0), 0.0)
+        highs[i] = jnp.where(first, 0.0, pltpu.roll(above, 4, 0))
+        highs[i + 4] = jnp.where(first, 0.0, above)
     out = []
     for p in range(VX):
-        i, r = p % 4, 4 * (p // 4)
-        a, b = m3[f, i, l, r : r + 4, :], m4[f, i, l, r : r + 4, :]
-        rows_low[p, 0:4, :] = jnp.where(has_below, pick(gy_even, b, a), 0.0)
-        rows_high[p, 8:12, :] = jnp.where(has_above, pick(gy_even, a, b), 0.0)
-    for p in range(VX):
-        below = COEF[1] * rows_low[p, 3:11, :]
-        above = COEF[1] * rows_high[p, 1:9, :]
-        for d in range(2, 5):
-            below = below + COEF[d] * rows_low[p, 4 - d : 12 - d, :]
-            above = above + COEF[d] * rows_high[p, d : d + 8, :]
-        total = jnp.concatenate((below, above), axis=0)
+        total = jnp.concatenate((lows[p], highs[p]), axis=0)
         for d in range(1, 5):
             if p - d < 0:
                 total = total + COEF[d] * left[4 + p - d]
@@ -356,12 +362,6 @@
         gy > 0,
         gy < lax.axis_size("gy") - 1,
     )
-
-
-def clear_rows(rows_low, rows_high):
-    for p in range(VX):
-        rows_low[p] = jnp.zeros((16, 128), F32)
-        rows_high[p] = jnp.zeros((16, 128), F32)
 
 
 def first_halo_kernel(
@@ -379,16 +379,13 @@
     s3,
     s4,
     coarse_ref,
-    rows_low,
-    rows_high,
 ):
     flags = flags_of()
     gx_even, gy_even = flags[0], flags[3]
-    clear_rows(rows_low, rows_high)
     for f, (part, out) in enumerate(((source_part, source_ref), (receiver_part, receiver_ref))):
 
         def tile(l, carry, f=f, part=part, out=out):
-            terms = halo_terms(m1, m2, m3, m4, rows_low, rows_high, f, l, flags)
+            terms = halo_terms(m1, m2, m3, m4, f, l, flags)
             new = []
             for p in range(VX):
                 value = part[p, l] + velocity_ref[p, :, lanes_of(l)] * terms[p]
@@ -424,16 +421,13 @@
     source_ref,
     receiver_ref,
     coarse_ref,
-    rows_low,
-    rows_high,
     stage,
 ):
     flags = flags_of()
-    clear_rows(rows_low, rows_high)
     for f, (part, out) in enumerate(((source_part, source_ref), (receiver_part, receiver_ref))):
 
         def tile(l, carry, f=f, part=part, out=out):
-            terms = halo_terms(m1, m2, m3, m4, rows_low, rows_high, f, l, flags)
+            terms = halo_terms(m1, m2, m3, m4, f, l, flags)
             for p in range(VX):
                 value = part[p, l] + velocity_ref[p, :, lanes_of(l)] * terms[p]
                 out[p, :, lanes_of(l)] = value
@@ -610,7 +604,6 @@
 ):
     block = (VX, VY, VZ)
     ext = pltpu.VMEM((VX, LT + 2, 32, 128), F32)
-    rows = pltpu.VMEM((VX, 16, 128), F32)
     whole = pltpu.VMEM(block, F32)
     m1, m2, m3, m4, source, receiver = call(
         first_pack_kernel,
@@ -664,7 +657,6 @@
         first_halo_kernel,
         vmem(source_part, receiver_part, velocity, g2, g1, g3, g4),
         vmem(FIELD, FIELD, XSLAB_COARSE, XSLAB_COARSE, YSLAB, YSLAB, COARSE),
-        (rows, rows),
         name="halo1",
     )
     g4 = outer_y(m4)
@@ -682,7 +674,7 @@
         second_halo_kernel,
         vmem(source_part, receiver_part, velocity, g2, g1, g3, g4),
         vmem(block, block, COARSE),
-        (rows, rows, pltpu.VMEM(FIELD, F32)),
+        (pltpu.VMEM(FIELD, F32),),
         name="halo2",
     )
     far = along_x(last, last)

time: 46.3 us -> 46.1 us (level)
  no operation moved by 1% of the time
where the time goes in v5:
time: 46.1 us; the launch traced here: 45.9 us
  waiting for transfers between devices  17 us (37%)
  Pallas kernels  16.6 us (36%)
  starting transfers between devices  11.7 us (25%)
  between operations  0.71 us (2%)
    pallas_call x8, Pallas kernels, call(): pl.pallas_call(kernel, out_shape=[jax.ShapeDtypeStruct(s, F32) for _, s i...  16.6 us
    ppermute x2, waiting for transfers between devices, outer_y(): return lax.ppermute(m4, ('gx', 'gy'), y_outer())  10.8 us
    ppermute x3, waiting for transfers between devices, along_x(): lax.ppermute(m2, ('gx', 'gy'), x_outer(near))  6.15 us
    ppermute x2, starting transfers between devices, outer_y(): return lax.ppermute(m4, ('gx', 'gy'), y_outer())  5.01 us
    ppermute x3, starting transfers between devices, along_x(): lax.ppermute(m2, ('gx', 'gy'), x_outer(near))  4.87 us
    ppermute x2, starting transfers between devices, inner_y(): return lax.ppermute(m3, 'gy', inner('gy'))  1.49 us
  transfers between devices with their start and end apart: 10, of which 4 were waited for; matrix products, arithmetic and copies ran while one was open for 0% of the time, Pallas kernels for 26%

profile of v5, /device:TPU:24, one launch (start us, length us, event | category | flops | bytes accessed | tf_op | source)
XLA Modules:
  0.0 45.9 jit_solution(6609651043013453369)
XLA Ops:
  0.6 1.4 %pack.1 = (f32[2,4,8,16,128]{4,3,2,1,0:T(8,128)S(1)}, f32[2,4,8,16,128]{4,3,2,1,0:T(8,128)S(1)}, f32[2,4,8,8,128]{4,3,2,1,0:T(8,128)S(1)}, f32[2,4,8,8,128]{4,3,...) custom-call(f32[8,16,1024]{2,1,0:T(8,128)} %source_hbm.1, f32[8,16,1024]{2,1,0:T(8,128)} %receiver_hbm.1), custom_call_target="tpu_custom_call" | custom-call | tf_op jit(solution)/shard_map/pack/pallas_call | solution.py:512
  2.0 3.7 %collective-permute-start = (f32[2,4,8,16,128]{4,3,2,1,0:T(8,128)S(1)}, f32[2,4,8,16,128]{4,3,2,1,0:T(8,128)S(1)}, u32[]{:S(2)}, u32[]{:S(2)}) collective-permute-start(f32[2,4,8,16,128]{4,3,2,1,0:T(8,128)S(1)} %get-tuple-element.39), channel_id=1, source_target_pairs={{0,1},{1,0},{2,3},{3,2},{4,5},{5,4},{6,7},{7,6},{8,16},{9,17},{10,... | collective-permute-start | bytes 1572872 | tf_op jit(solution)/shard_map/ppermute | solution.py:583
  5.8 0.0 collective-permute-start.1
  5.8 1.5 %collective-permute-start.2 = (f32[2,4,8,8,128]{4,3,2,1,0:T(8,128)S(1)}, f32[2,4,8,8,128]{4,3,2,1,0:T(8,128)S(1)}, u32[]{:S(2)}, u32[]{:S(2)}) collective-permute-start(f32[2,4,8,8,128]{4,3,2,1,0:T(8,128)S(1)} %get-tuple-element.41), channel_id=1, source_target_pairs={{0,1},{1,0},{2,3},{3,2},{4,5},{5,4},{6,7},{7,6},{8,9},{9,8},{10,11... | collective-permute-start | bytes 786440 | tf_op jit(solution)/shard_map/ppermute | solution.py:587
  7.3 3.0 %source1.1 = (f32[8,8,16,128]{3,2,1,0:T(8,128)S(1)}, f32[8,16,1024]{2,1,0:T(8,128)S(1)}) custom-call(f32[8,16,1024]{2,1,0:T(8,128)S(1)} %get-tuple-element.33.now_ref.source_old, f32[8,16,1024]{2,1,0:T(8,128)} %prev_hbm.2, f32[8,16,1024]{2,1,0:T(8,128)} %velocity_hbm.1, s32[4]{0:T(128)} %cells_hbm.5, f32[2,4]{1,0:T(2,128)} %wavelet_hbm.3), custom_call_target="tpu_custom_call" | custom-call | tf_op jit(solution)/shard_map/source1/pallas_call | solution.py:512
  10.3 2.6 %collective-permute-start.3 = (f32[2,4,8,8,128]{4,3,2,1,0:T(8,128)S(1)}, f32[2,4,8,8,128]{4,3,2,1,0:T(8,128)S(1)}, u32[]{:S(2)}, u32[]{:S(2)}) collective-permute-start(f32[2,4,8,8,128]{4,3,2,1,0:T(8,128)S(1)} %get-tuple-element.42), channel_id=1, source_target_pairs={{0,8},{1,2},{2,1},{3,4},{4,3},{5,6},{6,5},{7,15},{8,0},{9,10},{10,... | collective-permute-start | bytes 786440 | tf_op jit(solution)/shard_map/ppermute | solution.py:591
  12.8 4.3 %receiver1.1 = (f32[8,8,16,128]{3,2,1,0:T(8,128)S(1)}, f32[8,8,16,128]{3,2,1,0:T(8,128)S(1)}) custom-call(f32[8,16,1024]{2,1,0:T(8,128)S(1)} %get-tuple-element.36.now_ref.receiver_old, f32[8,16,1024]{2,1,0:T(8,128)S(1)} %get-tuple-element.37.velocity_ref, f32[8,16,1024]{2,1,0:T(8,128)} %prev_hbm.3, s32[32,128]{1,0:T(8,128)} %bitcast.1, s32[4096]{0:T(1024)} %cells_hbm.4, ...), custom_call_target="tpu_custom_call" | custom-call | tf_op jit(solution)/shard_map/receiver1/pallas_call | solution.py:512
  17.1 0.0 collective-permute-done.2.m3
  17.1 5.4 %collective-permute-done.3.m4 = f32[2,4,8,8,128]{4,3,2,1,0:T(8,128)S(1)} collective-permute-done((f32[2,4,8,8,128]{4,3,2,1,0:T(8,128)S(1)}, f32[2,4,8,8,128]{4,3,2,1,0:T(8,128)S(1)}, u32[]{:S(2)}, u32[]{:S(2)}) %collective-permute-start.3) | collective-permute-done | bytes 262176 | tf_op jit(solution)/shard_map/ppermute | solution.py:591
  22.5 0.0 collective-permute-done.m2
  22.5 0.0 collective-permute-done.1.m1
  22.5 1.1 %halo1.1 = (f32[8,8,16,128]{3,2,1,0:T(8,128)S(1)}, f32[8,8,16,128]{3,2,1,0:T(8,128)S(1)}, f32[2,5,8,16,128]{4,3,2,1,0:T(8,128)S(1)}, f32[2,5,8,16,128]{4,3,2,1,0...) custom-call(f32[8,8,16,128]{3,2,1,0:T(8,128)S(1)} %get-tuple-element, ...), custom_call_target="tpu_custom_call" | custom-call | tf_op jit(solution)/shard_map/halo1/pallas_call | solution.py:512
  23.6 0.1 collective-permute-start.5
  23.7 2.5 %collective-permute-start.6 = (f32[2,4,8,8,128]{4,3,2,1,0:T(8,128)S(1)}, f32[2,4,8,8,128]{4,3,2,1,0:T(8,128)S(1)}, u32[]{:S(2)}, u32[]{:S(2)}) collective-permute-start(f32[2,4,8,8,128]{4,3,2,1,0:T(8,128)S(1)} %get-tuple-element.46), channel_id=1, source_target_pairs={{0,8},{1,2},{2,1},{3,4},{4,3},{5,6},{6,5},{7,15},{8,0},{9,10},{10,... | collective-permute-start | bytes 786440 | tf_op jit(solution)/shard_map/ppermute | solution.py:591
  26.2 0.0 collective-permute-start.4
  26.2 0.0 collective-permute-start.7
  26.2 3.7 %local2.1 = (f32[8,8,16,128]{3,2,1,0:T(8,128)S(1)}, f32[8,8,16,128]{3,2,1,0:T(8,128)S(1)}) custom-call(f32[8,8,16,128]{3,2,1,0:T(8,128)S(1)} %get-tuple-element.48.source_ref, f32[8,8,16,128]{3,2,1,0:T(8,128)S(1)} %get-tuple-element.49.receiver_ref, f32[8,16,1024]{2,1,0:T(8,128)S(1)} %get-tuple-element.33.now_ref.source_old, ...), custom_call_target="tpu_custom_call" | custom-call | tf_op jit(solution)/shard_map/local2/pallas_call | solution.py:512
  29.9 5.4 %collective-permute-done.6.refs_1_ = f32[2,4,8,8,128]{4,3,2,1,0:T(8,128)S(1)} collective-permute-done((f32[2,4,8,8,128]{4,3,2,1,0:T(8,128)S(1)}, f32[2,4,8,8,128]{4,3,2,1,0:T(8,128)S(1)}, u32[]{:S(2)}, u32[]{:S(2)}) %collective-permute-start.6) | collective-permute-done | bytes 262176 | tf_op jit(solution)/shard_map/ppermute | solution.py:591
  35.3 0.5 %collective-permute-done.5.refs_0_ = f32[2,5,8,16,128]{4,3,2,1,0:T(8,128)S(1)} collective-permute-done((f32[2,5,8,16,128]{4,3,2,1,0:T(8,128)S(1)}, f32[2,5,8,16,128]{4,3,2,1,0:T(8,128)S(1)}, u32[]{:S(2)}, u32[]{:S(2)}) %collective-permute-start.5) | collective-permute-done | bytes 655392 | tf_op jit(solution)/shard_map/ppermute | solution.py:583
  35.8 0.0 collective-permute-done.7.m3
  35.8 0.0 collective-permute-done.4.m1
  35.8 1.0 %halo2.1 = (f32[8,16,1024]{2,1,0:T(8,128)S(1)}, f32[8,16,1024]{2,1,0:T(8,128)S(1)}, f32[2,8,4,8,128]{4,3,2,1,0:T(8,128)S(1)}) custom-call(f32[8,8,16,128]{3,2,1,0:T(8,128)S(1)} %get-tuple-element.51.source_part, f32[8,8,16,128]{3,2,1,0:T(8,128)S(1)} %get-tuple-element.52.receiver_part, f32[8,16,1024]{2,1,0:T(8,128)S(1)} %get-tuple-element.37.velocity_ref, ...), custom_call_target="tpu_custom_call" | custom-call | tf_op jit(solution)/shard_map/halo2/pallas_call | solution.py:512
  36.8 1.0 %collective-permute-start.9 = (f32[2,8,4,8,128]{4,3,2,1,0:T(8,128)S(1)}, f32[2,8,4,8,128]{4,3,2,1,0:T(8,128)S(1)}, u32[]{:S(2)}, u32[]{:S(2)}) collective-permute-start(f32[2,8,4,8,128]{4,3,2,1,0:T(8,128)S(1)} %get-tuple-element.59.coarse_ref), channel_id=1, source_target_pairs={{0,1},{1,0},{2,3},{3,2},{4,5},{5,4},{6,7},{7,6},{8,16},{9,17},{10,... | collective-permute-start | bytes 786440 | tf_op jit(solution)/shard_map/ppermute | solution.py:583
  37.9 0.3 collective-permute-start.8
  38.2 1.0 %image1.1 = (f32[17,4,4,8,128]{4,3,2,1,0:T(8,128)S(1)}, f32[8,16,1024]{2,1,0:T(8,128)}, f32[8,16,1024]{2,1,0:T(8,128)}) custom-call(f32[2,8,4,8,128]{4,3,2,1,0:T(8,128)S(1)} %get-tuple-element.43.coarse_ref, f32[2,5,8,16,128]{4,3,2,1,0:T(8,128)S(1)} %collective-permute-done.4.m1, f32[2,5,8,16,128]{4,3,2,1,0:T(8,128)S(1)} %get-tuple-element.47.m2, ...), custom_call_target="tpu_custom_call" | custom-call | tf_op jit(solution)/shard_map/image1/pallas_call | solution.py:512
  39.2 5.7 %collective-permute-done.9.m2 = f32[2,8,4,8,128]{4,3,2,1,0:T(8,128)S(1)} collective-permute-done((f32[2,8,4,8,128]{4,3,2,1,0:T(8,128)S(1)}, f32[2,8,4,8,128]{4,3,2,1,0:T(8,128)S(1)}, u32[]{:S(2)}, u32[]{:S(2)}) %collective-permute-start.9) | collective-permute-done | bytes 262176 | tf_op jit(solution)/shard_map/ppermute | solution.py:583
  44.8 0.0 collective-permute-done.8.m1
  44.8 1.1 %image2.1 = f32[17,4,8,512]{3,2,1,0:T(8,128)} custom-call(f32[2,8,4,8,128]{4,3,2,1,0:T(8,128)S(1)} %get-tuple-element.59.coarse_ref, f32[2,8,4,8,128]{4,3,2,1,0:T(8,128)S(1)} %collective-permute-done.8.m1, f32[2,8,4,8,128]{4,3,2,1,0:T(8,128)S(1)} %collective-permute-done.9.m2, f32[17,4,4,8,128]{4,3,2,1,0:T(8,128)S(1)} %get-tuple-element.60.before_ref), custom_call_target="tpu_custom_call" | custom-call | tf_op jit(solution)/shard_map/image2/pallas_call | solution.py:512
  (1 shorter events, 0.0 us)
Async XLA Ops:
  2.0 20.5 %collective-permute-start = (f32[2,4,8,16,128]{4,3,2,1,0:T(8,128)S(1)}, f32[2,4,8,16,128]{4,3,2,1,0:T(8,128)S(1)}, u32[]{:S(2)}, u32[]{:S(2)}) collective-permute-start(f32[2,4,8,16,128]{4,3,2,1,0:T(8,128)S(1)} %get-tuple-element.39), channel_id=1, source_target_pairs={{0,1},{1,0},{2,3},{3,2},{4,5},{5,4},{6,7},{7,6},{8,16},{9,17},{10,... | collective-permute-start | bytes 1572872 | tf_op jit(solution)/shard_map/ppermute | solution.py:583
  5.8 16.8 %collective-permute-start.1 = (f32[2,4,8,16,128]{4,3,2,1,0:T(8,128)S(1)}, f32[2,4,8,16,128]{4,3,2,1,0:T(8,128)S(1)}, u32[]{:S(2)}, u32[]{:S(2)}) collective-permute-start(f32[2,4,8,16,128]{4,3,2,1,0:T(8,128)S(1)} %get-tuple-element.40), channel_id=1, source_target_pairs={{0,8},{8,0},{16,24},{24,16},{32,40},{40,32},{48,56},{56,48},{64,72... | collective-permute-start | bytes 1572872 | tf_op jit(solution)/shard_map/ppermute | solution.py:583
  5.8 11.4 %collective-permute-start.2 = (f32[2,4,8,8,128]{4,3,2,1,0:T(8,128)S(1)}, f32[2,4,8,8,128]{4,3,2,1,0:T(8,128)S(1)}, u32[]{:S(2)}, u32[]{:S(2)}) collective-permute-start(f32[2,4,8,8,128]{4,3,2,1,0:T(8,128)S(1)} %get-tuple-element.41), channel_id=1, source_target_pairs={{0,1},{1,0},{2,3},{3,2},{4,5},{5,4},{6,7},{7,6},{8,9},{9,8},{10,11... | collective-permute-start | bytes 786440 | tf_op jit(solution)/shard_map/ppermute | solution.py:587
  10.3 12.2 %collective-permute-start.3 = (f32[2,4,8,8,128]{4,3,2,1,0:T(8,128)S(1)}, f32[2,4,8,8,128]{4,3,2,1,0:T(8,128)S(1)}, u32[]{:S(2)}, u32[]{:S(2)}) collective-permute-start(f32[2,4,8,8,128]{4,3,2,1,0:T(8,128)S(1)} %get-tuple-element.42), channel_id=1, source_target_pairs={{0,8},{1,2},{2,1},{3,4},{4,3},{5,6},{6,5},{7,15},{8,0},{9,10},{10,... | collective-permute-start | bytes 786440 | tf_op jit(solution)/shard_map/ppermute | solution.py:591
  23.6 12.2 %collective-permute-start.5 = (f32[2,5,8,16,128]{4,3,2,1,0:T(8,128)S(1)}, f32[2,5,8,16,128]{4,3,2,1,0:T(8,128)S(1)}, u32[]{:S(2)}, u32[]{:S(2)}) collective-permute-start(f32[2,5,8,16,128]{4,3,2,1,0:T(8,128)S(1)} %get-tuple-element.45), channel_id=1, source_target_pairs={{0,1},{1,0},{2,122},{3,123},{4,124},{5,125},{6,7},{7,6},{8,16},{9,... | collective-permute-start | bytes 1966088 | tf_op jit(solution)/shard_map/ppermute | solution.py:583
  23.7 11.6 %collective-permute-start.6 = (f32[2,4,8,8,128]{4,3,2,1,0:T(8,128)S(1)}, f32[2,4,8,8,128]{4,3,2,1,0:T(8,128)S(1)}, u32[]{:S(2)}, u32[]{:S(2)}) collective-permute-start(f32[2,4,8,8,128]{4,3,2,1,0:T(8,128)S(1)} %get-tuple-element.46), channel_id=1, source_target_pairs={{0,8},{1,2},{2,1},{3,4},{4,3},{5,6},{6,5},{7,15},{8,0},{9,10},{10,... | collective-permute-start | bytes 786440 | tf_op jit(solution)/shard_map/ppermute | solution.py:591
  26.2 9.7 %collective-permute-start.4 = (f32[2,5,8,16,128]{4,3,2,1,0:T(8,128)S(1)}, f32[2,5,8,16,128]{4,3,2,1,0:T(8,128)S(1)}, u32[]{:S(2)}, u32[]{:S(2)}) collective-permute-start(f32[2,5,8,16,128]{4,3,2,1,0:T(8,128)S(1)} %get-tuple-element.44), channel_id=1, source_target_pairs={{0,8},{8,0},{16,24},{24,16},{32,40},{40,32},{48,56},{56,48},{64,72... | collective-permute-start | bytes 1966088 | tf_op jit(solution)/shard_map/ppermute | solution.py:583
  26.2 9.7 %collective-permute-start.7 = (f32[2,4,8,8,128]{4,3,2,1,0:T(8,128)S(1)}, f32[2,4,8,8,128]{4,3,2,1,0:T(8,128)S(1)}, u32[]{:S(2)}, u32[]{:S(2)}) collective-permute-start(f32[2,4,8,8,128]{4,3,2,1,0:T(8,128)S(1)} %get-tuple-element.53), channel_id=1, source_target_pairs={{0,1},{1,0},{2,3},{3,2},{4,5},{5,4},{6,7},{7,6},{8,9},{9,8},{10,11... | collective-permute-start | bytes 786440 | tf_op jit(solution)/shard_map/ppermute | solution.py:587
  36.8 8.0 %collective-permute-start.9 = (f32[2,8,4,8,128]{4,3,2,1,0:T(8,128)S(1)}, f32[2,8,4,8,128]{4,3,2,1,0:T(8,128)S(1)}, u32[]{:S(2)}, u32[]{:S(2)}) collective-permute-start(f32[2,8,4,8,128]{4,3,2,1,0:T(8,128)S(1)} %get-tuple-element.59.coarse_ref), channel_id=1, source_target_pairs={{0,1},{1,0},{2,3},{3,2},{4,5},{5,4},{6,7},{7,6},{8,16},{9,17},{10,... | collective-permute-start | bytes 786440 | tf_op jit(solution)/shard_map/ppermute | solution.py:583
  37.9 6.9 %collective-permute-start.8 = (f32[2,8,4,8,128]{4,3,2,1,0:T(8,128)S(1)}, f32[2,8,4,8,128]{4,3,2,1,0:T(8,128)S(1)}, u32[]{:S(2)}, u32[]{:S(2)}) collective-permute-start(f32[2,8,4,8,128]{4,3,2,1,0:T(8,128)S(1)} %get-tuple-element.59.coarse_ref), channel_id=1, source_target_pairs={{0,8},{8,0},{16,24},{24,16},{32,40},{40,32},{48,56},{56,48},{64,72... | collective-permute-start | bytes 786440 | tf_op jit(solution)/shard_map/ppermute | solution.py:583

commit v6 on v5

--- a/solution.py
+++ b/solution.py
@@ -317,16 +317,21 @@
     stencil(ext, receiver_old, velocity_ref, receiver_part, inject_ref)
 
 
+def row_factors():
+    row = lax.broadcasted_iota(jnp.int32, (8, 128), 0)
+    step = row & 3
+    below = {d: jnp.where(step < d, COEF[d], 0.0) for d in range(1, 4)}
+    above = {d: jnp.where(step >= 4 - d, COEF[d], 0.0) for d in range(1, 4)}
+    return row < 4, below, above
+
+
 def halo_terms(m1, m2, m3, m4, f, l, flags):
-    gx_even, has_left, has_right, gy_even, has_below, has_above = flags
+    gx_even, has_left, has_right, gy_even, has_below, has_above, (first, below_of, above_of) = flags
     left, right = [], []
     for p in range(4):
         a, b = m1[f, p, l], m2[f, p, l]
         left.append(jnp.where(has_left, pick(gx_even, b, a), 0.0))
         right.append(jnp.where(has_right, pick(gx_even, a, b), 0.0))
-    row = lax.broadcasted_iota(jnp.int32, (8, 128), 0)
-    step = row & 3
-    first = row < 4
     lows, highs = [None] * VX, [None] * VX
     for i in range(4):
         a, b = m3[f, i, l], m4[f, i, l]
@@ -334,8 +339,8 @@
         high = jnp.where(has_above, pick(gy_even, a, b), 0.0)
         below, above = COEF[4] * low, COEF[4] * high
         for d in range(1, 4):
-            below = below + jnp.where(step < d, COEF[d], 0.0) * pltpu.roll(low, 4 + d, 0)
-            above = above + jnp.where(step >= 4 - d, COEF[d], 0.0) * pltpu.roll(high, 4 - d, 0)
+            below = below + below_of[d] * pltpu.roll(low, 4 + d, 0)
+            above = above + above_of[d] * pltpu.roll(high, 4 - d, 0)
         lows[i] = jnp.where(first, below, 0.0)
         lows[i + 4] = jnp.where(first, pltpu.roll(below, 4, 0), 0.0)
         highs[i] = jnp.where(first, 0.0, pltpu.roll(above, 4, 0))
@@ -380,7 +385,7 @@
     s4,
     coarse_ref,
 ):
-    flags = flags_of()
+    flags = flags_of() + (row_factors(),)
     gx_even, gy_even = flags[0], flags[3]
     for f, (part, out) in enumerate(((source_part, source_ref), (receiver_part, receiver_ref))):
 
@@ -423,7 +428,7 @@
     coarse_ref,
     stage,
 ):
-    flags = flags_of()
+    flags = flags_of() + (row_factors(),)
     for f, (part, out) in enumerate(((source_part, source_ref), (receiver_part, receiver_ref))):
 
         def tile(l, carry, f=f, part=part, out=out):

time: 46.1 us -> 46.1 us (level)
  no operation moved by 1% of the time
where the time goes in v6:
time: 46.1 us; the launch traced here: 45.9 us
  waiting for transfers between devices  17.2 us (37%)
  Pallas kernels  16.3 us (35%)
  starting transfers between devices  11.7 us (25%)
  between operations  0.71 us (2%)
    pallas_call x8, Pallas kernels, call(): pl.pallas_call(kernel, out_shape=[jax.ShapeDtypeStruct(s, F32) for _, s i...  16.3 us
    ppermute x2, waiting for transfers between devices, outer_y(): return lax.ppermute(m4, ('gx', 'gy'), y_outer())  11.1 us
    ppermute x3, waiting for transfers between devices, along_x(): lax.ppermute(m2, ('gx', 'gy'), x_outer(near))  6.15 us
    ppermute x2, starting transfers between devices, outer_y(): return lax.ppermute(m4, ('gx', 'gy'), y_outer())  5.01 us
    ppermute x3, starting transfers between devices, along_x(): lax.ppermute(m2, ('gx', 'gy'), x_outer(near))  4.87 us
    ppermute x2, starting transfers between devices, inner_y(): return lax.ppermute(m3, 'gy', inner('gy'))  1.49 us
  transfers between devices with their start and end apart: 10, of which 4 were waited for; matrix products, arithmetic and copies ran while one was open for 0% of the time, Pallas kernels for 26%

profile of v6, /device:TPU:24, one launch (start us, length us, event | category | flops | bytes accessed | tf_op | source)
XLA Modules:
  0.0 45.9 jit_solution(10614713577203794450)
XLA Ops:
  0.6 1.4 %pack.1 = (f32[2,4,8,16,128]{4,3,2,1,0:T(8,128)S(1)}, f32[2,4,8,16,128]{4,3,2,1,0:T(8,128)S(1)}, f32[2,4,8,8,128]{4,3,2,1,0:T(8,128)S(1)}, f32[2,4,8,8,128]{4,3,...) custom-call(f32[8,16,1024]{2,1,0:T(8,128)} %source_hbm.1, f32[8,16,1024]{2,1,0:T(8,128)} %receiver_hbm.1), custom_call_target="tpu_custom_call" | custom-call | tf_op jit(solution)/shard_map/pack/pallas_call | solution.py:517
  2.0 3.7 %collective-permute-start = (f32[2,4,8,16,128]{4,3,2,1,0:T(8,128)S(1)}, f32[2,4,8,16,128]{4,3,2,1,0:T(8,128)S(1)}, u32[]{:S(2)}, u32[]{:S(2)}) collective-permute-start(f32[2,4,8,16,128]{4,3,2,1,0:T(8,128)S(1)} %get-tuple-element.39), channel_id=1, source_target_pairs={{0,1},{1,0},{2,3},{3,2},{4,5},{5,4},{6,7},{7,6},{8,16},{9,17},{10,... | collective-permute-start | bytes 1572872 | tf_op jit(solution)/shard_map/ppermute | solution.py:588
  5.8 0.0 collective-permute-start.1
  5.8 1.5 %collective-permute-start.2 = (f32[2,4,8,8,128]{4,3,2,1,0:T(8,128)S(1)}, f32[2,4,8,8,128]{4,3,2,1,0:T(8,128)S(1)}, u32[]{:S(2)}, u32[]{:S(2)}) collective-permute-start(f32[2,4,8,8,128]{4,3,2,1,0:T(8,128)S(1)} %get-tuple-element.41), channel_id=1, source_target_pairs={{0,1},{1,0},{2,3},{3,2},{4,5},{5,4},{6,7},{7,6},{8,9},{9,8},{10,11... | collective-permute-start | bytes 786440 | tf_op jit(solution)/shard_map/ppermute | solution.py:592
  7.3 3.0 %source1.1 = (f32[8,8,16,128]{3,2,1,0:T(8,128)S(1)}, f32[8,16,1024]{2,1,0:T(8,128)S(1)}) custom-call(f32[8,16,1024]{2,1,0:T(8,128)S(1)} %get-tuple-element.33.now_ref.source_old, f32[8,16,1024]{2,1,0:T(8,128)} %prev_hbm.2, f32[8,16,1024]{2,1,0:T(8,128)} %velocity_hbm.1, s32[4]{0:T(128)} %cells_hbm.5, f32[2,4]{1,0:T(2,128)} %wavelet_hbm.3), custom_call_target="tpu_custom_call" | custom-call | tf_op jit(solution)/shard_map/source1/pallas_call | solution.py:517
  10.3 2.6 %collective-permute-start.3 = (f32[2,4,8,8,128]{4,3,2,1,0:T(8,128)S(1)}, f32[2,4,8,8,128]{4,3,2,1,0:T(8,128)S(1)}, u32[]{:S(2)}, u32[]{:S(2)}) collective-permute-start(f32[2,4,8,8,128]{4,3,2,1,0:T(8,128)S(1)} %get-tuple-element.42), channel_id=1, source_target_pairs={{0,8},{1,2},{2,1},{3,4},{4,3},{5,6},{6,5},{7,15},{8,0},{9,10},{10,... | collective-permute-start | bytes 786440 | tf_op jit(solution)/shard_map/ppermute | solution.py:596
  12.8 4.0 %receiver1.1 = (f32[8,8,16,128]{3,2,1,0:T(8,128)S(1)}, f32[8,8,16,128]{3,2,1,0:T(8,128)S(1)}) custom-call(f32[8,16,1024]{2,1,0:T(8,128)S(1)} %get-tuple-element.36.now_ref.receiver_old, f32[8,16,1024]{2,1,0:T(8,128)S(1)} %get-tuple-element.37.velocity_ref, f32[8,16,1024]{2,1,0:T(8,128)} %prev_hbm.3, s32[32,128]{1,0:T(8,128)} %bitcast.1, s32[4096]{0:T(1024)} %cells_hbm.4, ...), custom_call_target="tpu_custom_call" | custom-call | tf_op jit(solution)/shard_map/receiver1/pallas_call | solution.py:517
  16.9 0.0 collective-permute-done.2.m3
  16.9 5.6 %collective-permute-done.3.m4 = f32[2,4,8,8,128]{4,3,2,1,0:T(8,128)S(1)} collective-permute-done((f32[2,4,8,8,128]{4,3,2,1,0:T(8,128)S(1)}, f32[2,4,8,8,128]{4,3,2,1,0:T(8,128)S(1)}, u32[]{:S(2)}, u32[]{:S(2)}) %collective-permute-start.3) | collective-permute-done | bytes 262176 | tf_op jit(solution)/shard_map/ppermute | solution.py:596
  22.5 0.0 collective-permute-done.m2
  22.5 0.0 collective-permute-done.1.m1
  22.5 1.1 %halo1.1 = (f32[8,8,16,128]{3,2,1,0:T(8,128)S(1)}, f32[8,8,16,128]{3,2,1,0:T(8,128)S(1)}, f32[2,5,8,16,128]{4,3,2,1,0:T(8,128)S(1)}, f32[2,5,8,16,128]{4,3,2,1,0...) custom-call(f32[8,8,16,128]{3,2,1,0:T(8,128)S(1)} %get-tuple-element, ...), custom_call_target="tpu_custom_call" | custom-call | tf_op jit(solution)/shard_map/halo1/pallas_call | solution.py:517
  23.6 0.1 collective-permute-start.5
  23.7 2.5 %collective-permute-start.6 = (f32[2,4,8,8,128]{4,3,2,1,0:T(8,128)S(1)}, f32[2,4,8,8,128]{4,3,2,1,0:T(8,128)S(1)}, u32[]{:S(2)}, u32[]{:S(2)}) collective-permute-start(f32[2,4,8,8,128]{4,3,2,1,0:T(8,128)S(1)} %get-tuple-element.46), channel_id=1, source_target_pairs={{0,8},{1,2},{2,1},{3,4},{4,3},{5,6},{6,5},{7,15},{8,0},{9,10},{10,... | collective-permute-start | bytes 786440 | tf_op jit(solution)/shard_map/ppermute | solution.py:596
  26.2 0.0 collective-permute-start.4
  26.2 0.0 collective-permute-start.7
  26.2 3.7 %local2.1 = (f32[8,8,16,128]{3,2,1,0:T(8,128)S(1)}, f32[8,8,16,128]{3,2,1,0:T(8,128)S(1)}) custom-call(f32[8,8,16,128]{3,2,1,0:T(8,128)S(1)} %get-tuple-element.48.source_ref, f32[8,8,16,128]{3,2,1,0:T(8,128)S(1)} %get-tuple-element.49.receiver_ref, f32[8,16,1024]{2,1,0:T(8,128)S(1)} %get-tuple-element.33.now_ref.source_old, ...), custom_call_target="tpu_custom_call" | custom-call | tf_op jit(solution)/shard_map/local2/pallas_call | solution.py:517
  29.9 5.4 %collective-permute-done.6.refs_1_ = f32[2,4,8,8,128]{4,3,2,1,0:T(8,128)S(1)} collective-permute-done((f32[2,4,8,8,128]{4,3,2,1,0:T(8,128)S(1)}, f32[2,4,8,8,128]{4,3,2,1,0:T(8,128)S(1)}, u32[]{:S(2)}, u32[]{:S(2)}) %collective-permute-start.6) | collective-permute-done | bytes 262176 | tf_op jit(solution)/shard_map/ppermute | solution.py:596
  35.3 0.5 %collective-permute-done.5.refs_0_ = f32[2,5,8,16,128]{4,3,2,1,0:T(8,128)S(1)} collective-permute-done((f32[2,5,8,16,128]{4,3,2,1,0:T(8,128)S(1)}, f32[2,5,8,16,128]{4,3,2,1,0:T(8,128)S(1)}, u32[]{:S(2)}, u32[]{:S(2)}) %collective-permute-start.5) | collective-permute-done | bytes 655392 | tf_op jit(solution)/shard_map/ppermute | solution.py:588
  35.8 0.0 collective-permute-done.7.m3
  35.8 0.0 collective-permute-done.4.m1
  35.8 1.0 %halo2.1 = (f32[8,16,1024]{2,1,0:T(8,128)S(1)}, f32[8,16,1024]{2,1,0:T(8,128)S(1)}, f32[2,8,4,8,128]{4,3,2,1,0:T(8,128)S(1)}) custom-call(f32[8,8,16,128]{3,2,1,0:T(8,128)S(1)} %get-tuple-element.51.source_part, f32[8,8,16,128]{3,2,1,0:T(8,128)S(1)} %get-tuple-element.52.receiver_part, f32[8,16,1024]{2,1,0:T(8,128)S(1)} %get-tuple-element.37.velocity_ref, ...), custom_call_target="tpu_custom_call" | custom-call | tf_op jit(solution)/shard_map/halo2/pallas_call | solution.py:517
  36.8 1.0 %collective-permute-start.9 = (f32[2,8,4,8,128]{4,3,2,1,0:T(8,128)S(1)}, f32[2,8,4,8,128]{4,3,2,1,0:T(8,128)S(1)}, u32[]{:S(2)}, u32[]{:S(2)}) collective-permute-start(f32[2,8,4,8,128]{4,3,2,1,0:T(8,128)S(1)} %get-tuple-element.59.coarse_ref), channel_id=1, source_target_pairs={{0,1},{1,0},{2,3},{3,2},{4,5},{5,4},{6,7},{7,6},{8,16},{9,17},{10,... | collective-permute-start | bytes 786440 | tf_op jit(solution)/shard_map/ppermute | solution.py:588
  37.9 0.3 collective-permute-start.8
  38.2 1.0 %image1.1 = (f32[17,4,4,8,128]{4,3,2,1,0:T(8,128)S(1)}, f32[8,16,1024]{2,1,0:T(8,128)}, f32[8,16,1024]{2,1,0:T(8,128)}) custom-call(f32[2,8,4,8,128]{4,3,2,1,0:T(8,128)S(1)} %get-tuple-element.43.coarse_ref, f32[2,5,8,16,128]{4,3,2,1,0:T(8,128)S(1)} %collective-permute-done.4.m1, f32[2,5,8,16,128]{4,3,2,1,0:T(8,128)S(1)} %get-tuple-element.47.m2, ...), custom_call_target="tpu_custom_call" | custom-call | tf_op jit(solution)/shard_map/image1/pallas_call | solution.py:517
  39.1 5.7 %collective-permute-done.9.m2 = f32[2,8,4,8,128]{4,3,2,1,0:T(8,128)S(1)} collective-permute-done((f32[2,8,4,8,128]{4,3,2,1,0:T(8,128)S(1)}, f32[2,8,4,8,128]{4,3,2,1,0:T(8,128)S(1)}, u32[]{:S(2)}, u32[]{:S(2)}) %collective-permute-start.9) | collective-permute-done | bytes 262176 | tf_op jit(solution)/shard_map/ppermute | solution.py:588
  44.8 0.0 collective-permute-done.8.m1
  44.8 1.1 %image2.1 = f32[17,4,8,512]{3,2,1,0:T(8,128)} custom-call(f32[2,8,4,8,128]{4,3,2,1,0:T(8,128)S(1)} %get-tuple-element.59.coarse_ref, f32[2,8,4,8,128]{4,3,2,1,0:T(8,128)S(1)} %collective-permute-done.8.m1, f32[2,8,4,8,128]{4,3,2,1,0:T(8,128)S(1)} %collective-permute-done.9.m2, f32[17,4,4,8,128]{4,3,2,1,0:T(8,128)S(1)} %get-tuple-element.60.before_ref), custom_call_target="tpu_custom_call" | custom-call | tf_op jit(solution)/shard_map/image2/pallas_call | solution.py:517
  (1 shorter events, 0.0 us)
Async XLA Ops:
  2.0 20.5 %collective-permute-start = (f32[2,4,8,16,128]{4,3,2,1,0:T(8,128)S(1)}, f32[2,4,8,16,128]{4,3,2,1,0:T(8,128)S(1)}, u32[]{:S(2)}, u32[]{:S(2)}) collective-permute-start(f32[2,4,8,16,128]{4,3,2,1,0:T(8,128)S(1)} %get-tuple-element.39), channel_id=1, source_target_pairs={{0,1},{1,0},{2,3},{3,2},{4,5},{5,4},{6,7},{7,6},{8,16},{9,17},{10,... | collective-permute-start | bytes 1572872 | tf_op jit(solution)/shard_map/ppermute | solution.py:588
  5.8 16.8 %collective-permute-start.1 = (f32[2,4,8,16,128]{4,3,2,1,0:T(8,128)S(1)}, f32[2,4,8,16,128]{4,3,2,1,0:T(8,128)S(1)}, u32[]{:S(2)}, u32[]{:S(2)}) collective-permute-start(f32[2,4,8,16,128]{4,3,2,1,0:T(8,128)S(1)} %get-tuple-element.40), channel_id=1, source_target_pairs={{0,8},{8,0},{16,24},{24,16},{32,40},{40,32},{48,56},{56,48},{64,72... | collective-permute-start | bytes 1572872 | tf_op jit(solution)/shard_map/ppermute | solution.py:588
  5.8 11.1 %collective-permute-start.2 = (f32[2,4,8,8,128]{4,3,2,1,0:T(8,128)S(1)}, f32[2,4,8,8,128]{4,3,2,1,0:T(8,128)S(1)}, u32[]{:S(2)}, u32[]{:S(2)}) collective-permute-start(f32[2,4,8,8,128]{4,3,2,1,0:T(8,128)S(1)} %get-tuple-element.41), channel_id=1, source_target_pairs={{0,1},{1,0},{2,3},{3,2},{4,5},{5,4},{6,7},{7,6},{8,9},{9,8},{10,11... | collective-permute-start | bytes 786440 | tf_op jit(solution)/shard_map/ppermute | solution.py:592
  10.3 12.2 %collective-permute-start.3 = (f32[2,4,8,8,128]{4,3,2,1,0:T(8,128)S(1)}, f32[2,4,8,8,128]{4,3,2,1,0:T(8,128)S(1)}, u32[]{:S(2)}, u32[]{:S(2)}) collective-permute-start(f32[2,4,8,8,128]{4,3,2,1,0:T(8,128)S(1)} %get-tuple-element.42), channel_id=1, source_target_pairs={{0,8},{1,2},{2,1},{3,4},{4,3},{5,6},{6,5},{7,15},{8,0},{9,10},{10,... | collective-permute-start | bytes 786440 | tf_op jit(solution)/shard_map/ppermute | solution.py:596
  23.6 12.2 %collective-permute-start.5 = (f32[2,5,8,16,128]{4,3,2,1,0:T(8,128)S(1)}, f32[2,5,8,16,128]{4,3,2,1,0:T(8,128)S(1)}, u32[]{:S(2)}, u32[]{:S(2)}) collective-permute-start(f32[2,5,8,16,128]{4,3,2,1,0:T(8,128)S(1)} %get-tuple-element.45), channel_id=1, source_target_pairs={{0,1},{1,0},{2,122},{3,123},{4,124},{5,125},{6,7},{7,6},{8,16},{9,... | collective-permute-start | bytes 1966088 | tf_op jit(solution)/shard_map/ppermute | solution.py:588
  23.7 11.6 %collective-permute-start.6 = (f32[2,4,8,8,128]{4,3,2,1,0:T(8,128)S(1)}, f32[2,4,8,8,128]{4,3,2,1,0:T(8,128)S(1)}, u32[]{:S(2)}, u32[]{:S(2)}) collective-permute-start(f32[2,4,8,8,128]{4,3,2,1,0:T(8,128)S(1)} %get-tuple-element.46), channel_id=1, source_target_pairs={{0,8},{1,2},{2,1},{3,4},{4,3},{5,6},{6,5},{7,15},{8,0},{9,10},{10,... | collective-permute-start | bytes 786440 | tf_op jit(solution)/shard_map/ppermute | solution.py:596
  26.2 9.7 %collective-permute-start.4 = (f32[2,5,8,16,128]{4,3,2,1,0:T(8,128)S(1)}, f32[2,5,8,16,128]{4,3,2,1,0:T(8,128)S(1)}, u32[]{:S(2)}, u32[]{:S(2)}) collective-permute-start(f32[2,5,8,16,128]{4,3,2,1,0:T(8,128)S(1)} %get-tuple-element.44), channel_id=1, source_target_pairs={{0,8},{8,0},{16,24},{24,16},{32,40},{40,32},{48,56},{56,48},{64,72... | collective-permute-start | bytes 1966088 | tf_op jit(solution)/shard_map/ppermute | solution.py:588
  26.2 9.7 %collective-permute-start.7 = (f32[2,4,8,8,128]{4,3,2,1,0:T(8,128)S(1)}, f32[2,4,8,8,128]{4,3,2,1,0:T(8,128)S(1)}, u32[]{:S(2)}, u32[]{:S(2)}) collective-permute-start(f32[2,4,8,8,128]{4,3,2,1,0:T(8,128)S(1)} %get-tuple-element.53), channel_id=1, source_target_pairs={{0,1},{1,0},{2,3},{3,2},{4,5},{5,4},{6,7},{7,6},{8,9},{9,8},{10,11... | collective-permute-start | bytes 786440 | tf_op jit(solution)/shard_map/ppermute | solution.py:592
  36.8 8.0 %collective-permute-start.9 = (f32[2,8,4,8,128]{4,3,2,1,0:T(8,128)S(1)}, f32[2,8,4,8,128]{4,3,2,1,0:T(8,128)S(1)}, u32[]{:S(2)}, u32[]{:S(2)}) collective-permute-start(f32[2,8,4,8,128]{4,3,2,1,0:T(8,128)S(1)} %get-tuple-element.59.coarse_ref), channel_id=1, source_target_pairs={{0,1},{1,0},{2,3},{3,2},{4,5},{5,4},{6,7},{7,6},{8,16},{9,17},{10,... | collective-permute-start | bytes 786440 | tf_op jit(solution)/shard_map/ppermute | solution.py:588
  37.9 6.9 %collective-permute-start.8 = (f32[2,8,4,8,128]{4,3,2,1,0:T(8,128)S(1)}, f32[2,8,4,8,128]{4,3,2,1,0:T(8,128)S(1)}, u32[]{:S(2)}, u32[]{:S(2)}) collective-permute-start(f32[2,8,4,8,128]{4,3,2,1,0:T(8,128)S(1)} %get-tuple-element.59.coarse_ref), channel_id=1, source_target_pairs={{0,8},{8,0},{16,24},{24,16},{32,40},{40,32},{48,56},{56,48},{64,72... | collective-permute-start | bytes 786440 | tf_op jit(solution)/shard_map/ppermute | solution.py:588
